TPU v7x, 256 devices: a whole 4x4x8 slice. The times are simulated.
256 devices in a mesh: seq: 128 (over z, x, y), section: 2 (over core).
Axes of the slice: x: 4, y: 4, z: 8, core: 2. Of those that a mesh axis runs over, the one named last changes fastest.
Arguments:
- layer_input: bfloat16 [2, 16384, 512], P('section', 'seq'), may hold values from -6 to 6
- conv_out: bfloat16 [2, 2, 16384, 512], P('section', None, 'seq'), may hold values from -6 to 6
- filters: bfloat16 [2, 2, 16384, 512], P('section', None, 'seq'), may hold values from -1.1 to 1.1
- skip_gain: float32 [2, 2, 512], P('section'), may hold values from -4 to 4
- weight_in: bfloat16 [2, 512, 1536], P('section'), may hold values from -0.25 to 0.25
- weight_out: bfloat16 [2, 512, 512], P('section'), may hold values from -0.25 to 0.25
- grad_output: bfloat16 [16384, 512], P('seq'), may hold values from -18 to 18
Outputs:
- grad_input: bfloat16 [2, 16384, 512], P('section', 'seq')
- grad_filter: bfloat16 [2, 2, 16384, 512], P('section', None, 'seq')
- grad_skip: float32 [2, 2, 512], P('section')
All inputs are finite; a program needn't handle non-finite values.
Results may differ from a plain program's by a relative error of at most 0.009.
Values may be sent and summed in bfloat16 or wider, within the bound.
No kernel may reach another device: no remote copies, remote signals or barrier semaphores. Data moves between devices by JAX's collectives and lax.ppermute only.
A program may use at most 128 MiB of HBM per device.

v0:
```python
import math

import jax
import jax.numpy as jnp
from jax import lax
from jax.sharding import PartitionSpec as P

HIGHEST = lax.Precision.HIGHEST


def from_behind(value, axis, steps):
    count = lax.axis_size(axis)
    leading, last = (max(0, -steps), min(count, count - steps))
    return lax.ppermute(value, axis, [(source, source + steps) for source in range(leading, last)])


def angle_table(count_rows, count_cols, period):
    row_index = lax.broadcasted_iota(jnp.int32, (count_rows, count_cols), 0)
    col_index = lax.broadcasted_iota(jnp.int32, (count_rows, count_cols), 1)
    angles = (row_index * col_index % period).astype(jnp.float32) * (2.0 * math.pi / period)
    return (jnp.cos(angles), jnp.sin(angles))


def time_twist(part_count, row_count):
    panel_rows = row_count // part_count
    device_index = lax.axis_index("seq")
    part_index = lax.broadcasted_iota(jnp.int32, (part_count, panel_rows, 1), 0)
    row_index = lax.broadcasted_iota(jnp.int32, (part_count, panel_rows, 1), 1)
    position = part_index * row_count + device_index * panel_rows + row_index
    angles = position.astype(jnp.float32) * (math.pi / (part_count * row_count))
    return (jnp.cos(angles), jnp.sin(angles))


def panel_twiddle(part_count, row_count):
    panel_rows = row_count // part_count
    device_index = lax.axis_index("seq")
    freq_index = lax.broadcasted_iota(jnp.int32, (part_count, panel_rows, 1), 0)
    row_index = lax.broadcasted_iota(jnp.int32, (part_count, panel_rows, 1), 1)
    phases = freq_index * (device_index * panel_rows + row_index) % (part_count * row_count)
    angles = phases.astype(jnp.float32) * (2.0 * math.pi / (part_count * row_count))
    return (jnp.cos(angles), jnp.sin(angles))


def across_parts(matrix, operand):
    return jnp.einsum("bp,kprd->kbrd", matrix, operand, precision=HIGHEST)


def to_spectrum(signals):
    signal_count, row_count, channels = signals.shape
    part_count = lax.axis_size("seq")
    panel_data = lax.all_to_all(
        signals.reshape(signal_count, 1, row_count, channels),
        "seq",
        split_axis=2,
        concat_axis=1,
        tiled=True,
    )
    twist_cos, twist_sin = time_twist(part_count, row_count)
    odd_real = panel_data * twist_cos
    odd_imag = -panel_data * twist_sin
    part_cos, part_sin = angle_table(part_count, part_count, part_count)
    real_part = jnp.stack(
        [
            across_parts(part_cos, panel_data),
            across_parts(part_cos, odd_real) + across_parts(part_sin, odd_imag),
        ],
        axis=1,
    )
    imag_part = jnp.stack(
        [
            -across_parts(part_sin, panel_data),
            across_parts(part_cos, odd_imag) - across_parts(part_sin, odd_real),
        ],
        axis=1,
    )
    twid_cos, twid_sin = panel_twiddle(part_count, row_count)
    turned_real = real_part * twid_cos + imag_part * twid_sin
    turned_imag = imag_part * twid_cos - real_part * twid_sin
    row_cos, row_sin = angle_table(row_count, row_count, row_count)
    real_in = lax.all_to_all(turned_real, "seq", split_axis=2, concat_axis=3, tiled=True)
    imag_in = lax.all_to_all(turned_imag, "seq", split_axis=2, concat_axis=3, tiled=True)
    out_real = jnp.einsum("cm,kesmd->kescd", row_cos, real_in, precision=HIGHEST) + jnp.einsum(
        "cm,kesmd->kescd", row_sin, imag_in, precision=HIGHEST
    )
    out_imag = jnp.einsum("cm,kesmd->kescd", row_cos, imag_in, precision=HIGHEST) - jnp.einsum(
        "cm,kesmd->kescd", row_sin, real_in, precision=HIGHEST
    )
    return (out_real, out_imag)


def from_spectrum(real_part, imag_part):
    signal_count = real_part.shape[0]
    row_count = real_part.shape[3]
    channels = real_part.shape[4]
    part_count = lax.axis_size("seq")
    full_length = part_count * row_count
    row_cos, row_sin = angle_table(row_count, row_count, row_count)
    back_real = jnp.einsum("mc,kescd->kesmd", row_cos, real_part, precision=HIGHEST) - jnp.einsum(
        "mc,kescd->kesmd", row_sin, imag_part, precision=HIGHEST
    )
    back_imag = jnp.einsum("mc,kescd->kesmd", row_cos, imag_part, precision=HIGHEST) + jnp.einsum(
        "mc,kescd->kesmd", row_sin, real_part, precision=HIGHEST
    )
    twid_cos, twid_sin = panel_twiddle(part_count, row_count)
    twist_cos, twist_sin = time_twist(part_count, row_count)
    part_cos, part_sin = angle_table(part_count, part_count, part_count)
    real_in = lax.all_to_all(back_real, "seq", split_axis=3, concat_axis=2, tiled=True)
    imag_in = lax.all_to_all(back_imag, "seq", split_axis=3, concat_axis=2, tiled=True)
    turned_real = real_in * twid_cos - imag_in * twid_sin
    turned_imag = imag_in * twid_cos + real_in * twid_sin
    even_real = across_parts(part_cos, turned_real[:, 0]) - across_parts(
        part_sin, turned_imag[:, 0]
    )
    odd_real = across_parts(part_cos, turned_real[:, 1]) - across_parts(part_sin, turned_imag[:, 1])
    odd_imag = across_parts(part_cos, turned_imag[:, 1]) + across_parts(part_sin, turned_real[:, 1])
    panel_data = (even_real + odd_real * twist_cos - odd_imag * twist_sin) / (2.0 * full_length)
    panel_data = lax.all_to_all(panel_data, "seq", split_axis=1, concat_axis=2, tiled=True)
    return panel_data.reshape(signal_count, row_count, channels)


def conj_times(left_real, left_imag, right_real, right_imag):
    return (
        left_real * right_real + left_imag * right_imag,
        left_real * right_imag - left_imag * right_real,
    )


def on_device(layer_input, conv_out, filters, skip_gain, weight_in, weight_out, grad_output):
    row_count, channels = grad_output.shape
    part_count = lax.axis_size("seq")
    input_rows = layer_input[0]
    conv_rows = conv_out[0]
    filter_rows = filters[0]
    in_matrix = weight_in[0]
    out_matrix = weight_out[0]
    projected = jnp.dot(input_rows, in_matrix, preferred_element_type=jnp.float32).astype(
        jnp.bfloat16
    )
    values = projected[:, :channels].astype(jnp.float32)
    gate_one = projected[:, channels : 2 * channels].astype(jnp.float32)
    gate_two = projected[:, 2 * channels :].astype(jnp.float32)
    conv_one = conv_rows[0].astype(jnp.float32)
    conv_two = conv_rows[1].astype(jnp.float32)
    gated_mix = gate_one * conv_one
    known_real, known_imag = to_spectrum(
        jnp.stack(
            [
                filter_rows[0].astype(jnp.float32),
                filter_rows[1].astype(jnp.float32),
                values,
                gated_mix,
            ]
        )
    )

    def run_tick(incoming):
        grad_mix_two = lax.dot_general(
            incoming, out_matrix, (((1,), (1,)), ((), ())), preferred_element_type=jnp.float32
        )
        grad_gate_two = grad_mix_two * conv_two
        grad_conv_two = grad_mix_two * gate_two
        sum_two = jnp.sum(grad_conv_two * gated_mix, axis=0)
        sum_two = lax.psum(sum_two, "seq")
        two_real, two_imag = to_spectrum(grad_conv_two[None])
        prod_real, prod_imag = conj_times(known_real[1:2], known_imag[1:2], two_real, two_imag)
        grad_mix_one = from_spectrum(prod_real, prod_imag)[0] + skip_gain[0, 1] * grad_conv_two
        grad_gate_one = grad_mix_one * conv_one
        grad_conv_one = grad_mix_one * gate_one
        sum_one = jnp.sum(grad_conv_one * values, axis=0)
        sum_one = lax.psum(sum_one, "seq")
        one_real, one_imag = to_spectrum(grad_conv_one[None])
        prod_real, prod_imag = conj_times(known_real[0:1], known_imag[0:1], one_real, one_imag)
        grad_values = from_spectrum(prod_real, prod_imag)[0] + skip_gain[0, 0] * grad_conv_one
        grad_proj = jnp.concatenate([grad_values, grad_gate_one, grad_gate_two], axis=1).astype(
            jnp.bfloat16
        )
        result = incoming.astype(jnp.float32) + lax.dot_general(
            grad_proj, in_matrix, (((1,), (1,)), ((), ())), preferred_element_type=jnp.float32
        )
        return (
            result.astype(jnp.bfloat16),
            (one_real, one_imag, two_real, two_imag),
            sum_one,
            sum_two,
        )

    late_result, late_spectra, late_one, late_two = run_tick(grad_output)
    handed = from_behind(late_result, "section", -1)
    early_result, early_spectra, early_one, early_two = run_tick(handed)
    is_late = lax.axis_index("section") == 1

    def select_section(late_value, early_value):
        return jnp.where(is_late, late_value, early_value)

    grad_rows = select_section(late_result, early_result)
    one_real, one_imag, two_real, two_imag = jax.tree.map(
        select_section, late_spectra, early_spectra
    )
    sum_one = select_section(late_one, early_one)
    sum_two = select_section(late_two, early_two)
    filt_one_real, filt_one_imag = conj_times(known_real[2:3], known_imag[2:3], one_real, one_imag)
    filt_two_real, filt_two_imag = conj_times(known_real[3:4], known_imag[3:4], two_real, two_imag)
    filter_grads = from_spectrum(
        jnp.concatenate([filt_one_real, filt_two_real]),
        jnp.concatenate([filt_one_imag, filt_two_imag]),
    )
    rescale = 1.0 / math.sqrt(part_count * row_count)
    filter_grads = (filter_grads * rescale).astype(jnp.bfloat16)
    skip_grads = (jnp.stack([sum_one, sum_two]) * rescale)[None]
    return (grad_rows[None], filter_grads[None], skip_grads)


def solution(mesh):
    in_specs = (
        P("section", "seq", None),
        P("section", None, "seq", None),
        P("section", None, "seq", None),
        P("section", None, None),
        P("section", None, None),
        P("section", None, None),
        P("seq", None),
    )
    out_specs = (
        P("section", "seq", None),
        P("section", None, "seq", None),
        P("section", None, None),
    )
    return jax.shard_map(
        on_device, mesh=mesh, in_specs=in_specs, out_specs=out_specs, check_vma=False
    )
```

profile of v0, /device:TPU:8, one launch (start us, length us, event | category | flops | bytes accessed | tf_op | source)
XLA Modules:
  0.0 1205.2 jit_solution(2175008082813027188)
XLA Ops:
  6.1 15.3 %all-to-all-start.3 = ((f32[1,1,128,512]{3,1,0,2:T(1,128)}), f32[1,1,128,512]{3,1,0,2:T(1,128)S(1)}, u32[]{:S(2)}, u32[]{:S(2)}) async-start(f32[1,1,128,512]{3,1,0,2:T(1,128)} %copy.51), calls=%async_computation.3 | async-start | bytes 524288 | tf_op jit(solution)/shard_map/all_to_all | solution.py:51
  23.3 12.7 %all-to-all-done.3 = f32[1,1,128,512]{3,1,0,2:T(1,128)S(1)} async-done(((f32[1,1,128,512]{3,1,0,2:T(1,128)}), f32[1,1,128,512]{3,1,0,2:T(1,128)S(1)}, u32[]{:S(2)}, u32[]{:S(2)}) %all-to-all-start.3) | async-done | bytes 262176 | tf_op jit(solution)/shard_map/all_to_all | solution.py:51
  50.3 21.5 %all-to-all-done = f32[4,1,128,512]{3,0,1,2:T(4,128)S(1)} async-done(((f32[4,1,128,512]{3,0,1,2:T(4,128)}), f32[4,1,128,512]{3,0,1,2:T(4,128)S(1)}, u32[]{:S(2)}, u32[]{:S(2)}) %all-to-all-start) | async-done | bytes 1048608 | tf_op jit(solution)/shard_map/all_to_all | solution.py:51
  87.7 9.4 all-to-all-done.4
  120.7 8.5 all-to-all-start.2
  132.4 44.7 %all-to-all-done.2 = f32[4,2,128,1,512]{4,0,3,1,2:T(4,128)} async-done(((f32[4,2,128,1,512]{4,0,3,1,2:T(4,128)}), f32[4,2,128,1,512]{4,0,3,1,2:T(4,128)}, u32[]{:S(2)}, u32[]{:S(2)}) %all-to-all-start.2) | async-done | bytes 2097184 | tf_op jit(solution)/shard_map/all_to_all | solution.py:81
  202.1 31.3 %all-to-all-done.1 = f32[4,2,128,1,512]{4,0,3,1,2:T(4,128)} async-done(((f32[4,2,128,1,512]{4,0,3,1,2:T(4,128)}), f32[4,2,128,1,512]{4,0,3,1,2:T(4,128)}, u32[]{:S(2)}, u32[]{:S(2)}) %all-to-all-start.1) | async-done | bytes 2097184 | tf_op jit(solution)/shard_map/all_to_all | solution.py:80
  258.4 13.5 %all-to-all-done.6 = f32[1,2,1,128,512]{4,1,2,0,3:T(2,128)} async-done(((f32[1,2,1,128,512]{4,1,2,0,3:T(2,128)}), f32[1,2,1,128,512]{4,1,2,0,3:T(2,128)}, u32[]{:S(2)}, u32[]{:S(2)}) %all-to-all-start.6) | async-done | bytes 524320 | tf_op jit(solution)/shard_map/all_to_all | solution.py:107
  280.0 14.7 %all-to-all-done.7 = f32[1,2,1,128,512]{4,1,2,0,3:T(2,128)S(1)} async-done(((f32[1,2,1,128,512]{4,1,2,0,3:T(2,128)}), f32[1,2,1,128,512]{4,1,2,0,3:T(2,128)S(1)}, u32[]{:S(2)}, u32[]{:S(2)}) %all-to-all-start.7) | async-done | bytes 524320 | tf_op jit(solution)/shard_map/all_to_all | solution.py:108
  306.8 12.7 %all-to-all-done.8 = f32[1,128,1,512]{3,2,0,1:T(1,128)S(1)} async-done(((f32[1,128,1,512]{3,2,0,1:T(1,128)}), f32[1,128,1,512]{3,2,0,1:T(1,128)S(1)}, u32[]{:S(2)}, u32[]{:S(2)}) %all-to-all-start.8) | async-done | bytes 262176 | tf_op jit(solution)/shard_map/all_to_all | solution.py:117
  320.5 19.7 %all_to_all.300 = f32[1,1,128,512]{3,1,0,2:T(1,128)S(1)} all-to-all(f32[1,1,128,512]{3,1,0,2:T(1,128)S(1)} %copy.61), channel_id=1, replica_groups=mesh['seq'=128,'section'=2] {'seq'}, dimensions={2} | all-to-all | bytes 524288 | tf_op jit(solution)/shard_map/all_to_all | solution.py:51
  353.6 14.8 %all-to-all-done.10 = f32[1,2,128,1,512]{4,3,1,0,2:T(1,128)S(1)} async-done(((f32[1,2,128,1,512]{4,3,1,0,2:T(1,128)}), f32[1,2,128,1,512]{4,3,1,0,2:T(1,128)S(1)}, u32[]{:S(2)}, u32[]{:S(2)}) %all-to-all-start.10) | async-done | bytes 524320 | tf_op jit(solution)/shard_map/all_to_all | solution.py:80
  377.8 14.1 %all-to-all-done.11 = f32[1,2,128,1,512]{4,3,1,0,2:T(1,128)} async-done(((f32[1,2,128,1,512]{4,3,1,0,2:T(1,128)}), f32[1,2,128,1,512]{4,3,1,0,2:T(1,128)}, u32[]{:S(2)}, u32[]{:S(2)}) %all-to-all-start.11) | async-done | bytes 524320 | tf_op jit(solution)/shard_map/all_to_all | solution.py:81
  410.0 13.2 %all-to-all-done.12 = f32[1,2,1,128,512]{4,1,2,0,3:T(2,128)S(1)} async-done(((f32[1,2,1,128,512]{4,1,2,0,3:T(2,128)}), f32[1,2,1,128,512]{4,1,2,0,3:T(2,128)S(1)}, u32[]{:S(2)}, u32[]{:S(2)}) %all-to-all-start.12) | async-done | bytes 524320 | tf_op jit(solution)/shard_map/all_to_all | solution.py:107
  430.6 15.5 %all-to-all-done.13 = f32[1,2,1,128,512]{4,1,2,0,3:T(2,128)S(1)} async-done(((f32[1,2,1,128,512]{4,1,2,0,3:T(2,128)}), f32[1,2,1,128,512]{4,1,2,0,3:T(2,128)S(1)}, u32[]{:S(2)}, u32[]{:S(2)}) %all-to-all-start.13) | async-done | bytes 524320 | tf_op jit(solution)/shard_map/all_to_all | solution.py:108
  450.4 19.5 %all_to_all.301 = f32[1,128,1,512]{3,2,0,1:T(1,128)S(1)} all-to-all(f32[1,128,1,512]{3,2,0,1:T(1,128)S(1)} %copy.70), channel_id=1, replica_groups=mesh['seq'=128,'section'=2] {'seq'}, dimensions={1} | all-to-all | bytes 524288 | tf_op jit(solution)/shard_map/all_to_all | solution.py:117
  474.9 21.7 %all_to_all.302 = f32[1,1,128,512]{3,1,0,2:T(1,128)S(1)} all-to-all(f32[1,1,128,512]{3,1,0,2:T(1,128)S(1)} %copy.71), channel_id=1, replica_groups=mesh['seq'=128,'section'=2] {'seq'}, dimensions={2} | all-to-all | bytes 524288 | tf_op jit(solution)/shard_map/all_to_all | solution.py:51
  510.0 17.8 %all-to-all-done.17 = f32[1,2,128,1,512]{4,3,1,0,2:T(1,128)S(1)} async-done(((f32[1,2,128,1,512]{4,3,1,0,2:T(1,128)}), f32[1,2,128,1,512]{4,3,1,0,2:T(1,128)S(1)}, u32[]{:S(2)}, u32[]{:S(2)}) %all-to-all-start.17) | async-done | bytes 524320 | tf_op jit(solution)/shard_map/all_to_all | solution.py:81
  537.2 15.8 %all-to-all-done.16 = f32[1,2,128,1,512]{4,3,1,0,2:T(1,128)} async-done(((f32[1,2,128,1,512]{4,3,1,0,2:T(1,128)}), f32[1,2,128,1,512]{4,3,1,0,2:T(1,128)}, u32[]{:S(2)}, u32[]{:S(2)}) %all-to-all-start.16) | async-done | bytes 524320 | tf_op jit(solution)/shard_map/all_to_all | solution.py:80
  571.6 14.1 %all-to-all-done.18 = f32[1,2,1,128,512]{4,1,2,0,3:T(2,128)S(1)} async-done(((f32[1,2,1,128,512]{4,1,2,0,3:T(2,128)}), f32[1,2,1,128,512]{4,1,2,0,3:T(2,128)S(1)}, u32[]{:S(2)}, u32[]{:S(2)}) %all-to-all-start.18) | async-done | bytes 524320 | tf_op jit(solution)/shard_map/all_to_all | solution.py:107
  592.9 15.9 %all-to-all-done.19 = f32[1,2,1,128,512]{4,1,2,0,3:T(2,128)S(1)} async-done(((f32[1,2,1,128,512]{4,1,2,0,3:T(2,128)}), f32[1,2,1,128,512]{4,1,2,0,3:T(2,128)S(1)}, u32[]{:S(2)}, u32[]{:S(2)}) %all-to-all-start.19) | async-done | bytes 524320 | tf_op jit(solution)/shard_map/all_to_all | solution.py:108
  613.1 19.2 %all_to_all.303 = f32[1,128,1,512]{3,2,0,1:T(1,128)S(1)} all-to-all(f32[1,128,1,512]{3,2,0,1:T(1,128)S(1)} %copy.80), channel_id=1, replica_groups=mesh['seq'=128,'section'=2] {'seq'}, dimensions={1} | all-to-all | bytes 524288 | tf_op jit(solution)/shard_map/all_to_all | solution.py:117
  634.8 19.7 %all_to_all.304 = f32[1,1,128,512]{3,1,0,2:T(1,128)S(1)} all-to-all(f32[1,1,128,512]{3,1,0,2:T(1,128)S(1)} %copy.81), channel_id=1, replica_groups=mesh['seq'=128,'section'=2] {'seq'}, dimensions={2} | all-to-all | bytes 524288 | tf_op jit(solution)/shard_map/all_to_all | solution.py:51
  667.9 14.8 %all-to-all-done.23 = f32[1,2,128,1,512]{4,3,1,0,2:T(1,128)S(1)} async-done(((f32[1,2,128,1,512]{4,3,1,0,2:T(1,128)}), f32[1,2,128,1,512]{4,3,1,0,2:T(1,128)S(1)}, u32[]{:S(2)}, u32[]{:S(2)}) %all-to-all-start.23) | async-done | bytes 524320 | tf_op jit(solution)/shard_map/all_to_all | solution.py:81
  692.1 14.1 %all-to-all-done.22 = f32[1,2,128,1,512]{4,3,1,0,2:T(1,128)} async-done(((f32[1,2,128,1,512]{4,3,1,0,2:T(1,128)}), f32[1,2,128,1,512]{4,3,1,0,2:T(1,128)}, u32[]{:S(2)}, u32[]{:S(2)}) %all-to-all-start.22) | async-done | bytes 524320 | tf_op jit(solution)/shard_map/all_to_all | solution.py:80
  727.8 11.0 all-to-all-done.24
  738.8 8.2 all-to-all-start.25
  752.8 9.6 all-to-all-done.25
  777.0 13.9 %all-to-all-done.27 = f32[2,2,1,128,512]{4,1,0,2,3:T(2,128)} async-done(((f32[2,2,1,128,512]{4,1,0,2,3:T(2,128)}), f32[2,2,1,128,512]{4,1,0,2,3:T(2,128)}, u32[]{:S(2)}, u32[]{:S(2)}) %all-to-all-start.27) | async-done | bytes 1048608 | tf_op jit(solution)/shard_map/all_to_all | solution.py:107
  807.7 11.8 all-to-all-done.28
  839.7 10.6 all-to-all-start.29
  850.3 350.1 %all-reduce = (f32[512]{0:T(512)}, f32[512]{0:T(512)}, f32[512]{0:T(512)}, f32[512]{0:T(512)}) all-reduce(f32[512]{0:T(512)S(1)} %copy-done.46, f32[512]{0:T(512)S(1)} %copy-done.45, f32[512]{0:T(512)} %get-tuple-element.12, f32[512]{0:T(512)S(1)} %copy-done.47), channel_id=1, replica_groups=mesh['seq'=128,'section'=2] {'seq'}, use_global_device_ids=true, to_apply=%region_5.6 | all-reduce | flops 2048 | bytes 16384 | tf_op jit(solution)/shard_map/psum | solution.py:163
  (310 shorter events, 352.6 us)
Async XLA Ops:
  6.1 29.9 %all-to-all-start.3 = ((f32[1,1,128,512]{3,1,0,2:T(1,128)}), f32[1,1,128,512]{3,1,0,2:T(1,128)S(1)}, u32[]{:S(2)}, u32[]{:S(2)}) async-start(f32[1,1,128,512]{3,1,0,2:T(1,128)} %copy.51), calls=%async_computation.3 | async-start | bytes 524288 | tf_op jit(solution)/shard_map/all_to_all | solution.py:51
  36.0 35.9 %all-to-all-start = ((f32[4,1,128,512]{3,0,1,2:T(4,128)}), f32[4,1,128,512]{3,0,1,2:T(4,128)S(1)}, u32[]{:S(2)}, u32[]{:S(2)}) async-start(f32[4,1,128,512]{3,0,1,2:T(4,128)} %copy.45), calls=%async_computation | async-start | bytes 2097152 | tf_op jit(solution)/shard_map/all_to_all | solution.py:51
  71.9 25.3 %all-to-all-start.4 = ((f32[1,2,128,1,512]{4,3,1,0,2:T(1,128)}), f32[1,2,128,1,512]{4,3,1,0,2:T(1,128)}, u32[]{:S(2)}, u32[]{:S(2)}) async-start(f32[1,2,128,1,512]{4,3,1,0,2:T(1,128)} %copy.52), calls=%async_computation.4 | async-start | bytes 1048576 | tf_op jit(solution)/shard_map/all_to_all | solution.py:80
  97.2 23.5 %all-to-all-start.5 = ((f32[1,2,128,1,512]{4,3,1,0,2:T(1,128)}), f32[1,2,128,1,512]{4,3,1,0,2:T(1,128)S(1)}, u32[]{:S(2)}, u32[]{:S(2)}) async-start(f32[1,2,128,1,512]{4,3,1,0,2:T(1,128)} %copy.54), calls=%async_computation.5 | async-start | bytes 1048576 | tf_op jit(solution)/shard_map/all_to_all | solution.py:81
  120.7 56.4 %all-to-all-start.2 = ((f32[4,2,128,1,512]{4,0,3,1,2:T(4,128)}), f32[4,2,128,1,512]{4,0,3,1,2:T(4,128)}, u32[]{:S(2)}, u32[]{:S(2)}) async-start(f32[4,2,128,1,512]{4,0,3,1,2:T(4,128)} %copy.49), calls=%async_computation.2 | async-start | bytes 4194304 | tf_op jit(solution)/shard_map/all_to_all | solution.py:81
  177.1 56.2 %all-to-all-start.1 = ((f32[4,2,128,1,512]{4,0,3,1,2:T(4,128)}), f32[4,2,128,1,512]{4,0,3,1,2:T(4,128)}, u32[]{:S(2)}, u32[]{:S(2)}) async-start(f32[4,2,128,1,512]{4,0,3,1,2:T(4,128)} %copy.47), calls=%async_computation.1 | async-start | bytes 4194304 | tf_op jit(solution)/shard_map/all_to_all | solution.py:80
  189.0 54.2 %copy-start.6 = (f32[1,2,1,128,512]{3,4,1,0,2:T(8,128)}, f32[1,2,1,128,512]{3,4,1,0,2:T(8,128)S(1)}, u32[]{:S(2)}) copy-start(f32[1,2,1,128,512]{3,4,1,0,2:T(8,128)S(1)} %fusion.40) | copy-start | bytes 1572868
  247.6 24.3 %all-to-all-start.6 = ((f32[1,2,1,128,512]{4,1,2,0,3:T(2,128)}), f32[1,2,1,128,512]{4,1,2,0,3:T(2,128)}, u32[]{:S(2)}, u32[]{:S(2)}) async-start(f32[1,2,1,128,512]{4,1,2,0,3:T(2,128)} %copy.56), calls=%async_computation.6 | async-start | bytes 1048576 | tf_op jit(solution)/shard_map/all_to_all | solution.py:107
  272.0 22.8 %all-to-all-start.7 = ((f32[1,2,1,128,512]{4,1,2,0,3:T(2,128)}), f32[1,2,1,128,512]{4,1,2,0,3:T(2,128)S(1)}, u32[]{:S(2)}, u32[]{:S(2)}) async-start(f32[1,2,1,128,512]{4,1,2,0,3:T(2,128)} %copy.58), calls=%async_computation.7 | async-start | bytes 1048576 | tf_op jit(solution)/shard_map/all_to_all | solution.py:108
  299.7 19.7 %all-to-all-start.8 = ((f32[1,128,1,512]{3,2,0,1:T(1,128)}), f32[1,128,1,512]{3,2,0,1:T(1,128)S(1)}, u32[]{:S(2)}, u32[]{:S(2)}) async-start(f32[1,128,1,512]{3,2,0,1:T(1,128)} %copy.60), calls=%async_computation.8 | async-start | bytes 524288 | tf_op jit(solution)/shard_map/all_to_all | solution.py:117
  345.9 22.5 %all-to-all-start.10 = ((f32[1,2,128,1,512]{4,3,1,0,2:T(1,128)}), f32[1,2,128,1,512]{4,3,1,0,2:T(1,128)S(1)}, u32[]{:S(2)}, u32[]{:S(2)}) async-start(f32[1,2,128,1,512]{4,3,1,0,2:T(1,128)} %copy.62), calls=%async_computation.10 | async-start | bytes 1048576 | tf_op jit(solution)/shard_map/all_to_all | solution.py:80
  368.4 23.5 %all-to-all-start.11 = ((f32[1,2,128,1,512]{4,3,1,0,2:T(1,128)}), f32[1,2,128,1,512]{4,3,1,0,2:T(1,128)}, u32[]{:S(2)}, u32[]{:S(2)}) async-start(f32[1,2,128,1,512]{4,3,1,0,2:T(1,128)} %copy.64), calls=%async_computation.11 | async-start | bytes 1048576 | tf_op jit(solution)/shard_map/all_to_all | solution.py:81
  400.5 22.7 %all-to-all-start.12 = ((f32[1,2,1,128,512]{4,1,2,0,3:T(2,128)}), f32[1,2,1,128,512]{4,1,2,0,3:T(2,128)S(1)}, u32[]{:S(2)}, u32[]{:S(2)}) async-start(f32[1,2,1,128,512]{4,1,2,0,3:T(2,128)} %copy.66), calls=%async_computation.12 | async-start | bytes 1048576 | tf_op jit(solution)/shard_map/all_to_all | solution.py:107
  423.2 22.9 %all-to-all-start.13 = ((f32[1,2,1,128,512]{4,1,2,0,3:T(2,128)}), f32[1,2,1,128,512]{4,1,2,0,3:T(2,128)S(1)}, u32[]{:S(2)}, u32[]{:S(2)}) async-start(f32[1,2,1,128,512]{4,1,2,0,3:T(2,128)} %copy.68), calls=%async_computation.13 | async-start | bytes 1048576 | tf_op jit(solution)/shard_map/all_to_all | solution.py:108
  470.7 3.2 collective-permute-start
  502.3 25.5 %all-to-all-start.17 = ((f32[1,2,128,1,512]{4,3,1,0,2:T(1,128)}), f32[1,2,128,1,512]{4,3,1,0,2:T(1,128)S(1)}, u32[]{:S(2)}, u32[]{:S(2)}) async-start(f32[1,2,128,1,512]{4,3,1,0,2:T(1,128)} %copy.74), calls=%async_computation.17 | async-start | bytes 1048576 | tf_op jit(solution)/shard_map/all_to_all | solution.py:81
  527.8 25.2 %all-to-all-start.16 = ((f32[1,2,128,1,512]{4,3,1,0,2:T(1,128)}), f32[1,2,128,1,512]{4,3,1,0,2:T(1,128)}, u32[]{:S(2)}, u32[]{:S(2)}) async-start(f32[1,2,128,1,512]{4,3,1,0,2:T(1,128)} %copy.72), calls=%async_computation.16 | async-start | bytes 1048576 | tf_op jit(solution)/shard_map/all_to_all | solution.py:80
  562.2 23.5 %all-to-all-start.18 = ((f32[1,2,1,128,512]{4,1,2,0,3:T(2,128)}), f32[1,2,1,128,512]{4,1,2,0,3:T(2,128)S(1)}, u32[]{:S(2)}, u32[]{:S(2)}) async-start(f32[1,2,1,128,512]{4,1,2,0,3:T(2,128)} %copy.76), calls=%async_computation.18 | async-start | bytes 1048576 | tf_op jit(solution)/shard_map/all_to_all | solution.py:107
  585.7 23.1 %all-to-all-start.19 = ((f32[1,2,1,128,512]{4,1,2,0,3:T(2,128)}), f32[1,2,1,128,512]{4,1,2,0,3:T(2,128)S(1)}, u32[]{:S(2)}, u32[]{:S(2)}) async-start(f32[1,2,1,128,512]{4,1,2,0,3:T(2,128)} %copy.78), calls=%async_computation.19 | async-start | bytes 1048576 | tf_op jit(solution)/shard_map/all_to_all | solution.py:108
  660.2 22.5 %all-to-all-start.23 = ((f32[1,2,128,1,512]{4,3,1,0,2:T(1,128)}), f32[1,2,128,1,512]{4,3,1,0,2:T(1,128)S(1)}, u32[]{:S(2)}, u32[]{:S(2)}) async-start(f32[1,2,128,1,512]{4,3,1,0,2:T(1,128)} %copy.84), calls=%async_computation.23 | async-start | bytes 1048576 | tf_op jit(solution)/shard_map/all_to_all | solution.py:81
  682.7 23.5 %all-to-all-start.22 = ((f32[1,2,128,1,512]{4,3,1,0,2:T(1,128)}), f32[1,2,128,1,512]{4,3,1,0,2:T(1,128)}, u32[]{:S(2)}, u32[]{:S(2)}) async-start(f32[1,2,128,1,512]{4,3,1,0,2:T(1,128)} %copy.82), calls=%async_computation.22 | async-start | bytes 1048576 | tf_op jit(solution)/shard_map/all_to_all | solution.py:80
  715.4 23.3 %all-to-all-start.24 = ((f32[1,2,1,128,512]{4,1,2,0,3:T(2,128)}), f32[1,2,1,128,512]{4,1,2,0,3:T(2,128)}, u32[]{:S(2)}, u32[]{:S(2)}) async-start(f32[1,2,1,128,512]{4,1,2,0,3:T(2,128)} %copy.86), calls=%async_computation.24 | async-start | bytes 1048576 | tf_op jit(solution)/shard_map/all_to_all | solution.py:107
  738.8 23.6 %all-to-all-start.25 = ((f32[1,2,1,128,512]{4,1,2,0,3:T(2,128)}), f32[1,2,1,128,512]{4,1,2,0,3:T(2,128)}, u32[]{:S(2)}, u32[]{:S(2)}) async-start(f32[1,2,1,128,512]{4,1,2,0,3:T(2,128)} %copy.88), calls=%async_computation.25 | async-start | bytes 1048576 | tf_op jit(solution)/shard_map/all_to_all | solution.py:108
  762.4 28.6 %all-to-all-start.27 = ((f32[2,2,1,128,512]{4,1,0,2,3:T(2,128)}), f32[2,2,1,128,512]{4,1,0,2,3:T(2,128)}, u32[]{:S(2)}, u32[]{:S(2)}) async-start(f32[2,2,1,128,512]{4,1,0,2,3:T(2,128)} %copy.91), calls=%async_computation.27 | async-start | bytes 2097152 | tf_op jit(solution)/shard_map/all_to_all | solution.py:107
  790.9 28.6 %all-to-all-start.28 = ((f32[2,2,1,128,512]{4,1,0,2,3:T(2,128)}), f32[2,2,1,128,512]{4,1,0,2,3:T(2,128)}, u32[]{:S(2)}, u32[]{:S(2)}) async-start(f32[2,2,1,128,512]{4,1,0,2,3:T(2,128)} %copy.93), calls=%async_computation.28 | async-start | bytes 2097152 | tf_op jit(solution)/shard_map/all_to_all | solution.py:108
  819.5 20.2 %all-to-all-start.26 = ((f32[1,128,1,512]{3,2,0,1:T(1,128)}), f32[1,128,1,512]{3,2,0,1:T(1,128)S(1)}, u32[]{:S(2)}, u32[]{:S(2)}) async-start(f32[1,128,1,512]{3,2,0,1:T(1,128)} %copy.90), calls=%async_computation.26 | async-start | bytes 524288 | tf_op jit(solution)/shard_map/all_to_all | solution.py:117
  834.5 367.9 %copy-start.25 = (f32[128,512]{1,0:T(8,128)S(1)}, f32[128,512]{1,0:T(8,128)}, u32[]{:S(2)}) copy-start(f32[128,512]{1,0:T(8,128)} %copy-done.24) | copy-start | bytes 786436
  834.5 367.9 %copy-start.29 = (bf16[1,2,128,512]{3,2,1,0:T(8,128)(2,1)S(1)}, bf16[1,2,128,512]{3,2,1,0:T(8,128)(2,1)}, u32[]{:S(2)}) copy-start(bf16[1,2,128,512]{3,2,1,0:T(8,128)(2,1)} %param.8) | copy-start | bytes 786436
  834.5 367.9 %copy-start.43 = (f32[1,1,512]{2,1,0:T(1,128)S(1)}, f32[1,1,512]{2,1,0:T(1,128)}, u32[]{:S(2)}) copy-start(f32[1,1,512]{2,1,0:T(1,128)} %get-tuple-element.62) | copy-start | bytes 6148
  835.3 367.1 %copy-start.39 = (bf16[128,512]{1,0:T(8,128)(2,1)S(1)}, bf16[128,512]{1,0:T(8,128)(2,1)}, u32[]{:S(2)}) copy-start(bf16[128,512]{1,0:T(8,128)(2,1)} %copy-done.38) | copy-start | bytes 393220
  835.3 367.1 %copy-start.40 = (bf16[128,512]{1,0:T(8,128)(2,1)S(1)}, bf16[128,512]{1,0:T(8,128)(2,1)}, u32[]{:S(2)}) copy-start(bf16[128,512]{1,0:T(8,128)(2,1)} %get-tuple-element.52) | copy-start | bytes 393220
  839.7 364.1 %all-to-all-start.29 = ((f32[2,128,1,512]{3,0,2,1:T(2,128)}), f32[2,128,1,512]{3,0,2,1:T(2,128)S(1)}, u32[]{:S(2)}, u32[]{:S(2)}) async-start(f32[2,128,1,512]{3,0,2,1:T(2,128)} %copy.95), calls=%async_computation.29 | async-start | bytes 1048576 | tf_op jit(solution)/shard_map/all_to_all | solution.py:117
  (44 other events, 548.7 us)
where the time goes:
time: 1220 us; the launch traced here: 1210 us
  blocking collectives  450 us (37%)
  waiting for transfers between devices  368 us (30%)
  starting transfers between devices  197 us (16%)
  matrix products  110 us (9%)
  local copies, waits for them, and re-layouts  63.9 us (5%)
  other arithmetic  12.3 us (1%)
    psum x1, blocking collectives, run_tick(): sum_two = lax.psum(sum_two, 'seq')  350 us
    all_to_all x5, waiting for transfers between devices, to_spectrum(): lax.all_to_all(turned_imag, 'seq', split_axis=2, concat_axis=3, tiled=True)  97.7 us
    all_to_all x5, waiting for transfers between devices, to_spectrum(): lax.all_to_all(turned_real, 'seq', split_axis=2, concat_axis=3, tiled=True)  85.4 us
    all_to_all x5, waiting for transfers between devices, from_spectrum(): lax.all_to_all(back_imag, 'seq', split_axis=3, concat_axis=2, tiled=True)  67.5 us
    all_to_all x5, waiting for transfers between devices, from_spectrum(): lax.all_to_all(back_real, 'seq', split_axis=3, concat_axis=2, tiled=True)  65.8 us
    all_to_all x3, blocking collectives, to_spectrum(): lax.all_to_all(signals.reshape(signal_count, 1, row_count, channels), 'se...  61.1 us
    dot_general x60, matrix products, across_parts(): return jnp.einsum('bp,kprd->kbrd', matrix, operand, precision=HIGHEST)  46.9 us
    all_to_all x5, starting transfers between devices, to_spectrum(): lax.all_to_all(turned_real, 'seq', split_axis=2, concat_axis=3, tiled=True)  39 us
  transfers between devices with their start and end apart: 26, of which 25 were waited for; matrix products, arithmetic and copies ran while one was open for 9% of the time, Pallas kernels for 0%

commit v1 on v0

v1 whole, which is shorter than its diff:
```python
import functools
import math

import jax
import jax.numpy as jnp
import ml_dtypes
import numpy as np
from jax import lax
from jax.experimental import pallas as pl
from jax.experimental.pallas import tpu as pltpu
from jax.sharding import PartitionSpec as P

BF = jnp.bfloat16
F32 = jnp.float32
VMEM_LIMIT = 48 * 1024 * 1024


def split_table(table, axis):
    high = table.astype(np.float32).astype(ml_dtypes.bfloat16)
    low = (table - high.astype(np.float64)).astype(np.float32).astype(ml_dtypes.bfloat16)
    return np.concatenate([high, low], axis=axis)


def transform_tables(blocks, width):
    period = 2 * blocks * width
    half = np.arange(blocks) + 0.5
    outer = 2.0 * np.pi * np.outer(half, np.arange(blocks)) / (2 * blocks)
    inner = 2.0 * np.pi * np.outer(np.arange(width), np.arange(width)) / width
    turn = 2.0 * np.pi * np.outer(half, np.arange(width)) / period
    cos_in, sin_in = np.cos(inner), np.sin(inner)
    outer_fwd = split_table(np.concatenate([np.cos(outer), -np.sin(outer)], 0), 1)
    inner_fwd = split_table(np.block([[cos_in, -sin_in], [sin_in, cos_in]]), 0)
    inner_inv = split_table(np.block([[cos_in, sin_in], [-sin_in, cos_in]]), 0)
    outer_inv = split_table(
        np.concatenate([np.cos(outer).T, -np.sin(outer).T], 1) * (2.0 / period), 1
    )
    turns = np.stack([np.cos(turn), np.sin(turn)]).astype(np.float32)
    return outer_fwd, inner_fwd, inner_inv, outer_inv, turns


def mm(left, right):
    return jnp.dot(left, right, preferred_element_type=F32)


def mm_t(left, right):
    return lax.dot_general(left, right, (((1,), (1,)), ((), ())), preferred_element_type=F32)


def to_spectrum(signals, outer, inner, turns):
    count = len(signals)
    size = signals[0].shape[0]
    width = signals[0].shape[1]
    data = jnp.concatenate([signal.astype(BF) for signal in signals], axis=1)
    mixed = mm(outer[...], jnp.concatenate([data, data], axis=0))
    turn_cos, turn_sin = turns[0], turns[1]
    rows = []
    for c in range(count):
        real = mixed[:size, c * width : (c + 1) * width]
        imag = mixed[size:, c * width : (c + 1) * width]
        rows.append(
            jnp.concatenate(
                [real * turn_cos + imag * turn_sin, imag * turn_cos - real * turn_sin], axis=1
            ).astype(BF)
        )
    turned = jnp.concatenate(rows, axis=0)
    return mm(jnp.concatenate([turned, turned], axis=1), inner[...])


def conj_times(left, right):
    width = left.shape[1] // 2
    left_real, left_imag = left[:, :width], left[:, width:]
    right_real, right_imag = right[:, :width], right[:, width:]
    return jnp.concatenate(
        [
            left_real * right_real + left_imag * right_imag,
            left_real * right_imag - left_imag * right_real,
        ],
        axis=1,
    )


def from_spectrum(product, inner, outer, turns):
    width = product.shape[1] // 2
    size = turns.shape[1]
    count = product.shape[0] // size
    data = product.astype(BF)
    mixed = mm(jnp.concatenate([data, data], axis=1), inner[...])
    turn_cos, turn_sin = turns[0], turns[1]
    reals, imags = [], []
    for c in range(count):
        real = mixed[c * size : (c + 1) * size, :width]
        imag = mixed[c * size : (c + 1) * size, width:]
        reals.append((real * turn_cos - imag * turn_sin).astype(BF))
        imags.append((imag * turn_cos + real * turn_sin).astype(BF))
    turned = jnp.concatenate(
        [jnp.concatenate(reals, axis=1), jnp.concatenate(imags, axis=1)], axis=0
    )
    result = mm(outer[...], jnp.concatenate([turned, turned], axis=0))
    return [result[:, c * width : (c + 1) * width] for c in range(count)]


def put_rows(scratch, value, first, stride):
    size = value.shape[0]
    for k in range(value.shape[1] // size):
        block = value[:, k * size : (k + 1) * size].astype(F32).T
        scratch[pl.ds(first + k, size, stride=stride), :] = block


def get_rows(scratch, first, stride, count):
    size = scratch.shape[1]
    return jnp.concatenate(
        [scratch[pl.ds(first + k, size, stride=stride), :].T for k in range(count)], axis=1
    )


def prepare_body(rows, conv, filt, w_in, w_out, inc, packed, gate_two_out, part_two_out, scratch):
    channels = rows.shape[1]
    per = channels // rows.shape[0]
    stride = 6 * per
    projected = mm(rows[...], w_in[...]).astype(BF)
    values = projected[:, :channels]
    gate_one = projected[:, channels : 2 * channels]
    gate_two = projected[:, 2 * channels :]
    mix_two = mm_t(inc[...], w_out[...])
    gate_two_out[...] = gate_two
    part_two_out[...] = (mix_two * conv[1].astype(F32)).astype(BF)
    put_rows(scratch, filt[0], 0, stride)
    put_rows(scratch, filt[1], per, stride)
    put_rows(scratch, values, 2 * per, stride)
    put_rows(scratch, gate_one, 3 * per, stride)
    put_rows(scratch, conv[0], 4 * per, stride)
    put_rows(scratch, mix_two * gate_two.astype(F32), 5 * per, stride)
    packed[...] = scratch[...].astype(BF)


def regrad_body(inc, w_out, gate_two, conv_two, packed, part_two_out, scratch):
    per = inc.shape[1] // inc.shape[0]
    mix_two = mm_t(inc[...], w_out[...])
    part_two_out[...] = (mix_two * conv_two[...].astype(F32)).astype(BF)
    put_rows(scratch, mix_two * gate_two[...].astype(F32), 0, per)
    packed[...] = scratch[...].astype(BF)


def early_body(
    per, gains, data, outer_fwd, inner_fwd, inner_inv, outer_inv, turns, packed, filt_out, known, out
):
    size = data.shape[1]
    known[...] = data[...].astype(F32)

    def signals(s):
        return [known[pl.ds(s * per + k, size, stride=6 * per), :] for k in range(per)]

    grad_two = signals(5)
    filt_two = to_spectrum(signals(1), outer_fwd, inner_fwd, turns)
    filt_out[1] = filt_two
    spec_two = to_spectrum(grad_two, outer_fwd, inner_fwd, turns)
    mixed = from_spectrum(conj_times(filt_two, spec_two), inner_inv, outer_inv, turns)
    mix_one = [mixed[k] + gains[1, k] * grad_two[k] for k in range(per)]
    conv_one, gate_one = signals(4), signals(3)
    for k in range(per):
        out[pl.ds(per + k, size, stride=2 * per), :] = mix_one[k] * conv_one[k]
    grad_one = [mix_one[k] * gate_one[k] for k in range(per)]
    filt_one = to_spectrum(signals(0), outer_fwd, inner_fwd, turns)
    filt_out[0] = filt_one
    spec_one = to_spectrum(grad_one, outer_fwd, inner_fwd, turns)
    mixed = from_spectrum(conj_times(filt_one, spec_one), inner_inv, outer_inv, turns)
    for k in range(per):
        out[pl.ds(k, size, stride=2 * per), :] = mixed[k] + gains[0, k] * grad_one[k]
    packed[...] = out[...].astype(BF)


def known_body(per, data, outer_fwd, inner_fwd, turns, spec_out, known):
    size = data.shape[1]
    known[...] = data[...].astype(F32)

    def signals(s):
        return [known[pl.ds(s * per + k, size, stride=6 * per), :] for k in range(per)]

    spec_out[0] = to_spectrum(signals(2), outer_fwd, inner_fwd, turns)
    gated = [gate * conv for gate, conv in zip(signals(3), signals(4))]
    spec_out[1] = to_spectrum(gated, outer_fwd, inner_fwd, turns)


def late_body(
    per,
    gains,
    data,
    fresh,
    filt,
    spec,
    outer_fwd,
    inner_fwd,
    inner_inv,
    outer_inv,
    turns,
    packed,
    known,
    fresh_known,
    out,
):
    size = data.shape[1]
    rows = out.shape[0] // size
    known[...] = data[...].astype(F32)
    fresh_known[...] = fresh[...].astype(F32)

    def signals(s):
        return [known[pl.ds(s * per + k, size, stride=6 * per), :] for k in range(per)]

    def send(s, values):
        for k in range(per):
            out[pl.ds(s * per + k, size, stride=rows), :] = values[k]

    grad_two = [fresh_known[pl.ds(k, size, stride=per), :] for k in range(per)]
    spec_two = to_spectrum(grad_two, outer_fwd, inner_fwd, turns)
    mixed = from_spectrum(conj_times(filt[1], spec_two), inner_inv, outer_inv, turns)
    send(3, from_spectrum(conj_times(spec[1], spec_two), inner_inv, outer_inv, turns))
    mix_one = [mixed[k] + gains[1, k] * grad_two[k] for k in range(per)]
    conv_one, gate_one = signals(4), signals(3)
    send(1, [mix_one[k] * conv_one[k] for k in range(per)])
    grad_one = [mix_one[k] * gate_one[k] for k in range(per)]
    spec_one = to_spectrum(grad_one, outer_fwd, inner_fwd, turns)
    mixed = from_spectrum(conj_times(filt[0], spec_one), inner_inv, outer_inv, turns)
    send(2, from_spectrum(conj_times(spec[0], spec_one), inner_inv, outer_inv, turns))
    send(0, [mixed[k] + gains[0, k] * grad_one[k] for k in range(per)])
    values = signals(2)
    lane = lax.broadcasted_iota(jnp.int32, (1, size), 1)
    skip_row = jnp.zeros((1, size), F32)
    for k in range(per):
        for w, term in ((0, grad_one[k] * values[k]), (1, grad_two[k] * (gate_one[k] * conv_one[k]))):
            total = jnp.sum(jnp.sum(term, axis=0, keepdims=True), axis=1, keepdims=True)
            high = total.astype(BF).astype(F32)
            skip_row = jnp.where(lane == w * per + k, high, skip_row)
            skip_row = jnp.where(lane == (2 + w) * per + k, total - high, skip_row)
    out[pl.ds(4 * per, size, stride=rows), :] = jnp.broadcast_to(skip_row, (size, size))
    for r in range(4 * per + 1, rows):
        out[pl.ds(r, size, stride=rows), :] = jnp.zeros((size, size), F32)
    packed[...] = out[...].astype(BF)


def input_grad(inc, values, gate_one, part_two, w_in):
    proj = jnp.concatenate([values.astype(BF), gate_one.astype(BF), part_two], axis=1)
    return (inc.astype(F32) + mm_t(proj, w_in)).astype(BF)


def hand_body(per, data, part_two, inc, w_in, result, scratch):
    scratch[...] = data[...].astype(F32)
    values = get_rows(scratch, 0, 2 * per, per)
    gate_one = get_rows(scratch, per, 2 * per, per)
    result[...] = input_grad(inc[...], values, gate_one, part_two[...], w_in[...])


def finish_body(per, rescale, data, part_two, inc, w_in, result, filt_grads, skip_grads, scratch):
    size = data.shape[1]
    stride = data.shape[0] // size
    scratch[...] = data[...].astype(F32)
    values = get_rows(scratch, 0, stride, per)
    gate_one = get_rows(scratch, per, stride, per)
    result[...] = input_grad(inc[...], values, gate_one, part_two[...], w_in[...])
    filt_grads[0] = (get_rows(scratch, 2 * per, stride, per) * rescale).astype(BF)
    filt_grads[1] = (get_rows(scratch, 3 * per, stride, per) * rescale).astype(BF)
    sums = scratch[pl.ds(4 * per, size, stride=stride), :].T
    sums = (sums[: 2 * per] + sums[2 * per : 4 * per]) * rescale
    for w in range(2):
        for k in range(per):
            row = w * per + k
            skip_grads[pl.ds(w, 1), pl.ds(k * size, size)] = sums[row : row + 1]


def call(body, out_shapes, scratch, *operands, smem=0):
    specs = [
        pl.BlockSpec(memory_space=pltpu.SMEM if i < smem else pltpu.VMEM)
        for i in range(len(operands))
    ]
    return pl.pallas_call(
        body,
        out_shape=[jax.ShapeDtypeStruct(shape, dtype) for shape, dtype in out_shapes],
        in_specs=specs,
        out_specs=[pl.BlockSpec(memory_space=pltpu.VMEM) for _ in out_shapes],
        scratch_shapes=[pltpu.VMEM(shape, F32) for shape in scratch],
        compiler_params=pltpu.CompilerParams(vmem_limit_bytes=VMEM_LIMIT),
    )(*operands)


def exchange(rows):
    return lax.all_to_all(rows, "seq", split_axis=0, concat_axis=0, tiled=True)


def on_device(layer_input, conv_out, filters, skip_gain, weight_in, weight_out, grad_output):
    tokens, channels = grad_output.shape
    parts = lax.axis_size("seq")
    per = channels // parts
    w_in, w_out, conv = weight_in[0], weight_out[0], conv_out[0]
    outer_fwd, inner_fwd, inner_inv, outer_inv, turns = transform_tables(parts, tokens)
    is_late = lax.axis_index("section") == 1
    own = lax.dynamic_slice_in_dim(
        skip_gain[0].reshape(2, per, parts), lax.axis_index("seq"), 1, axis=2
    )[:, :, 0]
    token_rows = ((tokens, channels), BF)
    spectra = ((2, per * parts, 2 * tokens), F32)

    packed, gate_two, part_two = call(
        prepare_body,
        [((parts * 6 * per, tokens), BF), token_rows, token_rows],
        [(parts * 6 * per, tokens)],
        layer_input[0], conv, filters[0], w_in, w_out, grad_output,
    )
    data = exchange(packed)
    packed, filt = call(
        functools.partial(early_body, per),
        [((parts * 2 * per, tokens), BF), spectra],
        [(parts * 6 * per, tokens), (parts * 2 * per, tokens)],
        own, data, outer_fwd, inner_fwd, inner_inv, outer_inv, turns,
        smem=1,
    )
    back = exchange(packed)
    (spec,) = call(
        functools.partial(known_body, per),
        [spectra],
        [(parts * 6 * per, tokens)],
        data, outer_fwd, inner_fwd, turns,
    )
    (late,) = call(
        functools.partial(hand_body, per),
        [token_rows],
        [(parts * 2 * per, tokens)],
        back, part_two, grad_output, w_in,
    )
    handed = lax.ppermute(late, "section", [(1, 0)])
    incoming = jnp.where(is_late, grad_output, handed)
    packed, part_two = call(
        regrad_body,
        [((parts * per, tokens), BF), token_rows],
        [(parts * per, tokens)],
        incoming, w_out, gate_two, conv[1],
    )
    fresh = exchange(packed)
    out_rows = 8 * ((4 * per + 1 + 7) // 8)
    (packed,) = call(
        functools.partial(late_body, per),
        [((parts * out_rows, tokens), BF)],
        [(parts * 6 * per, tokens), (parts * per, tokens), (parts * out_rows, tokens)],
        own, data, fresh, filt, spec, outer_fwd, inner_fwd, inner_inv, outer_inv, turns,
        smem=1,
    )
    back = exchange(packed)
    grad_rows, filter_grads, skip_grads = call(
        functools.partial(finish_body, per, 1.0 / math.sqrt(parts * tokens)),
        [token_rows, ((2, tokens, channels), BF), ((2, channels), F32)],
        [(parts * out_rows, tokens)],
        back, part_two, incoming, w_in,
    )
    return (grad_rows[None], filter_grads[None], skip_grads[None])


def solution(mesh):
    in_specs = (
        P("section", "seq", None),
        P("section", None, "seq", None),
        P("section", None, "seq", None),
        P("section", None, None),
        P("section", None, None),
        P("section", None, None),
        P("seq", None),
    )
    out_specs = (
        P("section", "seq", None),
        P("section", None, "seq", None),
        P("section", None, None),
    )
    return jax.shard_map(
        on_device, mesh=mesh, in_specs=in_specs, out_specs=out_specs, check_vma=False
    )
```

time: 1220 us -> 144 us (0.12); the launches traced: 1210 us -> 142 us
  blocking collectives: 450 us -> 30.7 us
  waiting for transfers between devices: 368 us -> 50 us
  starting transfers between devices: 197 us -> 31.4 us
  matrix products: 110 us -> 0 us
  local copies, waits for them, and re-layouts: 63.9 us -> 18 us
  other arithmetic: 12.3 us -> 0.02 us
    psum x1 -> x0, blocking collectives: 350 us -> none  [run_tick(): sum_two = lax.psum(sum_two, 'seq')]
    all_to_all x25 -> x3, waiting for transfers between devices: 366 us -> 48.1 us  [exchange(): return lax.all_to_all(rows, 'seq', split_axis=0, concat_axis=0, tiled=True)]
    all_to_all x25 -> x3, starting transfers between devices: 196 us -> 30.1 us  [exchange(): return lax.all_to_all(rows, 'seq', split_axis=0, concat_axis=0, tiled=True)]
    dot_general x105 -> x0, matrix products: 110 us -> none  [the longest x60 46.9 us: across_parts(): return jnp.einsum('bp,kprd->kbrd', matrix, operand, precision=HIGHEST)]
    all_to_all x5 -> x1, blocking collectives: 99.9 us -> 30.7 us  [exchange(): return lax.all_to_all(rows, 'seq', split_axis=0, concat_axis=0, tiled=True)]
    all_to_all x21 -> x0, local copies, waits for them, and re-layouts: 22.8 us -> none  [the longest x5 7.21 us: to_spectrum(): lax.all_to_all(turned_real, 'seq', split_axis=2, concat_axis=3, tiled=True)]
    add x10 -> x0, local copies, waits for them, and re-layouts: 15.8 us -> none  [the longest x5 8.35 us: to_spectrum(): turned_real = real_part * twid_cos + imag_part * twid_sin]
    sub x10 -> x0, local copies, waits for them, and re-layouts: 14.6 us -> none  [the longest x5 8.23 us: to_spectrum(): turned_imag = imag_part * twid_cos - real_part * twid_sin]
  transfers between devices with their start and end apart: 26 -> 4, of which waited for: 25 -> 4; matrix products, arithmetic and copies ran while one was open for 9% -> 0% of each run, Pallas kernels for 0% -> 1%
where the time goes in v1:
time: 144 us; the launch traced here: 142 us
  waiting for transfers between devices  50 us (35%)
  starting transfers between devices  31.4 us (22%)
  blocking collectives  30.7 us (21%)
  local copies, waits for them, and re-layouts  18 us (12%)
  Pallas kernels  11.5 us (8%)
    all_to_all x3, waiting for transfers between devices, exchange(): return lax.all_to_all(rows, 'seq', split_axis=0, concat_axis=0, tiled=True)  48.1 us
    all_to_all x1, blocking collectives, exchange(): return lax.all_to_all(rows, 'seq', split_axis=0, concat_axis=0, tiled=True)  30.7 us
    all_to_all x3, starting transfers between devices, exchange(): return lax.all_to_all(rows, 'seq', split_axis=0, concat_axis=0, tiled=True)  30.1 us
    unnamed x65, local copies, waits for them, and re-layouts  17.9 us
    pallas_call x7, Pallas kernels, call(): pl.pallas_call(body, out_shape=[jax.ShapeDtypeStruct(shape, dtype) for sh...  11.5 us
  transfers between devices with their start and end apart: 4, of which 4 were waited for; matrix products, arithmetic and copies ran while one was open for 0% of the time, Pallas kernels for 1%

profile of v1, /device:TPU:8, one launch (start us, length us, event | category | flops | bytes accessed | tf_op | source)
XLA Modules:
  0.0 142.4 jit_solution(17664513220422631646)
XLA Ops:
  0.6 1.4 copy-done
  2.0 1.0 copy-done.5
  3.1 0.9 copy-done.11
  4.0 0.9 copy-done.20
  4.9 0.9 copy-done.25
  5.9 0.9 copy-done.26
  6.8 0.7 shard_map.139
  7.6 0.9 copy-done.19
  9.1 15.5 %all-to-all-start = ((bf16[128,24,128]{2,1,0:T(8,128)(2,1)}), bf16[128,24,128]{2,1,0:T(8,128)(2,1)S(1)}, u32[]{:S(2)}, u32[]{:S(2)}) async-start(bf16[128,24,128]{2,1,0:T(8,128)(2,1)} %bitcast.30), calls=%async_computation | async-start | bytes 1572864 | tf_op jit(solution)/shard_map/all_to_all | solution.py:285
  24.8 25.1 %all-to-all-done = bf16[128,24,128]{2,1,0:T(8,128)(2,1)S(1)} async-done(((bf16[128,24,128]{2,1,0:T(8,128)(2,1)}), bf16[128,24,128]{2,1,0:T(8,128)(2,1)S(1)}, u32[]{:S(2)}, u32[]{:S(2)}) %all-to-all-start) | async-done | bytes 786464 | tf_op jit(solution)/shard_map/all_to_all | solution.py:285
  49.9 2.9 %shard_map.140 = (bf16[1024,128]{1,0:T(8,128)(2,1)S(1)}, f32[2,512,256]{2,1,0:T(8,128)S(1)}) custom-call(f32[2,4]{1,0:T(2,128)S(1)} %bitcast.35, bf16[3072,128]{1,0:T(8,128)(2,1)S(1)} %bitcast.22, bf16[256,256]{1,0:T(8,128)(2,1)S(1)} %copy-done.8, bf16[512,256]{1,0:T(8,128)(2,1)S(1)} %copy-done.2, bf16[512,256]{1,0:T(8,128)(2,1)S(1)} %copy-done.17, ...), custom_call_target="tpu_custom_call" | custom-call | tf_op jit(solution)/shard_map/pallas_call | solution.py:274
  52.8 1.0 copy-done.15
  53.8 0.7 copy-done.24
  54.5 6.9 %all-to-all-start.1 = ((bf16[128,8,128]{2,1,0:T(8,128)(2,1)}), bf16[128,8,128]{2,1,0:T(8,128)(2,1)S(1)}, u32[]{:S(2)}, u32[]{:S(2)}) async-start(bf16[128,8,128]{2,1,0:T(8,128)(2,1)} %bitcast.32), calls=%async_computation.1 | async-start | bytes 524288 | tf_op jit(solution)/shard_map/all_to_all | solution.py:285
  61.4 13.5 %all-to-all-done.1 = bf16[128,8,128]{2,1,0:T(8,128)(2,1)S(1)} async-done(((bf16[128,8,128]{2,1,0:T(8,128)(2,1)}), bf16[128,8,128]{2,1,0:T(8,128)(2,1)S(1)}, u32[]{:S(2)}, u32[]{:S(2)}) %all-to-all-start.1) | async-done | bytes 262176 | tf_op jit(solution)/shard_map/all_to_all | solution.py:285
  75.0 0.9 copy-done.28
  76.6 1.3 collective-permute-start
  77.9 1.9 %collective-permute-done = bf16[128,512]{1,0:T(8,128)(2,1)S(1)} collective-permute-done((bf16[128,512]{1,0:T(8,128)(2,1)S(1)}, bf16[128,512]{1,0:T(8,128)(2,1)S(1)}, u32[]{:S(2)}, u32[]{:S(2)}) %collective-permute-start) | collective-permute-done | bytes 131104 | tf_op jit(solution)/shard_map/ppermute | solution.py:328
  79.9 1.1 shard_map.142
  81.6 7.7 %all-to-all-start.2 = ((bf16[128,4,128]{2,1,0:T(4,128)(2,1)}), bf16[128,4,128]{2,1,0:T(4,128)(2,1)}, u32[]{:S(2)}, u32[]{:S(2)}) async-start(bf16[128,4,128]{2,1,0:T(4,128)(2,1)} %bitcast.11), calls=%async_computation.2 | async-start | bytes 262144 | tf_op jit(solution)/shard_map/all_to_all | solution.py:285
  89.3 0.9 copy-done.3
  90.2 0.9 copy-done.9
  91.2 0.8 shard_map.143.spec
  91.9 9.5 %all-to-all-done.2 = bf16[128,4,128]{2,1,0:T(4,128)(2,1)} async-done(((bf16[128,4,128]{2,1,0:T(4,128)(2,1)}), bf16[128,4,128]{2,1,0:T(4,128)(2,1)}, u32[]{:S(2)}, u32[]{:S(2)}) %all-to-all-start.2) | async-done | bytes 131104 | tf_op jit(solution)/shard_map/all_to_all | solution.py:285
  101.5 0.9 copy-done.4
  102.4 0.9 copy-done.10
  103.3 1.2 copy-done.16
  104.5 0.9 copy-done.18
  105.5 0.9 copy-done.23
  106.4 3.9 %shard_map.144 = bf16[3072,128]{1,0:T(8,128)(2,1)S(1)} custom-call(f32[2,4]{1,0:T(2,128)S(1)} %bitcast.36, bf16[3072,128]{1,0:T(8,128)(2,1)S(1)} %bitcast.24, bf16[512,128]{1,0:T(8,128)(2,1)} %bitcast.12.fresh, f32[2,512,256]{2,1,0:T(8,128)S(1)} %copy-done.16, f32[2,512,256]{2,1,0:T(8,128)S(1)} %shard_map.143.spec, bf16[256,256]{1,0:T(8,128)(2,1)S(1)} %copy-done.10, ...), custom_call_target="tpu_custom_call" | custom-call | tf_op jit(solution)/shard_map/pallas_call | solution.py:274
  110.3 30.7 %all_to_all.44 = bf16[128,24,128]{2,1,0:T(8,128)(2,1)S(1)} all-to-all(bf16[128,24,128]{2,1,0:T(8,128)(2,1)S(1)} %bitcast.25), channel_id=1, replica_groups=mesh['seq'=128,'section'=2] {'seq'}, dimensions={0} | all-to-all | bytes 1572864 | tf_op jit(solution)/shard_map/all_to_all | solution.py:285
  141.0 1.4 %shard_map.145 = (bf16[128,512]{1,0:T(8,128)(2,1)}, bf16[2,128,512]{2,1,0:T(8,128)(2,1)}, f32[2,512]{1,0:T(2,128)}) custom-call(bf16[3072,128]{1,0:T(8,128)(2,1)S(1)} %bitcast.26, bf16[128,512]{1,0:T(8,128)(2,1)S(1)} %copy-done.30, bf16[128,512]{1,0:T(8,128)(2,1)S(1)} %copy-done.14, bf16[512,1536]{1,0:T(8,128)(2,1)S(1)} %bitcast.21), custom_call_target="tpu_custom_call" | custom-call | tf_op jit(solution)/shard_map/pallas_call | solution.py:274
  (53 shorter events, 2.3 us)
Async XLA Ops:
  0.6 1.4 copy-start
  2.0 1.0 copy-start.5
  3.1 0.9 copy-start.11
  4.0 0.9 copy-start.20
  4.9 0.9 copy-start.25
  5.9 0.9 copy-start.26
  6.8 17.8 %copy-start.31 = (f32[1,2,512]{2,1,0:T(2,128)S(1)}, f32[1,2,512]{2,1,0:T(2,128)}, u32[]{:S(2)}) copy-start(f32[1,2,512]{2,1,0:T(2,128)} %param.15) | copy-start | bytes 12292
  6.8 43.1 %copy-start.2 = (bf16[512,256]{1,0:T(8,128)(2,1)S(1)}, bf16[512,256]{1,0:T(8,128)(2,1)}, u32[]{:S(2)}) copy-start(bf16[512,256]{1,0:T(8,128)(2,1)} %constant.25.clone.inner_fwd) | copy-start | bytes 786436
  6.8 43.1 %copy-start.7 = (f32[2,128,128]{2,1,0:T(8,128)S(1)}, f32[2,128,128]{2,1,0:T(8,128)}, u32[]{:S(2)}) copy-start(f32[2,128,128]{2,1,0:T(8,128)} %constant.28.clone.turns) | copy-start | bytes 393220
  6.8 43.1 %copy-start.8 = (bf16[256,256]{1,0:T(8,128)(2,1)S(1)}, bf16[256,256]{1,0:T(8,128)(2,1)}, u32[]{:S(2)}) copy-start(bf16[256,256]{1,0:T(8,128)(2,1)} %constant.24.clone.outer_fwd) | copy-start | bytes 393220
  6.8 43.1 %copy-start.17 = (bf16[512,256]{1,0:T(8,128)(2,1)S(1)}, bf16[512,256]{1,0:T(8,128)(2,1)}, u32[]{:S(2)}) copy-start(bf16[512,256]{1,0:T(8,128)(2,1)} %constant.26.clone.inner_inv) | copy-start | bytes 786436
  6.8 43.1 %copy-start.22 = (bf16[128,512]{1,0:T(8,128)(2,1)S(1)}, bf16[128,512]{1,0:T(8,128)(2,1)}, u32[]{:S(2)}) copy-start(bf16[128,512]{1,0:T(8,128)(2,1)} %constant.27.clone.outer_inv) | copy-start | bytes 393220
  7.6 0.9 copy-start.19
  9.1 65.8 %copy-start.1 = (bf16[1,512,1536]{2,1,0:T(8,128)(2,1)S(1)}, bf16[1,512,1536]{2,1,0:T(8,128)(2,1)}, u32[]{:S(2)}) copy-start(bf16[1,512,1536]{2,1,0:T(8,128)(2,1)} %param.16) | copy-start | bytes 4718596
  9.1 65.8 %copy-start.12 = (bf16[128,512]{1,0:T(8,128)(2,1)S(1)}, bf16[128,512]{1,0:T(8,128)(2,1)}, u32[]{:S(2)}) copy-start(bf16[128,512]{1,0:T(8,128)(2,1)} %inc.3) | copy-start | bytes 393220
  9.1 40.7 %all-to-all-start = ((bf16[128,24,128]{2,1,0:T(8,128)(2,1)}), bf16[128,24,128]{2,1,0:T(8,128)(2,1)S(1)}, u32[]{:S(2)}, u32[]{:S(2)}) async-start(bf16[128,24,128]{2,1,0:T(8,128)(2,1)} %bitcast.30), calls=%async_computation | async-start | bytes 1572864 | tf_op jit(solution)/shard_map/all_to_all | solution.py:285
  52.8 1.0 copy-start.15
  54.5 20.5 %all-to-all-start.1 = ((bf16[128,8,128]{2,1,0:T(8,128)(2,1)}), bf16[128,8,128]{2,1,0:T(8,128)(2,1)S(1)}, u32[]{:S(2)}, u32[]{:S(2)}) async-start(bf16[128,8,128]{2,1,0:T(8,128)(2,1)} %bitcast.32), calls=%async_computation.1 | async-start | bytes 524288 | tf_op jit(solution)/shard_map/all_to_all | solution.py:285
  61.4 18.5 %copy-start.6 = (bf16[1,512,512]{2,1,0:T(8,128)(2,1)S(1)}, bf16[1,512,512]{2,1,0:T(8,128)(2,1)}, u32[]{:S(2)}) copy-start(bf16[1,512,512]{2,1,0:T(8,128)(2,1)} %param.17) | copy-start | bytes 1572868
  74.9 2.9 %copy-start.21 = (bf16[1,2,128,512]{3,2,1,0:T(8,128)(2,1)S(1)}, bf16[1,2,128,512]{3,2,1,0:T(8,128)(2,1)}, u32[]{:S(2)}) copy-start(bf16[1,2,128,512]{3,2,1,0:T(8,128)(2,1)} %param.13) | copy-start | bytes 786436
  74.9 0.9 copy-start.28
  76.6 3.2 %collective-permute-start = (bf16[128,512]{1,0:T(8,128)(2,1)S(1)}, bf16[128,512]{1,0:T(8,128)(2,1)S(1)}, u32[]{:S(2)}, u32[]{:S(2)}) collective-permute-start(bf16[128,512]{1,0:T(8,128)(2,1)S(1)} %shard_map.141), channel_id=1, source_target_pairs={{1,0},{3,2},{5,4},{7,6},{9,8},{11,10},{13,12},{15,14},{17,16},{19,... | collective-permute-start | bytes 393224 | tf_op jit(solution)/shard_map/ppermute | solution.py:328
  79.8 1.1 copy-start.13
  81.6 19.8 %all-to-all-start.2 = ((bf16[128,4,128]{2,1,0:T(4,128)(2,1)}), bf16[128,4,128]{2,1,0:T(4,128)(2,1)}, u32[]{:S(2)}, u32[]{:S(2)}) async-start(bf16[128,4,128]{2,1,0:T(4,128)(2,1)} %bitcast.11), calls=%async_computation.2 | async-start | bytes 262144 | tf_op jit(solution)/shard_map/all_to_all | solution.py:285
  89.3 1.0 copy-start.3
  90.2 0.9 copy-start.9
  101.5 1.0 copy-start.4
  102.4 0.9 copy-start.10
  103.3 1.2 copy-start.16
  104.5 0.9 copy-start.18
  110.3 30.7 %copy-start.14 = (bf16[128,512]{1,0:T(8,128)(2,1)S(1)}, bf16[128,512]{1,0:T(8,128)(2,1)}, u32[]{:S(2)}) copy-start(bf16[128,512]{1,0:T(8,128)(2,1)} %copy-done.13) | copy-start | bytes 393220
  110.3 30.7 %copy-start.30 = (bf16[128,512]{1,0:T(8,128)(2,1)S(1)}, bf16[128,512]{1,0:T(8,128)(2,1)}, u32[]{:S(2)}) copy-start(bf16[128,512]{1,0:T(8,128)(2,1)} %copy-done.29) | copy-start | bytes 393220
  (4 other events, 2.9 us)

commit v2 on v1

v2 whole, which is shorter than its diff:
```python
import functools
import math

import jax
import jax.numpy as jnp
import ml_dtypes
import numpy as np
from jax import lax
from jax.experimental import pallas as pl
from jax.experimental.pallas import tpu as pltpu
from jax.sharding import PartitionSpec as P

BF = jnp.bfloat16
F32 = jnp.float32
VMEM_LIMIT = 20 * 1024 * 1024


def split_table(table, axis):
    high = table.astype(np.float32).astype(ml_dtypes.bfloat16)
    low = (table - high.astype(np.float64)).astype(np.float32).astype(ml_dtypes.bfloat16)
    return np.concatenate([high, low], axis=axis)


def transform_tables(blocks, width):
    period = 2 * blocks * width
    half = np.arange(blocks) + 0.5
    outer = 2.0 * np.pi * np.outer(half, np.arange(blocks)) / (2 * blocks)
    inner = 2.0 * np.pi * np.outer(np.arange(width), np.arange(width)) / width
    turn = 2.0 * np.pi * np.outer(half, np.arange(width)) / period
    cos_in, sin_in = np.cos(inner), np.sin(inner)
    outer_fwd = split_table(np.concatenate([np.cos(outer), -np.sin(outer)], 0), 1)
    inner_fwd = split_table(np.block([[cos_in, -sin_in], [sin_in, cos_in]]), 0)
    inner_inv = split_table(np.block([[cos_in, sin_in], [-sin_in, cos_in]]), 0)
    outer_inv = split_table(
        np.concatenate([np.cos(outer).T, -np.sin(outer).T], 1) * (2.0 / period), 1
    )
    turns = np.stack([np.cos(turn), np.sin(turn)]).astype(np.float32)
    return outer_fwd, inner_fwd, inner_inv, outer_inv, turns


def mm(left, right):
    return jnp.dot(left, right, preferred_element_type=F32)


def mm_t(left, right):
    return lax.dot_general(left, right, (((1,), (1,)), ((), ())), preferred_element_type=F32)


def to_spectrum(signals, outer, inner, turns):
    count = len(signals)
    size = signals[0].shape[0]
    width = signals[0].shape[1]
    data = jnp.concatenate([signal.astype(BF) for signal in signals], axis=1)
    mixed = mm(outer[...], jnp.concatenate([data, data], axis=0))
    turn_cos, turn_sin = turns[0], turns[1]
    rows = []
    for c in range(count):
        real = mixed[:size, c * width : (c + 1) * width]
        imag = mixed[size:, c * width : (c + 1) * width]
        rows.append(
            jnp.concatenate(
                [real * turn_cos + imag * turn_sin, imag * turn_cos - real * turn_sin], axis=1
            ).astype(BF)
        )
    turned = jnp.concatenate(rows, axis=0)
    return mm(jnp.concatenate([turned, turned], axis=1), inner[...])


def conj_times(left, right):
    width = left.shape[1] // 2
    left_real, left_imag = left[:, :width], left[:, width:]
    right_real, right_imag = right[:, :width], right[:, width:]
    return jnp.concatenate(
        [
            left_real * right_real + left_imag * right_imag,
            left_real * right_imag - left_imag * right_real,
        ],
        axis=1,
    )


def from_spectrum(product, inner, outer, turns):
    width = product.shape[1] // 2
    size = turns.shape[1]
    count = product.shape[0] // size
    data = product.astype(BF)
    mixed = mm(jnp.concatenate([data, data], axis=1), inner[...])
    turn_cos, turn_sin = turns[0], turns[1]
    reals, imags = [], []
    for c in range(count):
        real = mixed[c * size : (c + 1) * size, :width]
        imag = mixed[c * size : (c + 1) * size, width:]
        reals.append((real * turn_cos - imag * turn_sin).astype(BF))
        imags.append((imag * turn_cos + real * turn_sin).astype(BF))
    turned = jnp.concatenate(
        [jnp.concatenate(reals, axis=1), jnp.concatenate(imags, axis=1)], axis=0
    )
    result = mm(outer[...], jnp.concatenate([turned, turned], axis=0))
    return [result[:, c * width : (c + 1) * width] for c in range(count)]


def put_rows(scratch, value, first, stride):
    size = value.shape[0]
    for k in range(value.shape[1] // size):
        block = value[:, k * size : (k + 1) * size].astype(F32).T
        scratch[pl.ds(first + k, size, stride=stride), :] = block


def get_rows(scratch, first, stride, count):
    size = scratch.shape[1]
    return jnp.concatenate(
        [scratch[pl.ds(first + k, size, stride=stride), :].T for k in range(count)], axis=1
    )


def fetch(pairs, sems):
    copies = [
        pltpu.make_async_copy(source, target, sems.at[i])
        for i, (source, target) in enumerate(pairs)
    ]
    for copy in copies:
        copy.start()
    return copies


def prepare_body(
    rows_in,
    conv_in,
    filt_in,
    w_in_in,
    w_out_in,
    inc_in,
    packed_out,
    later_out,
    gate_two_out,
    part_two_out,
    rows,
    conv,
    filt,
    w_in,
    w_out,
    inc,
    first,
    second,
    packed,
    later,
    gate_two_kept,
    part_two_kept,
    sems,
    out_sems,
):
    channels = rows.shape[1]
    per = channels // rows.shape[0]
    got_filt, got_rows, got_w_in, got_inc, got_w_out, got_conv = fetch(
        [
            (filt_in, filt),
            (rows_in, rows),
            (w_in_in, w_in),
            (inc_in, inc),
            (w_out_in, w_out),
            (conv_in, conv),
        ],
        sems,
    )
    got_filt.wait()
    put_rows(first, filt[0], 0, 4 * per)
    put_rows(first, filt[1], per, 4 * per)
    got_rows.wait()
    got_w_in.wait()
    projected = mm(rows[...], w_in[...]).astype(BF)
    gate_one = projected[:, channels : 2 * channels]
    gate_two = projected[:, 2 * channels :]
    put_rows(first, gate_one, 2 * per, 4 * per)
    got_inc.wait()
    got_w_out.wait()
    mix_two = mm_t(inc[...], w_out[...])
    put_rows(first, mix_two * gate_two.astype(F32), 3 * per, 4 * per)
    packed[...] = first[...].astype(BF)
    sends = [pltpu.make_async_copy(packed, packed_out, out_sems.at[0])]
    sends[0].start()
    gate_two_kept[...] = gate_two
    got_conv.wait()
    part_two_kept[...] = (mix_two * conv[1].astype(F32)).astype(BF)
    put_rows(second, projected[:, :channels], 0, 2 * per)
    put_rows(second, gate_one.astype(F32) * conv[0].astype(F32), per, 2 * per)
    later[...] = second[...].astype(BF)
    for i, (source, target) in enumerate(
        [(gate_two_kept, gate_two_out), (part_two_kept, part_two_out), (later, later_out)]
    ):
        send = pltpu.make_async_copy(source, target, out_sems.at[1 + i])
        send.start()
        sends.append(send)
    for send in sends:
        send.wait()


def regrad_body(
    late,
    inc,
    done,
    w_out,
    gate_two_in,
    conv,
    later,
    packed,
    part_two_out,
    kept_out,
    part_two,
    gate_two,
    scratch,
    sems,
):
    per = inc.shape[1] // inc.shape[0]

    @pl.when(late[0] == 0)
    def _():
        gate, keep = fetch([(gate_two_in, gate_two), (inc, kept_out)], sems)
        mix_two = mm_t(inc[...], w_out[...])
        part_two[...] = (mix_two * conv[1].astype(F32)).astype(BF)
        part = pltpu.make_async_copy(part_two, part_two_out, sems.at[2])
        part.start()
        gate.wait()
        put_rows(scratch, mix_two * gate_two[...].astype(F32), 0, 2 * per)
        for k in range(per):
            empty = jnp.zeros((inc.shape[0], inc.shape[0]), F32)
            scratch[pl.ds(per + k, inc.shape[0], stride=2 * per), :] = empty
        packed[...] = scratch[...].astype(BF)
        keep.wait()
        part.wait()

    @pl.when(late[0] == 1)
    def _():
        part_two[...] = jnp.zeros_like(part_two)
        copies = fetch([(done, kept_out), (part_two, part_two_out), (later, packed)], sems)
        for copy in copies:
            copy.wait()


def signals(scratch, s, per):
    size = scratch.shape[1]
    stride = scratch.shape[0] // size
    return [scratch[pl.ds(s * per + k, size, stride=stride), :] for k in range(per)]


def send_rows(scratch, s, values):
    size = scratch.shape[1]
    stride = scratch.shape[0] // size
    for k, value in enumerate(values):
        scratch[pl.ds(s * len(values) + k, size, stride=stride), :] = value


def early_body(
    per,
    late,
    gains,
    data,
    later,
    outer_fwd,
    inner_fwd,
    inner_inv,
    outer_inv,
    turns,
    packed,
    spec_out,
    grad_out,
    known,
    out,
    spec,
    grad,
    sems,
):
    size = data.shape[1]

    @pl.when(late[0] == 1)
    def _():
        known[...] = data[...].astype(F32)
        filt_two = to_spectrum(signals(known, 1, per), outer_fwd, inner_fwd, turns)
        grad_two = signals(known, 3, per)
        spec_two = to_spectrum(grad_two, outer_fwd, inner_fwd, turns)
        spec[1] = spec_two
        mixed = from_spectrum(conj_times(filt_two, spec_two), inner_inv, outer_inv, turns)
        mix_one = [mixed[k] + gains[1, k] * grad_two[k] for k in range(per)]
        send_rows(out, 1, mix_one)
        gate_one = signals(known, 2, per)
        grad_one = [mix_one[k] * gate_one[k] for k in range(per)]
        for k in range(per):
            grad[pl.ds(k * size, size), :] = grad_one[k]
        filt_one = to_spectrum(signals(known, 0, per), outer_fwd, inner_fwd, turns)
        spec_one = to_spectrum(grad_one, outer_fwd, inner_fwd, turns)
        spec[0] = spec_one
        copies = fetch([(spec, spec_out), (grad, grad_out)], sems)
        mixed = from_spectrum(conj_times(filt_one, spec_one), inner_inv, outer_inv, turns)
        send_rows(out, 0, [mixed[k] + gains[0, k] * grad_one[k] for k in range(per)])
        packed[...] = out[...].astype(BF)
        for copy in copies:
            copy.wait()

    @pl.when(late[0] == 0)
    def _():
        known[...] = data[...].astype(F32)
        grad[...] = jnp.zeros_like(grad)
        spec[0] = to_spectrum(signals(known, 0, per), outer_fwd, inner_fwd, turns)
        spec[1] = to_spectrum(signals(known, 1, per), outer_fwd, inner_fwd, turns)
        copies = fetch([(spec, spec_out), (grad, grad_out), (later, packed)], sems)
        for copy in copies:
            copy.wait()


def known_body(per, data, outer_fwd, inner_fwd, turns, spec_out, known):
    known[...] = data[...].astype(F32)
    spec_out[0] = to_spectrum(signals(known, 0, per), outer_fwd, inner_fwd, turns)
    spec_out[1] = to_spectrum(signals(known, 1, per), outer_fwd, inner_fwd, turns)


def skip_rows(per, grads, others, out):
    size = out.shape[1]
    rows = out.shape[0] // size
    lane = lax.broadcasted_iota(jnp.int32, (1, size), 1)
    skip_row = jnp.zeros((1, size), F32)
    for w in range(2):
        for k in range(per):
            term = grads[w][k] * others[w][k]
            total = jnp.sum(jnp.sum(term, axis=0, keepdims=True), axis=1, keepdims=True)
            high = total.astype(BF).astype(F32)
            skip_row = jnp.where(lane == w * per + k, high, skip_row)
            skip_row = jnp.where(lane == (2 + w) * per + k, total - high, skip_row)
    out[pl.ds(4 * per, size, stride=rows), :] = jnp.broadcast_to(skip_row, (size, size))
    for r in range(4 * per + 1, rows):
        out[pl.ds(r, size, stride=rows), :] = jnp.zeros((size, size), F32)


def late_body(
    per,
    late,
    gains,
    first,
    second,
    third,
    held_in,
    grad_in,
    spec,
    outer_fwd_in,
    inner_fwd_in,
    inner_inv_in,
    outer_inv_in,
    turns_in,
    packed,
    known,
    other,
    fresh,
    out,
    held,
    grad_held,
    outer_fwd,
    inner_fwd,
    inner_inv,
    outer_inv,
    turns,
    sems,
):
    size = first.shape[1]
    copies = fetch(
        [
            (outer_fwd_in, outer_fwd),
            (turns_in, turns),
            (inner_fwd_in, inner_fwd),
            (held_in, held),
            (inner_inv_in, inner_inv),
            (outer_inv_in, outer_inv),
            (grad_in, grad_held),
        ],
        sems,
    )
    fresh[...] = third[...].astype(F32)
    known[...] = first[...].astype(F32)
    for copy in copies:
        copy.wait()

    @pl.when(late[0] == 0)
    def _():
        other[...] = second[...].astype(F32)
        grad_two = signals(fresh, 0, per)
        spec_two = to_spectrum(grad_two, outer_fwd, inner_fwd, turns)
        mixed = from_spectrum(conj_times(held[1], spec_two), inner_inv, outer_inv, turns)
        send_rows(out, 3, from_spectrum(conj_times(spec[1], spec_two), inner_inv, outer_inv, turns))
        mix_one = [mixed[k] + gains[1, k] * grad_two[k] for k in range(per)]
        send_rows(out, 1, mix_one)
        gate_one = signals(known, 2, per)
        grad_one = [mix_one[k] * gate_one[k] for k in range(per)]
        spec_one = to_spectrum(grad_one, outer_fwd, inner_fwd, turns)
        mixed = from_spectrum(conj_times(held[0], spec_one), inner_inv, outer_inv, turns)
        send_rows(out, 2, from_spectrum(conj_times(spec[0], spec_one), inner_inv, outer_inv, turns))
        send_rows(out, 0, [mixed[k] + gains[0, k] * grad_one[k] for k in range(per)])
        skip_rows(
            per, (grad_one, grad_two), (signals(other, 0, per), signals(other, 1, per)), out
        )
        packed[...] = out[...].astype(BF)

    @pl.when(late[0] == 1)
    def _():
        values, gated = signals(fresh, 0, per), signals(fresh, 1, per)
        spec_one = to_spectrum(values, outer_fwd, inner_fwd, turns)
        spec_two = to_spectrum(gated, outer_fwd, inner_fwd, turns)
        send_rows(out, 2, from_spectrum(conj_times(spec_one, held[0]), inner_inv, outer_inv, turns))
        send_rows(out, 3, from_spectrum(conj_times(spec_two, held[1]), inner_inv, outer_inv, turns))
        empty = [jnp.zeros((size, size), F32)] * per
        send_rows(out, 0, empty)
        send_rows(out, 1, empty)
        grad_one = [grad_held[pl.ds(k * size, size), :] for k in range(per)]
        skip_rows(per, (grad_one, signals(known, 3, per)), (values, gated), out)
        packed[...] = out[...].astype(BF)


def input_grad(inc, values, mix_one, conv_one, part_two, w_in):
    gate_one = mix_one * conv_one.astype(F32)
    proj = jnp.concatenate([values.astype(BF), gate_one.astype(BF), part_two], axis=1)
    return (inc.astype(F32) + mm_t(proj, w_in)).astype(BF)


def hand_body(
    per, late, data, conv, part_two_in, inc_in, w_in, result, scratch, part_two, inc, sems
):
    @pl.when(late[0] == 1)
    def _():
        copies = fetch([(part_two_in, part_two), (inc_in, inc)], sems)
        scratch[...] = data[...].astype(F32)
        values = get_rows(scratch, 0, 2 * per, per)
        mix_one = get_rows(scratch, per, 2 * per, per)
        for copy in copies:
            copy.wait()
        result[...] = input_grad(inc[...], values, mix_one, conv[0], part_two[...], w_in[...])

    @pl.when(late[0] == 0)
    def _():
        result[...] = jnp.zeros_like(result)


def finish_body(
    per,
    rescale,
    late,
    data,
    conv,
    part_two,
    inc,
    w_in,
    result,
    filt_grads,
    skip_grads,
    scratch,
):
    size = data.shape[1]
    stride = data.shape[0] // size
    scratch[...] = data[...].astype(F32)

    @pl.when(late[0] == 0)
    def _():
        values = get_rows(scratch, 0, stride, per)
        mix_one = get_rows(scratch, per, stride, per)
        result[...] = input_grad(inc[...], values, mix_one, conv[0], part_two[...], w_in[...])

    @pl.when(late[0] == 1)
    def _():
        result[...] = inc[...]

    filt_grads[0] = (get_rows(scratch, 2 * per, stride, per) * rescale).astype(BF)
    filt_grads[1] = (get_rows(scratch, 3 * per, stride, per) * rescale).astype(BF)
    sums = scratch[pl.ds(4 * per, size, stride=stride), :].T
    sums = (sums[: 2 * per] + sums[2 * per : 4 * per]) * rescale
    for w in range(2):
        for k in range(per):
            row = w * per + k
            skip_grads[pl.ds(w, 1), pl.ds(k * size, size)] = sums[row : row + 1]


def call(body, out_shapes, scratch, *operands, smem=0, direct=(), direct_out=(), limit=VMEM_LIMIT):
    def space(i):
        if i < smem:
            return pltpu.SMEM
        return pltpu.HBM if i in direct else pltpu.VMEM

    return pl.pallas_call(
        body,
        out_shape=[
            (pltpu.HBM if i in direct_out else jax.ShapeDtypeStruct)(shape, dtype)
            for i, (shape, dtype) in enumerate(out_shapes)
        ],
        in_specs=[pl.BlockSpec(memory_space=space(i)) for i in range(len(operands))],
        out_specs=[
            pl.BlockSpec(memory_space=pltpu.HBM if i in direct_out else pltpu.VMEM)
            for i in range(len(out_shapes))
        ],
        scratch_shapes=[
            pltpu.VMEM(shape, F32) if isinstance(shape, tuple) else shape for shape in scratch
        ],
        compiler_params=pltpu.CompilerParams(vmem_limit_bytes=limit),
    )(
        *[
            pltpu.with_memory_space_constraint(x, pltpu.HBM) if i in direct else x
            for i, x in enumerate(operands)
        ]
    )


def exchange(rows, parts):
    per_part = rows.shape[0] // parts
    tile = math.gcd(per_part, 8)
    cut = rows.reshape(parts, per_part // tile, tile, rows.shape[1])
    return lax.all_to_all(cut, "seq", split_axis=0, concat_axis=0, tiled=True).reshape(rows.shape)


def on_device(layer_input, conv_out, filters, skip_gain, weight_in, weight_out, grad_output):
    tokens, channels = grad_output.shape
    parts = lax.axis_size("seq")
    per = channels // parts
    w_in, w_out, conv = weight_in[0], weight_out[0], conv_out[0]
    outer_fwd, inner_fwd, inner_inv, outer_inv, turns = transform_tables(parts, tokens)
    late = lax.axis_index("section").astype(jnp.int32).reshape(1)
    own = lax.dynamic_slice_in_dim(
        skip_gain[0].reshape(2, per, parts), lax.axis_index("seq"), 1, axis=2
    )[:, :, 0]

    def rows(count):
        return (parts * count, tokens)

    token_rows = ((tokens, channels), BF)
    spectra = ((2, per * parts, 2 * tokens), F32)

    packed, later, gate_two, part_two = call(
        prepare_body,
        [(rows(4 * per), BF), (rows(2 * per), BF), token_rows, token_rows],
        [
            pltpu.VMEM((tokens, channels), BF),
            pltpu.VMEM((2, tokens, channels), BF),
            pltpu.VMEM((2, tokens, channels), BF),
            pltpu.VMEM(w_in.shape, BF),
            pltpu.VMEM(w_out.shape, BF),
            pltpu.VMEM((tokens, channels), BF),
            rows(4 * per),
            rows(2 * per),
            pltpu.VMEM(rows(4 * per), BF),
            pltpu.VMEM(rows(2 * per), BF),
            pltpu.VMEM((tokens, channels), BF),
            pltpu.VMEM((tokens, channels), BF),
            pltpu.SemaphoreType.DMA((6,)),
            pltpu.SemaphoreType.DMA((4,)),
        ],
        layer_input[0], conv, filters[0], w_in, w_out, grad_output,
        direct=range(6), direct_out=range(4),
    )
    first = exchange(packed, parts)
    packed, held, grad_held = call(
        functools.partial(early_body, per),
        [(rows(2 * per), BF), spectra, (rows(per), F32)],
        [
            rows(4 * per), rows(2 * per), spectra[0], rows(per), pltpu.SemaphoreType.DMA((3,)),
        ],
        late, own, first, later, outer_fwd, inner_fwd, inner_inv, outer_inv, turns,
        smem=2, direct=(3,), direct_out=(1, 2),
    )
    second = exchange(packed, parts)
    (done,) = call(
        functools.partial(hand_body, per),
        [token_rows],
        [
            rows(2 * per), pltpu.VMEM((tokens, channels), BF), pltpu.VMEM((tokens, channels), BF),
            pltpu.SemaphoreType.DMA((2,)),
        ],
        late, second, conv, part_two, grad_output, w_in,
        smem=1, direct=(3, 4),
    )
    handed = lax.ppermute(done, "section", [(1, 0)])
    packed, part_two, kept = call(
        regrad_body,
        [(rows(2 * per), BF), token_rows, token_rows],
        [
            pltpu.VMEM((tokens, channels), BF), pltpu.VMEM((tokens, channels), BF), rows(2 * per),
            pltpu.SemaphoreType.DMA((3,)),
        ],
        late, handed, done, w_out, gate_two, conv, later,
        smem=1, direct=(4, 6), direct_out=(1, 2),
    )
    third = exchange(packed, parts)
    (spec,) = call(
        functools.partial(known_body, per),
        [spectra],
        [rows(2 * per)],
        second, outer_fwd, inner_fwd, turns,
    )
    out_rows = 4 * per + 2
    (packed,) = call(
        functools.partial(late_body, per),
        [(rows(out_rows), BF)],
        [
            rows(4 * per), rows(2 * per), rows(2 * per), rows(out_rows), spectra[0], rows(per),
            pltpu.VMEM(outer_fwd.shape, BF), pltpu.VMEM(inner_fwd.shape, BF),
            pltpu.VMEM(inner_inv.shape, BF), pltpu.VMEM(outer_inv.shape, BF),
            turns.shape, pltpu.SemaphoreType.DMA((7,)),
        ],
        late, own, first, second, third, held, grad_held, spec,
        outer_fwd, inner_fwd, inner_inv, outer_inv, turns,
        smem=2, direct=(5, 6, 8, 9, 10, 11, 12),
    )
    back = exchange(packed, parts)
    grad_rows, filter_grads, skip_grads = call(
        functools.partial(finish_body, per, 1.0 / math.sqrt(parts * tokens)),
        [token_rows, ((2, tokens, channels), BF), ((2, channels), F32)],
        [rows(out_rows)],
        late, back, conv, part_two, kept, w_in,
        smem=1,
    )
    return (grad_rows[None], filter_grads[None], skip_grads[None])


def solution(mesh):
    in_specs = (
        P("section", "seq", None),
        P("section", None, "seq", None),
        P("section", None, "seq", None),
        P("section", None, None),
        P("section", None, None),
        P("section", None, None),
        P("seq", None),
    )
    out_specs = (
        P("section", "seq", None),
        P("section", None, "seq", None),
        P("section", None, None),
    )
    return jax.shard_map(
        on_device, mesh=mesh, in_specs=in_specs, out_specs=out_specs, check_vma=False
    )
```

time: 144 us -> 124 us (0.86)
  waiting for transfers between devices: 50 us -> 34 us
  local copies, waits for them, and re-layouts: 18 us -> 2.11 us
  blocking collectives: 30.7 us -> 46 us
  starting transfers between devices: 31.4 us -> 24.5 us
  Pallas kernels: 11.5 us -> 16 us
    all_to_all x3 -> x2, waiting for transfers between devices: 48.1 us -> 32 us  [exchange(): lax.all_to_all(cut, 'seq', split_axis=0, concat_axis=0, tiled=True)]
    unnamed x65 -> x29, local copies, waits for them, and re-layouts: 17.9 us -> 2.02 us
    all_to_all x1 -> x2, blocking collectives: 30.7 us -> 46 us  [exchange(): lax.all_to_all(cut, 'seq', split_axis=0, concat_axis=0, tiled=True)]
    all_to_all x3 -> x2, starting transfers between devices: 30.1 us -> 23.2 us  [exchange(): lax.all_to_all(cut, 'seq', split_axis=0, concat_axis=0, tiled=True)]
    pallas_call x7, Pallas kernels: 11.5 us -> 16 us  [call(): pl.pallas_call(body, out_shape=[(pltpu.HBM if i in direct_out else jax.Sh...]
  transfers between devices with their start and end apart: 4 -> 3, of which waited for: 4 -> 3; matrix products, arithmetic and copies ran while one was open for 0% -> 0% of each run, Pallas kernels for 1% -> 1%
where the time goes in v2:
time: 124 us; the launch traced here: 123 us
  blocking collectives  46 us (37%)
  waiting for transfers between devices  34 us (27%)
  starting transfers between devices  24.5 us (20%)
  Pallas kernels  16 us (13%)
  local copies, waits for them, and re-layouts  2.11 us (2%)
    all_to_all x2, blocking collectives, exchange(): lax.all_to_all(cut, 'seq', split_axis=0, concat_axis=0, tiled=True)  46 us
    all_to_all x2, waiting for transfers between devices, exchange(): lax.all_to_all(cut, 'seq', split_axis=0, concat_axis=0, tiled=True)  32 us
    all_to_all x2, starting transfers between devices, exchange(): lax.all_to_all(cut, 'seq', split_axis=0, concat_axis=0, tiled=True)  23.2 us
    pallas_call x7, Pallas kernels, call(): pl.pallas_call(body, out_shape=[(pltpu.HBM if i in direct_out else jax.Sh...  16 us
  transfers between devices with their start and end apart: 3, of which 3 were waited for; matrix products, arithmetic and copies ran while one was open for 0% of the time, Pallas kernels for 1%

profile of v2, /device:TPU:8, one launch (start us, length us, event | category | flops | bytes accessed | tf_op | source)
XLA Modules:
  0.0 123.4 jit_solution(13998526144948204971)
XLA Ops:
  0.6 0.0 copy-start.3
  0.7 0.0 copy-start.6
  0.7 0.0 copy-start.7
  0.7 0.0 copy-start.9
  0.7 0.0 copy-start.10
  0.7 3.6 %shard_map.139 = (bf16[2048,128]{1,0:T(8,128)(2,1)}, bf16[1024,128]{1,0:T(8,128)(2,1)}, bf16[128,512]{1,0:T(8,128)(2,1)}, bf16[128,512]{1,0:T(8,128)(2,1)}) custom-call(bf16[128,512]{1,0:T(8,128)(2,1)} %bitcast.43, bf16[2,128,512]{2,1,0:T(8,128)(2,1)} %bitcast.30, bf16[2,128,512]{2,1,0:T(8,128)(2,1)} %bitcast.42, bf16[512,1536]{1,0:T(8,128)(2,1)} %bitcast.22, ...), custom_call_target="tpu_custom_call" | custom-call | tf_op jit(solution)/shard_map/pallas_call | solution.py:482
  4.3 0.0 copy-start
  4.3 0.0 copy-start.1
  4.3 15.5 %all-to-all-start = ((bf16[128,2,8,128]{3,2,1,0:T(8,128)(2,1)}), bf16[128,2,8,128]{3,2,1,0:T(8,128)(2,1)S(1)}, u32[]{:S(2)}, u32[]{:S(2)}) async-start(bf16[128,2,8,128]{3,2,1,0:T(8,128)(2,1)} %bitcast.41), calls=%async_computation | async-start | bytes 1048576 | tf_op jit(solution)/shard_map/all_to_all | solution.py:509
  19.8 0.0 copy-done.13
  19.8 0.1 constant_dynamic-slice_fusion
  19.9 0.1 copy.19
  20.0 19.9 %all-to-all-done = bf16[128,2,8,128]{3,2,1,0:T(8,128)(2,1)S(1)} async-done(((bf16[128,2,8,128]{3,2,1,0:T(8,128)(2,1)}), bf16[128,2,8,128]{3,2,1,0:T(8,128)(2,1)S(1)}, u32[]{:S(2)}, u32[]{:S(2)}) %all-to-all-start) | async-done | bytes 524320 | tf_op jit(solution)/shard_map/all_to_all | solution.py:509
  39.9 0.0 copy-done.6
  39.9 2.5 %shard_map.140 = (bf16[1024,128]{1,0:T(8,128)(2,1)S(1)}, f32[2,512,256]{2,1,0:T(8,128)}, f32[512,128]{1,0:T(8,128)}) custom-call(s32[1]{0:T(128)} %bitcast.late, f32[2,4]{1,0:T(2,128)S(1)} %bitcast.39, bf16[2048,128]{1,0:T(8,128)(2,1)S(1)} %bitcast.25, bf16[1024,128]{1,0:T(8,128)(2,1)} %get-tuple-element.17.later, bf16[256,256]{1,0:T(8,128)(2,1)S(1)} %copy-done.7, ...), custom_call_target="tpu_custom_call" | custom-call | tf_op jit(solution)/shard_map/pallas_call | solution.py:482
  42.5 0.0 copy-start.5
  42.5 20.8 %all_to_all.20 = bf16[128,1,8,128]{3,2,1,0:T(8,128)(2,1)S(1)} all-to-all(bf16[128,1,8,128]{3,2,1,0:T(8,128)(2,1)S(1)} %bitcast.38), channel_id=1, replica_groups=mesh['seq'=128,'section'=2] {'seq'}, dimensions={0} | all-to-all | bytes 524288 | tf_op jit(solution)/shard_map/all_to_all | solution.py:509
  63.3 0.0 copy-done.1
  63.4 1.3 %collective-permute-start = (bf16[128,512]{1,0:T(8,128)(2,1)S(1)}, bf16[128,512]{1,0:T(8,128)(2,1)S(1)}, u32[]{:S(2)}, u32[]{:S(2)}) collective-permute-start(bf16[128,512]{1,0:T(8,128)(2,1)S(1)} %shard_map.141.done), channel_id=1, source_target_pairs={{1,0},{3,2},{5,4},{7,6},{9,8},{11,10},{13,12},{15,14},{17,16},{19,... | collective-permute-start | bytes 393224 | tf_op jit(solution)/shard_map/ppermute | solution.py:572
  64.7 1.9 %collective-permute-done.inc = bf16[128,512]{1,0:T(8,128)(2,1)S(1)} collective-permute-done((bf16[128,512]{1,0:T(8,128)(2,1)S(1)}, bf16[128,512]{1,0:T(8,128)(2,1)S(1)}, u32[]{:S(2)}, u32[]{:S(2)}) %collective-permute-start) | collective-permute-done | bytes 131104 | tf_op jit(solution)/shard_map/ppermute | solution.py:572
  66.6 0.0 copy-done.5
  66.6 2.0 %shard_map.142 = (bf16[1024,128]{1,0:T(8,128)(2,1)}, bf16[128,512]{1,0:T(8,128)(2,1)}, bf16[128,512]{1,0:T(8,128)(2,1)}) custom-call(s32[1]{0:T(128)} %bitcast.late, bf16[128,512]{1,0:T(8,128)(2,1)S(1)} %collective-permute-done.inc, bf16[128,512]{1,0:T(8,128)(2,1)S(1)} %shard_map.141.done, bf16[512,512]{1,0:T(8,128)(2,1)S(1)} %bitcast.37, ...), custom_call_target="tpu_custom_call" | custom-call | tf_op jit(solution)/shard_map/pallas_call | solution.py:482
  68.6 7.7 %all-to-all-start.2 = ((bf16[128,1,8,128]{3,2,1,0:T(8,128)(2,1)}), bf16[128,1,8,128]{3,2,1,0:T(8,128)(2,1)}, u32[]{:S(2)}, u32[]{:S(2)}) async-start(bf16[128,1,8,128]{3,2,1,0:T(8,128)(2,1)} %bitcast.13), calls=%async_computation.2 | async-start | bytes 524288 | tf_op jit(solution)/shard_map/all_to_all | solution.py:509
  76.3 0.0 copy-start.4
  76.3 0.9 copy-done.4
  77.2 0.9 copy-done.8
  78.1 0.7 shard_map.143.spec
  78.8 12.2 %all-to-all-done.2 = bf16[128,1,8,128]{3,2,1,0:T(8,128)(2,1)} async-done(((bf16[128,1,8,128]{3,2,1,0:T(8,128)(2,1)}), bf16[128,1,8,128]{3,2,1,0:T(8,128)(2,1)}, u32[]{:S(2)}, u32[]{:S(2)}) %all-to-all-start.2) | async-done | bytes 262176 | tf_op jit(solution)/shard_map/all_to_all | solution.py:509
  91.0 5.6 %shard_map.144 = bf16[2304,128]{1,0:T(8,128)(2,1)S(1)} custom-call(s32[1]{0:T(128)} %bitcast.late, f32[2,4]{1,0:T(2,128)S(1)} %bitcast.40, bf16[2048,128]{1,0:T(8,128)(2,1)S(1)} %bitcast.26, bf16[1024,128]{1,0:T(8,128)(2,1)S(1)} %bitcast.29, bf16[1024,128]{1,0:T(8,128)(2,1)} %bitcast.14.third, f32[2,512,256]{2,1,0:T(8,128)} %get-tuple-element.22.held_in, ...), custom_call_target="tpu_custom_call" | custom-call | tf_op jit(solution)/shard_map/pallas_call | solution.py:482
  96.6 25.2 %all_to_all.21 = bf16[128,9,2,128]{3,2,1,0:T(2,128)(2,1)S(1)} all-to-all(bf16[128,9,2,128]{3,2,1,0:T(2,128)(2,1)S(1)} %bitcast.34), channel_id=1, replica_groups=mesh['seq'=128,'section'=2] {'seq'}, dimensions={0} | all-to-all | bytes 1179648 | tf_op jit(solution)/shard_map/all_to_all | solution.py:509
  121.8 0.0 copy-done.11
  121.8 1.6 %shard_map.145 = (bf16[128,512]{1,0:T(8,128)(2,1)}, bf16[2,128,512]{2,1,0:T(8,128)(2,1)}, f32[2,512]{1,0:T(2,128)}) custom-call(s32[1]{0:T(128)} %bitcast.late, bf16[2304,128]{1,0:T(8,128)(2,1)S(1)} %bitcast.35, bf16[2,128,512]{2,1,0:T(8,128)(2,1)S(1)} %bitcast.33, bf16[128,512]{1,0:T(8,128)(2,1)S(1)} %copy-done.11, bf16[128,512]{1,0:T(8,128)(2,1)S(1)} %copy-done.12, ...), custom_call_target="tpu_custom_call" | custom-call | tf_op jit(solution)/shard_map/pallas_call | solution.py:482
  (14 shorter events, 0.1 us)
Async XLA Ops:
  0.6 19.2 %copy-start.13 = (f32[1,2,512]{2,1,0:T(2,128)S(1)}, f32[1,2,512]{2,1,0:T(2,128)}, u32[]{:S(2)}) copy-start(f32[1,2,512]{2,1,0:T(2,128)} %param.15) | copy-start | bytes 12292
  0.6 39.3 %copy-start.3 = (bf16[512,256]{1,0:T(8,128)(2,1)S(1)}, bf16[512,256]{1,0:T(8,128)(2,1)}, u32[]{:S(2)}) copy-start(bf16[512,256]{1,0:T(8,128)(2,1)} %constant.23.clone.inner_fwd.inner_fwd_in) | copy-start | bytes 786436
  0.7 39.2 %copy-start.6 = (f32[2,128,128]{2,1,0:T(8,128)S(1)}, f32[2,128,128]{2,1,0:T(8,128)}, u32[]{:S(2)}) copy-start(f32[2,128,128]{2,1,0:T(8,128)} %constant.26.clone.turns.turns_in) | copy-start | bytes 393220
  0.7 39.2 %copy-start.7 = (bf16[256,256]{1,0:T(8,128)(2,1)S(1)}, bf16[256,256]{1,0:T(8,128)(2,1)}, u32[]{:S(2)}) copy-start(bf16[256,256]{1,0:T(8,128)(2,1)} %constant.22.clone.outer_fwd.outer_fwd_in) | copy-start | bytes 393220
  0.7 39.2 %copy-start.9 = (bf16[512,256]{1,0:T(8,128)(2,1)S(1)}, bf16[512,256]{1,0:T(8,128)(2,1)}, u32[]{:S(2)}) copy-start(bf16[512,256]{1,0:T(8,128)(2,1)} %constant.24.clone.inner_inv.inner_inv_in) | copy-start | bytes 786436
  0.7 39.2 %copy-start.10 = (bf16[128,512]{1,0:T(8,128)(2,1)S(1)}, bf16[128,512]{1,0:T(8,128)(2,1)}, u32[]{:S(2)}) copy-start(bf16[128,512]{1,0:T(8,128)(2,1)} %constant.25.clone.outer_inv.outer_inv_in) | copy-start | bytes 393220
  4.3 59.0 %copy-start = (bf16[1,512,1536]{2,1,0:T(8,128)(2,1)S(1)}, bf16[1,512,1536]{2,1,0:T(8,128)(2,1)}, u32[]{:S(2)}) copy-start(bf16[1,512,1536]{2,1,0:T(8,128)(2,1)} %param.16) | copy-start | bytes 4718596
  4.3 59.0 %copy-start.1 = (bf16[1,2,128,512]{3,2,1,0:T(8,128)(2,1)S(1)}, bf16[1,2,128,512]{3,2,1,0:T(8,128)(2,1)}, u32[]{:S(2)}) copy-start(bf16[1,2,128,512]{3,2,1,0:T(8,128)(2,1)} %param.13) | copy-start | bytes 786436
  4.3 35.6 %all-to-all-start = ((bf16[128,2,8,128]{3,2,1,0:T(8,128)(2,1)}), bf16[128,2,8,128]{3,2,1,0:T(8,128)(2,1)S(1)}, u32[]{:S(2)}, u32[]{:S(2)}) async-start(bf16[128,2,8,128]{3,2,1,0:T(8,128)(2,1)} %bitcast.41), calls=%async_computation | async-start | bytes 1048576 | tf_op jit(solution)/shard_map/all_to_all | solution.py:509
  42.5 24.1 %copy-start.5 = (bf16[1,512,512]{2,1,0:T(8,128)(2,1)S(1)}, bf16[1,512,512]{2,1,0:T(8,128)(2,1)}, u32[]{:S(2)}) copy-start(bf16[1,512,512]{2,1,0:T(8,128)(2,1)} %param.17) | copy-start | bytes 1572868
  63.4 3.2 %collective-permute-start = (bf16[128,512]{1,0:T(8,128)(2,1)S(1)}, bf16[128,512]{1,0:T(8,128)(2,1)S(1)}, u32[]{:S(2)}, u32[]{:S(2)}) collective-permute-start(bf16[128,512]{1,0:T(8,128)(2,1)S(1)} %shard_map.141.done), channel_id=1, source_target_pairs={{1,0},{3,2},{5,4},{7,6},{9,8},{11,10},{13,12},{15,14},{17,16},{19,... | collective-permute-start | bytes 393224 | tf_op jit(solution)/shard_map/ppermute | solution.py:572
  68.6 22.4 %all-to-all-start.2 = ((bf16[128,1,8,128]{3,2,1,0:T(8,128)(2,1)}), bf16[128,1,8,128]{3,2,1,0:T(8,128)(2,1)}, u32[]{:S(2)}, u32[]{:S(2)}) async-start(bf16[128,1,8,128]{3,2,1,0:T(8,128)(2,1)} %bitcast.13), calls=%async_computation.2 | async-start | bytes 524288 | tf_op jit(solution)/shard_map/all_to_all | solution.py:509
  76.3 1.0 copy-start.4
  77.2 0.9 copy-start.8
  91.0 30.8 %copy-start.2 = (bf16[1,2,128,512]{3,2,1,0:T(8,128)(2,1)S(1)}, bf16[1,2,128,512]{3,2,1,0:T(8,128)(2,1)}, u32[]{:S(2)}) copy-start(bf16[1,2,128,512]{3,2,1,0:T(8,128)(2,1)} %param.13) | copy-start | bytes 786436
  91.0 30.8 %copy-start.11 = (bf16[128,512]{1,0:T(8,128)(2,1)S(1)}, bf16[128,512]{1,0:T(8,128)(2,1)}, u32[]{:S(2)}) copy-start(bf16[128,512]{1,0:T(8,128)(2,1)} %get-tuple-element.24.part_two) | copy-start | bytes 393220
  91.0 30.8 %copy-start.12 = (bf16[128,512]{1,0:T(8,128)(2,1)S(1)}, bf16[128,512]{1,0:T(8,128)(2,1)}, u32[]{:S(2)}) copy-start(bf16[128,512]{1,0:T(8,128)(2,1)} %get-tuple-element.25.inc) | copy-start | bytes 393220

commit v3 on v2

v3 whole, which is shorter than its diff:
```python
import functools
import math

import jax
import jax.numpy as jnp
import ml_dtypes
import numpy as np
from jax import lax
from jax.experimental import pallas as pl
from jax.experimental.pallas import tpu as pltpu
from jax.sharding import PartitionSpec as P

BF = jnp.bfloat16
F32 = jnp.float32
VMEM_LIMIT = 20 * 1024 * 1024


def split_table(table, axis):
    high = table.astype(np.float32).astype(ml_dtypes.bfloat16)
    low = (table - high.astype(np.float64)).astype(np.float32).astype(ml_dtypes.bfloat16)
    return np.concatenate([high, low], axis=axis)


def transform_tables(blocks, width):
    period = 2 * blocks * width
    half = np.arange(blocks) + 0.5
    outer = 2.0 * np.pi * np.outer(half, np.arange(blocks)) / (2 * blocks)
    inner = 2.0 * np.pi * np.outer(np.arange(width), np.arange(width)) / width
    turn = 2.0 * np.pi * np.outer(half, np.arange(width)) / period
    cos_in, sin_in = np.cos(inner), np.sin(inner)
    outer_fwd = split_table(np.concatenate([np.cos(outer), -np.sin(outer)], 0), 1)
    inner_fwd = split_table(np.block([[cos_in, -sin_in], [sin_in, cos_in]]), 0)
    inner_inv = split_table(np.block([[cos_in, sin_in], [-sin_in, cos_in]]), 0)
    outer_inv = split_table(
        np.concatenate([np.cos(outer).T, -np.sin(outer).T], 1) * (2.0 / period), 1
    )
    turns = np.stack([np.cos(turn), np.sin(turn)]).astype(np.float32)
    return outer_fwd, inner_fwd, inner_inv, outer_inv, turns


def mm(left, right):
    return jnp.dot(left, right, preferred_element_type=F32)


def mm_t(left, right):
    return lax.dot_general(left, right, (((1,), (1,)), ((), ())), preferred_element_type=F32)


def to_spectrum(signals, outer, inner, turns):
    count = len(signals)
    size = signals[0].shape[0]
    width = signals[0].shape[1]
    data = jnp.concatenate([signal.astype(BF) for signal in signals], axis=1)
    mixed = mm(outer[...], jnp.concatenate([data, data], axis=0))
    turn_cos, turn_sin = turns[0], turns[1]
    rows = []
    for c in range(count):
        real = mixed[:size, c * width : (c + 1) * width]
        imag = mixed[size:, c * width : (c + 1) * width]
        rows.append(
            jnp.concatenate(
                [real * turn_cos + imag * turn_sin, imag * turn_cos - real * turn_sin], axis=1
            ).astype(BF)
        )
    turned = jnp.concatenate(rows, axis=0)
    return mm(jnp.concatenate([turned, turned], axis=1), inner[...])


def conj_times(left, right):
    width = left.shape[1] // 2
    left_real, left_imag = left[:, :width], left[:, width:]
    right_real, right_imag = right[:, :width], right[:, width:]
    return jnp.concatenate(
        [
            left_real * right_real + left_imag * right_imag,
            left_real * right_imag - left_imag * right_real,
        ],
        axis=1,
    )


def from_spectrum(product, inner, outer, turns):
    width = product.shape[1] // 2
    size = turns.shape[1]
    count = product.shape[0] // size
    data = product.astype(BF)
    mixed = mm(jnp.concatenate([data, data], axis=1), inner[...])
    turn_cos, turn_sin = turns[0], turns[1]
    reals, imags = [], []
    for c in range(count):
        real = mixed[c * size : (c + 1) * size, :width]
        imag = mixed[c * size : (c + 1) * size, width:]
        reals.append((real * turn_cos - imag * turn_sin).astype(BF))
        imags.append((imag * turn_cos + real * turn_sin).astype(BF))
    turned = jnp.concatenate(
        [jnp.concatenate(reals, axis=1), jnp.concatenate(imags, axis=1)], axis=0
    )
    result = mm(outer[...], jnp.concatenate([turned, turned], axis=0))
    return [result[:, c * width : (c + 1) * width] for c in range(count)]


def put_rows(scratch, value, first, stride):
    size = value.shape[0]
    for k in range(value.shape[1] // size):
        block = value[:, k * size : (k + 1) * size].astype(F32).T
        scratch[pl.ds(first + k, size, stride=stride), :] = block


def get_rows(scratch, first, stride, count):
    size = scratch.shape[1]
    return jnp.concatenate(
        [scratch[pl.ds(first + k, size, stride=stride), :].T for k in range(count)], axis=1
    )


def fetch(pairs, sems):
    copies = [
        pltpu.make_async_copy(source, target, sems.at[i])
        for i, (source, target) in enumerate(pairs)
    ]
    for copy in copies:
        copy.start()
    return copies


def half_of(ref, side):
    width = ref.shape[1] // 2
    return ref[:, side * width : (side + 1) * width]


def prepare_body(
    late,
    rows_in,
    conv_in,
    filt_in,
    w_in_in,
    w_out_in,
    inc_in,
    own_out,
    other_out,
    later_own_out,
    later_other_out,
    keep_out,
    send_out,
    rows,
    conv,
    filt,
    w_in,
    w_out,
    inc,
    first,
    second,
    packs,
    laters,
    pairs,
    sems,
    out_sems,
):
    mine = late[0]
    channels = rows.shape[1]
    per = channels // rows.shape[0] // 2
    got_filt, got_rows, got_w_in, got_inc, got_w_out, got_conv = fetch(
        [
            (filt_in, filt),
            (rows_in, rows),
            (w_in_in, w_in),
            (inc_in, inc),
            (w_out_in, w_out),
            (conv_in, conv),
        ],
        sems,
    )
    got_filt.wait()
    for side in range(2):
        put_rows(first.at[side], half_of(filt[0], side), 0, 4 * per)
        put_rows(first.at[side], half_of(filt[1], side), per, 4 * per)
    got_rows.wait()
    got_w_in.wait()
    projected = mm(rows[...], w_in[...]).astype(BF)
    values = projected[:, :channels]
    gate_one = projected[:, channels : 2 * channels]
    gate_two = projected[:, 2 * channels :]
    got_inc.wait()
    got_w_out.wait()
    mix_two = mm_t(inc[...], w_out[...])
    grad_two = mix_two * gate_two.astype(F32)
    for side in range(2):
        put_rows(first.at[side], half_of(gate_one, side), 2 * per, 4 * per)
        put_rows(first.at[side], half_of(grad_two, side), 3 * per, 4 * per)
        packs[side] = first[side].astype(BF)
    sends = fetch([(packs.at[1 - mine], other_out), (packs.at[mine], own_out)], out_sems)
    got_conv.wait()
    gated = gate_one.astype(F32) * conv[0].astype(F32)
    for side in range(2):
        put_rows(second.at[side], half_of(values, side), 0, 2 * per)
        put_rows(second.at[side], half_of(gated, side), per, 2 * per)
        laters[side] = second[side].astype(BF)

    @pl.when(mine == 1)
    def _():
        part_two = (mix_two * conv[1].astype(F32)).astype(BF)
        for side in range(2):
            pairs[side, 0] = half_of(part_two, side)
            pairs[side, 1] = half_of(conv[0], side)

    @pl.when(mine == 0)
    def _():
        for side in range(2):
            pairs[side, 0] = half_of(gate_two, side)
            pairs[side, 1] = half_of(conv[1], side)

    for i, (source, target) in enumerate(
        [
            (laters.at[1 - mine], later_other_out),
            (laters.at[mine], later_own_out),
            (pairs.at[1 - mine], send_out),
            (pairs.at[mine], keep_out),
        ]
    ):
        send = pltpu.make_async_copy(source, target, out_sems.at[2 + i])
        send.start()
        sends.append(send)
    for send in sends:
        send.wait()


def signals(scratch, s, per):
    size = scratch.shape[1]
    stride = scratch.shape[0] // size
    return [scratch[pl.ds(s * per + k, size, stride=stride), :] for k in range(per)]


def send_rows(scratch, s, values):
    size = scratch.shape[1]
    stride = scratch.shape[0] // size
    for k, value in enumerate(values):
        scratch[pl.ds(s * len(values) + k, size, stride=stride), :] = value


def early_body(
    per,
    late,
    gains,
    data,
    later_own,
    later_got,
    outer_fwd,
    inner_fwd,
    inner_inv,
    outer_inv,
    turns,
    packed,
    spec_out,
    grad_out,
    known,
    out,
    spec,
    grad,
    later,
    later_rows,
    sems,
):
    size = data.shape[1]
    mine = late[0]
    laters = fetch([(later_own, later.at[mine]), (later_got, later.at[1 - mine])], sems)
    known[...] = data[...].astype(F32)
    filt_two = to_spectrum(signals(known, 1, per), outer_fwd, inner_fwd, turns)
    grad_two = signals(known, 3, per)
    spec_two = to_spectrum(grad_two, outer_fwd, inner_fwd, turns)
    spec[1] = spec_two
    mixed = from_spectrum(conj_times(filt_two, spec_two), inner_inv, outer_inv, turns)
    mix_one = [mixed[k] + gains[1, k] * grad_two[k] for k in range(per)]
    send_rows(out, 1, mix_one)
    gate_one = signals(known, 2, per)
    grad_one = [mix_one[k] * gate_one[k] for k in range(per)]
    for k in range(per):
        grad[pl.ds(k * size, size), :] = grad_one[k]
    filt_one = to_spectrum(signals(known, 0, per), outer_fwd, inner_fwd, turns)
    spec_one = to_spectrum(grad_one, outer_fwd, inner_fwd, turns)
    spec[0] = spec_one
    copies = [
        pltpu.make_async_copy(spec, spec_out, sems.at[2]),
        pltpu.make_async_copy(grad, grad_out, sems.at[3]),
    ]
    for copy in copies:
        copy.start()
    for copy in laters:
        copy.wait()
    for layer in range(2):
        later_rows[...] = later[layer].astype(F32)
        for s in range(2):
            send_rows(out, 4 - 2 * layer + s, signals(later_rows, s, per))
    mixed = from_spectrum(conj_times(filt_one, spec_one), inner_inv, outer_inv, turns)
    send_rows(out, 0, [mixed[k] + gains[0, k] * grad_one[k] for k in range(per)])
    packed[...] = out[...].astype(BF)
    for copy in copies:
        copy.wait()


def skip_row(per, base, grads, others):
    size = grads[0][0].shape[1]
    lane = lax.broadcasted_iota(jnp.int32, (1, size), 1)
    row = jnp.zeros((1, size), F32)
    for w in range(2):
        for k in range(per):
            term = grads[w][k] * others[w][k]
            total = jnp.sum(jnp.sum(term, axis=0, keepdims=True), axis=1, keepdims=True)
            high = total.astype(BF).astype(F32)
            row = jnp.where(lane == base + w * per + k, high, row)
            row = jnp.where(lane == base + (2 + w) * per + k, total - high, row)
    return row


def known_body(
    per,
    first,
    second,
    held,
    grad_held,
    outer_fwd,
    inner_fwd,
    inner_inv,
    outer_inv,
    turns,
    spec_out,
    filt_out,
    skip_out,
    known,
    other,
):
    size = second.shape[1]
    known[...] = first[...].astype(F32)
    other[...] = second[...].astype(F32)
    for s in range(2):
        spec_out[s] = to_spectrum(signals(other, 4 + s, per), outer_fwd, inner_fwd, turns)
    values, gated = signals(other, 2, per), signals(other, 3, per)
    for s, signal in enumerate((values, gated)):
        spec = to_spectrum(signal, outer_fwd, inner_fwd, turns)
        grads = from_spectrum(conj_times(spec, held[s]), inner_inv, outer_inv, turns)
        for k in range(per):
            filt_out[pl.ds((s * per + k) * size, size), :] = grads[k]
    grad_one = [grad_held[pl.ds(k * size, size), :] for k in range(per)]
    row = skip_row(per, 4 * per, (grad_one, signals(known, 3, per)), (values, gated))
    skip_out[...] = jnp.broadcast_to(row, skip_out.shape)


def late_body(
    per,
    gains,
    second,
    third,
    spec,
    filt_held,
    skip_held,
    outer_fwd_in,
    inner_fwd_in,
    inner_inv_in,
    outer_inv_in,
    turns_in,
    packed,
    known,
    other,
    out,
    outer_fwd,
    inner_fwd,
    inner_inv,
    outer_inv,
    turns,
    sems,
):
    size = third.shape[1]
    got_outer, got_turns, got_inner, got_inner_inv, got_outer_inv = fetch(
        [
            (outer_fwd_in, outer_fwd),
            (turns_in, turns),
            (inner_fwd_in, inner_fwd),
            (inner_inv_in, inner_inv),
            (outer_inv_in, outer_inv),
        ],
        sems,
    )
    known[...] = third[...].astype(F32)
    other[...] = second[...].astype(F32)
    for s in range(2):
        send_rows(
            out, 4 + s, [filt_held[pl.ds((s * per + k) * size, size), :] for k in range(per)]
        )
    rows = out.shape[0] // size
    out[pl.ds(6 * per + 1, size, stride=rows), :] = jnp.zeros((size, size), F32)
    got_outer.wait()
    got_turns.wait()
    got_inner.wait()
    grad_two = signals(known, 3, per)
    spec_two = to_spectrum(grad_two, outer_fwd, inner_fwd, turns)
    filt_two = to_spectrum(signals(known, 1, per), outer_fwd, inner_fwd, turns)
    got_inner_inv.wait()
    got_outer_inv.wait()
    mixed = from_spectrum(conj_times(filt_two, spec_two), inner_inv, outer_inv, turns)
    filt_one = to_spectrum(signals(known, 0, per), outer_fwd, inner_fwd, turns)
    send_rows(out, 3, from_spectrum(conj_times(spec[1], spec_two), inner_inv, outer_inv, turns))
    mix_one = [mixed[k] + gains[1, k] * grad_two[k] for k in range(per)]
    send_rows(out, 1, mix_one)
    gate_one = signals(known, 2, per)
    grad_one = [mix_one[k] * gate_one[k] for k in range(per)]
    row = skip_row(
        per, 0, (grad_one, grad_two), (signals(other, 4, per), signals(other, 5, per))
    )
    row = row + skip_held[pl.ds(0, 1), :]
    out[pl.ds(6 * per, size, stride=rows), :] = jnp.broadcast_to(row, (size, size))
    spec_one = to_spectrum(grad_one, outer_fwd, inner_fwd, turns)
    mixed = from_spectrum(conj_times(filt_one, spec_one), inner_inv, outer_inv, turns)
    send_rows(out, 2, from_spectrum(conj_times(spec[0], spec_one), inner_inv, outer_inv, turns))
    send_rows(out, 0, [mixed[k] + gains[0, k] * grad_one[k] for k in range(per)])
    packed[...] = out[...].astype(BF)


def hand_body(
    per,
    late,
    data,
    pair_keep,
    pair_got,
    w_own,
    w_got,
    partial,
    scratch,
    pair,
    w_in,
    sems,
):
    mine = late[0]
    half = pair.shape[2]

    def copies(side):
        pairs, weights = (pair_keep, w_own) if side == 1 else (pair_got, w_got)
        moves = [(pairs, pair)]
        for b in range(3):
            columns = pl.ds((2 * b + side) * half, half)
            moves.append((weights.at[:, columns], w_in.at[:, pl.ds(b * half, half)]))
        return [pltpu.make_async_copy(a, b, sems.at[i]) for i, (a, b) in enumerate(moves)]

    for side in range(2):

        @pl.when(mine == side)
        def _():
            for copy in copies(side):
                copy.start()

    scratch[...] = data[...].astype(F32)
    values = get_rows(scratch, 0, 6 * per, per).astype(BF)
    mix_one = get_rows(scratch, per, 6 * per, per)
    for side in range(2):

        @pl.when(mine == side)
        def _():
            for copy in copies(side):
                copy.wait()

    gate_one = (mix_one * pair[1].astype(F32)).astype(BF)
    partial[...] = mm_t(jnp.concatenate([values, gate_one, pair[0]], axis=1), w_in[...])


def regrad_body(
    per,
    late,
    inc,
    part_own,
    part_got,
    pair_keep,
    pair_got,
    w_own,
    w_got,
    pack_own,
    pack_got,
    packed,
    kept_out,
    part_two_out,
    scratch,
    pair,
    w_out,
    pack,
    kept,
    part_two,
    sems,
    out_sems,
):
    mine = late[0]
    half = pair.shape[2]

    def copies(side):
        if side == 0:
            moves = [(w_own, w_out), (pair_keep, pair), (pack_own, pack)]
        else:
            moves = [(w_got, w_out), (pair_got, pair), (pack_got, pack)]
        moves[0] = (moves[0][0].at[pl.ds(side * half, half), :], w_out)
        return [pltpu.make_async_copy(a, b, sems.at[i]) for i, (a, b) in enumerate(moves)]

    for side in range(2):

        @pl.when(mine == side)
        def _():
            for copy in copies(side):
                copy.start()

    result = (inc[...].astype(F32) + (part_own[...] + part_got[...])).astype(BF)
    kept[...] = result
    keep = pltpu.make_async_copy(kept, kept_out, out_sems.at[0])
    keep.start()
    for side in range(2):

        @pl.when(mine == side)
        def _():
            for copy in copies(side):
                copy.wait()

    mix_two = mm_t(result, w_out[...])
    part_two[...] = (mix_two * pair[1].astype(F32)).astype(BF)
    part = pltpu.make_async_copy(part_two, part_two_out, out_sems.at[1])
    part.start()
    scratch[...] = pack[...].astype(F32)
    put_rows(scratch, mix_two * pair[0].astype(F32), 3 * per, 4 * per)
    packed[...] = scratch[...].astype(BF)
    keep.wait()
    part.wait()


def finish_body(
    per,
    rescale,
    late,
    own,
    got,
    conv,
    part_own,
    part_got,
    inc,
    w_in,
    result,
    filt_grads,
    skip_grads,
    sides,
):
    mine = late[0]
    size = own.shape[1]
    half = per * size
    stride = own.shape[0] // size
    sides[mine] = own[...].astype(F32)
    sides[1 - mine] = got[...].astype(F32)

    def both(s):
        return jnp.concatenate(
            [get_rows(sides.at[side], s * per, stride, per) for side in range(2)], axis=1
        )

    def filter_and_skip(layer):
        filt_grads[0] = (both(2 + 2 * layer) * rescale).astype(BF)
        filt_grads[1] = (both(3 + 2 * layer) * rescale).astype(BF)
        for side in range(2):
            sums = sides[side, pl.ds(6 * per, size, stride=stride), :].T
            base = 4 * layer * per
            sums = (sums[base : base + 2 * per] + sums[base + 2 * per : base + 4 * per]) * rescale
            for w in range(2):
                for k in range(per):
                    row = w * per + k
                    skip_grads[pl.ds(w, 1), pl.ds(side * half + k * size, size)] = sums[
                        row : row + 1
                    ]

    @pl.when(mine == 0)
    def _():
        gate_one = both(1) * conv[0].astype(F32)
        proj = jnp.concatenate(
            [both(0).astype(BF), gate_one.astype(BF), part_own[...], part_got[...]], axis=1
        )
        result[...] = (inc[...].astype(F32) + mm_t(proj, w_in[...])).astype(BF)
        filter_and_skip(0)

    @pl.when(mine == 1)
    def _():
        result[...] = inc[...]
        filter_and_skip(1)


def call(body, out_shapes, scratch, *operands, smem=0, direct=(), direct_out=(), limit=VMEM_LIMIT):
    def space(i):
        if i < smem:
            return pltpu.SMEM
        return pltpu.HBM if i in direct else pltpu.VMEM

    return pl.pallas_call(
        body,
        out_shape=[
            (pltpu.HBM if i in direct_out else jax.ShapeDtypeStruct)(shape, dtype)
            for i, (shape, dtype) in enumerate(out_shapes)
        ],
        in_specs=[pl.BlockSpec(memory_space=space(i)) for i in range(len(operands))],
        out_specs=[
            pl.BlockSpec(memory_space=pltpu.HBM if i in direct_out else pltpu.VMEM)
            for i in range(len(out_shapes))
        ],
        scratch_shapes=[
            pltpu.VMEM(shape, F32) if isinstance(shape, tuple) else shape for shape in scratch
        ],
        compiler_params=pltpu.CompilerParams(vmem_limit_bytes=limit),
    )(
        *[
            pltpu.with_memory_space_constraint(x, pltpu.HBM) if i in direct else x
            for i, x in enumerate(operands)
        ]
    )


def exchange(rows, parts):
    per_part = rows.shape[0] // parts
    tile = math.gcd(per_part, 8)
    cut = rows.reshape(parts, per_part // tile, tile, rows.shape[1])
    return lax.all_to_all(cut, "seq", split_axis=0, concat_axis=0, tiled=True).reshape(rows.shape)


def on_device(layer_input, conv_out, filters, skip_gain, weight_in, weight_out, grad_output):
    tokens, channels = grad_output.shape
    parts = lax.axis_size("seq")
    per = channels // parts // 2
    half = channels // 2
    w_in, w_out, conv = weight_in[0], weight_out[0], conv_out[0]
    tables = transform_tables(parts, tokens)
    outer_fwd, inner_fwd, inner_inv, outer_inv, turns = tables
    section = lax.axis_index("section").astype(jnp.int32)
    late = section.reshape(1)

    def rows(count):
        return (parts * count, tokens)

    def vmem(*shape):
        return pltpu.VMEM(shape, BF)

    def sems(count):
        return pltpu.SemaphoreType.DMA((count,))

    def swap(value, pairs=((0, 1), (1, 0))):
        return lax.ppermute(value, "section", pairs)

    spectra = (2, per * parts, 2 * tokens)
    pair = ((2, tokens, half), BF)

    pack_own, pack_other, later_own, later_other, pair_keep, pair_send = call(
        prepare_body,
        [(rows(4 * per), BF)] * 2 + [(rows(2 * per), BF)] * 2 + [pair] * 2,
        [
            vmem(tokens, channels),
            vmem(2, tokens, channels),
            vmem(2, tokens, channels),
            vmem(*w_in.shape),
            vmem(*w_out.shape),
            vmem(tokens, channels),
            (2, *rows(4 * per)),
            (2, *rows(2 * per)),
            vmem(2, *rows(4 * per)),
            vmem(2, *rows(2 * per)),
            vmem(2, *pair[0]),
            sems(6),
            sems(6),
        ],
        late, layer_input[0], conv, filters[0], w_in, w_out, grad_output,
        smem=1, direct=range(1, 7), direct_out=range(6),
    )
    pack_got = swap(pack_other)
    packed = jnp.where(section == 1, pack_own, pack_got)
    first = exchange(packed, parts)

    later_got = swap(later_other)
    gains_got = swap(skip_gain[0])
    pair_got = swap(pair_send)
    w_in_got = swap(w_in, ((1, 0),))
    w_out_got = swap(w_out, ((0, 1),))

    def own_channels(gains):
        return lax.dynamic_slice(
            gains.reshape(2, 2 * per, parts), (0, section * per, lax.axis_index("seq")), (2, per, 1)
        )[:, :, 0]

    gains_early = own_channels(jnp.where(section == 1, skip_gain[0], gains_got))
    gains_late = own_channels(jnp.where(section == 1, gains_got, skip_gain[0]))

    packed, held, grad_held = call(
        functools.partial(early_body, per),
        [(rows(6 * per), BF), (spectra, F32), (rows(per), F32)],
        [
            rows(4 * per), rows(6 * per), spectra, rows(per), vmem(2, *rows(2 * per)),
            rows(2 * per), sems(4),
        ],
        late, gains_early, first, later_own, later_got, *tables,
        smem=2, direct=(3, 4), direct_out=(1, 2),
    )
    second = exchange(packed, parts)
    (partial,) = call(
        functools.partial(hand_body, per),
        [((tokens, channels), F32)],
        [rows(6 * per), vmem(2, tokens, half), vmem(channels, 3 * half), sems(4)],
        late, second, pair_keep, pair_got, w_in, w_in_got,
        smem=1, direct=(2, 3, 4, 5),
    )
    partial_got = swap(partial)
    packed, kept, part_two = call(
        functools.partial(regrad_body, per),
        [(rows(4 * per), BF), ((tokens, channels), BF), ((tokens, half), BF)],
        [
            rows(4 * per), vmem(2, tokens, half), vmem(half, channels), vmem(*rows(4 * per)),
            vmem(tokens, channels), vmem(tokens, half), sems(3), sems(2),
        ],
        late, grad_output, partial, partial_got, pair_keep, pair_got, w_out, w_out_got,
        pack_own, pack_got,
        smem=1, direct=range(4, 10), direct_out=(1, 2),
    )
    third = exchange(packed, parts)
    part_two_got = swap(part_two)
    spec, filt_held, skip_held = call(
        functools.partial(known_body, per),
        [(spectra, F32), (rows(2 * per), F32), ((8, tokens), F32)],
        [rows(4 * per), rows(6 * per)],
        first, second, held, grad_held, *tables,
    )
    out_rows = 6 * per + 2
    (packed,) = call(
        functools.partial(late_body, per),
        [(rows(out_rows), BF)],
        [
            rows(4 * per), rows(6 * per), rows(out_rows),
            vmem(*outer_fwd.shape), vmem(*inner_fwd.shape), vmem(*inner_inv.shape),
            vmem(*outer_inv.shape), turns.shape, sems(5),
        ],
        gains_late, second, third, spec, filt_held, skip_held, *tables,
        smem=1, direct=range(6, 11),
    )
    back = exchange(packed, parts)
    back_got = swap(back)
    grad_rows, filter_grads, skip_grads = call(
        functools.partial(finish_body, per, 1.0 / math.sqrt(parts * tokens)),
        [((tokens, channels), BF), ((2, tokens, channels), BF), ((2, channels), F32)],
        [(2, *rows(out_rows))],
        late, back, back_got, conv, part_two, part_two_got, kept, w_in,
        smem=1,
    )
    return (grad_rows[None], filter_grads[None], skip_grads[None])


def solution(mesh):
    in_specs = (
        P("section", "seq", None),
        P("section", None, "seq", None),
        P("section", None, "seq", None),
        P("section", None, None),
        P("section", None, None),
        P("section", None, None),
        P("seq", None),
    )
    out_specs = (
        P("section", "seq", None),
        P("section", None, "seq", None),
        P("section", None, None),
    )
    return jax.shard_map(
        on_device, mesh=mesh, in_specs=in_specs, out_specs=out_specs, check_vma=False
    )
```

time: 124 us -> 127 us (1.024); the launches traced: 123 us -> 125 us
  blocking collectives: 46 us -> 24 us
  starting transfers between devices: 24.5 us -> 39.2 us
  waiting for transfers between devices: 34 us -> 40.8 us
  Pallas kernels: 16 us -> 18.7 us
  local copies, waits for them, and re-layouts: 2.11 us -> 0.39 us
    all_to_all x2 -> x1, blocking collectives: 46 us -> 24 us  [exchange(): lax.all_to_all(cut, 'seq', split_axis=0, concat_axis=0, tiled=True)]
    ppermute x1 -> x9, starting transfers between devices: 1.29 us -> 9.53 us  [swap(): return lax.ppermute(value, 'section', pairs)]
    all_to_all x2 -> x3, starting transfers between devices: 23.2 us -> 29.7 us  [exchange(): lax.all_to_all(cut, 'seq', split_axis=0, concat_axis=0, tiled=True)]
    ppermute x1 -> x9, waiting for transfers between devices: 1.94 us -> 5.78 us  [swap(): return lax.ppermute(value, 'section', pairs)]
    all_to_all x2 -> x3, waiting for transfers between devices: 32 us -> 35.1 us  [exchange(): lax.all_to_all(cut, 'seq', split_axis=0, concat_axis=0, tiled=True)]
    pallas_call x7, Pallas kernels: 16 us -> 18.7 us  [call(): pl.pallas_call(body, out_shape=[(pltpu.HBM if i in direct_out else jax.Sh...]
    unnamed x29 -> x36, local copies, waits for them, and re-layouts: 2.02 us -> 0.28 us
  transfers between devices with their start and end apart: 3 -> 12, of which waited for: 3 -> 9; matrix products, arithmetic and copies ran while one was open for 0% -> 1% of each run, Pallas kernels for 1% -> 6%
where the time goes in v3:
time: 127 us; the launch traced here: 125 us
  waiting for transfers between devices  40.8 us (32%)
  starting transfers between devices  39.2 us (31%)
  blocking collectives  24 us (19%)
  Pallas kernels  18.7 us (15%)
    all_to_all x3, waiting for transfers between devices, exchange(): lax.all_to_all(cut, 'seq', split_axis=0, concat_axis=0, tiled=True)  35.1 us
    all_to_all x3, starting transfers between devices, exchange(): lax.all_to_all(cut, 'seq', split_axis=0, concat_axis=0, tiled=True)  29.7 us
    all_to_all x1, blocking collectives, exchange(): lax.all_to_all(cut, 'seq', split_axis=0, concat_axis=0, tiled=True)  24 us
    pallas_call x7, Pallas kernels, call(): pl.pallas_call(body, out_shape=[(pltpu.HBM if i in direct_out else jax.Sh...  18.7 us
    ppermute x9, starting transfers between devices, swap(): return lax.ppermute(value, 'section', pairs)  9.53 us
    ppermute x9, waiting for transfers between devices, swap(): return lax.ppermute(value, 'section', pairs)  5.78 us
  transfers between devices with their start and end apart: 12, of which 9 were waited for; matrix products, arithmetic and copies ran while one was open for 1% of the time, Pallas kernels for 6%

profile of v3, /device:TPU:8, one launch (start us, length us, event | category | flops | bytes accessed | tf_op | source)
XLA Modules:
  0.0 124.8 jit_solution(4560644564468050931)
XLA Ops:
  0.7 0.0 copy-start.2
  0.7 3.6 %shard_map.139 = (bf16[1024,128]{1,0:T(8,128)(2,1)}, bf16[1024,128]{1,0:T(8,128)(2,1)}, bf16[512,128]{1,0:T(8,128)(2,1)}, bf16[512,128]{1,0:T(8,128)(2,1)}, bf16...) custom-call(s32[1]{0:T(128)} %bitcast.late, bf16[128,512]{1,0:T(8,128)(2,1)} %bitcast.48, ...), custom_call_target="tpu_custom_call" | custom-call | tf_op jit(solution)/shard_map/pallas_call | solution.py:590
  4.4 0.1 collective-permute-start.1
  4.5 1.3 %collective-permute-start.4 = (bf16[512,1536]{1,0:T(8,128)(2,1)S(1)}, bf16[512,1536]{1,0:T(8,128)(2,1)}, u32[]{:S(2)}, u32[]{:S(2)}) collective-permute-start(bf16[512,1536]{1,0:T(8,128)(2,1)S(1)} %bitcast.29), channel_id=1, source_target_pairs={{1,0},{3,2},{5,4},{7,6},{9,8},{11,10},{13,12},{15,14},{17,16},{19,... | collective-permute-start | bytes 4718600 | tf_op jit(solution)/shard_map/ppermute | solution.py:641
  5.8 0.4 collective-permute-done.1.pack_got
  6.2 0.8 select_bitcast_fusion
  7.0 15.3 %all-to-all-start = ((bf16[128,1,8,128]{3,2,1,0:T(8,128)(2,1)}), bf16[128,1,8,128]{3,2,1,0:T(8,128)(2,1)S(1)}, u32[]{:S(2)}, u32[]{:S(2)}) async-start(bf16[128,1,8,128]{3,2,1,0:T(8,128)(2,1)} %select_bitcast_fusion), calls=%async_computation | async-start | bytes 524288 | tf_op jit(solution)/shard_map/all_to_all | solution.py:617
  22.4 2.4 %collective-permute-start = (f32[2,512]{1,0:T(2,128)S(1)}, f32[2,512]{1,0:T(2,128)S(1)}, u32[]{:S(2)}, u32[]{:S(2)}) collective-permute-start(f32[2,512]{1,0:T(2,128)S(1)} %bitcast.49), channel_id=1, source_target_pairs={{0,1},{1,0},{2,3},{3,2},{4,5},{5,4},{6,7},{7,6},{8,9},{9,8},{10,11... | collective-permute-start | bytes 12296 | tf_op jit(solution)/shard_map/ppermute | solution.py:641
  24.8 0.1 collective-permute-start.2
  24.9 0.7 collective-permute-done
  25.6 0.1 constant_dynamic-slice_fusion
  25.7 0.1 copy.22
  25.8 0.5 collective-permute-done.2.later_got
  26.3 9.4 %all-to-all-done = bf16[128,1,8,128]{3,2,1,0:T(8,128)(2,1)S(1)} async-done(((bf16[128,1,8,128]{3,2,1,0:T(8,128)(2,1)}), bf16[128,1,8,128]{3,2,1,0:T(8,128)(2,1)S(1)}, u32[]{:S(2)}, u32[]{:S(2)}) %all-to-all-start) | async-done | bytes 262176 | tf_op jit(solution)/shard_map/all_to_all | solution.py:617
  35.8 3.6 %shard_map.140 = (bf16[1536,128]{1,0:T(8,128)(2,1)}, f32[2,256,256]{2,1,0:T(8,128)}, f32[256,128]{1,0:T(8,128)}) custom-call(s32[1]{0:T(128)} %bitcast.late, f32[2,2]{1,0:T(2,128)S(1)} %bitcast.43, bf16[1024,128]{1,0:T(8,128)(2,1)S(1)} %bitcast.34, bf16[512,128]{1,0:T(8,128)(2,1)} %get-tuple-element.23.later_own, bf16[512,128]{1,0:T(8,128)(2,1)} %copy-done.15, ...), custom_call_target="tpu_custom_call" | custom-call | tf_op jit(solution)/shard_map/pallas_call | solution.py:590
  39.4 7.7 %all-to-all-start.1 = ((bf16[128,3,4,128]{3,2,1,0:T(4,128)(2,1)}), bf16[128,3,4,128]{3,2,1,0:T(4,128)(2,1)S(1)}, u32[]{:S(2)}, u32[]{:S(2)}) async-start(bf16[128,3,4,128]{3,2,1,0:T(4,128)(2,1)} %bitcast.12), calls=%async_computation.1 | async-start | bytes 786432 | tf_op jit(solution)/shard_map/all_to_all | solution.py:617
  47.1 3.8 %collective-permute-start.6 = (bf16[512,512]{1,0:T(8,128)(2,1)}, bf16[512,512]{1,0:T(8,128)(2,1)}, u32[]{:S(2)}, u32[]{:S(2)}) collective-permute-start(bf16[512,512]{1,0:T(8,128)(2,1)} %bitcast.45), channel_id=1, source_target_pairs={{0,1},{2,3},{4,5},{6,7},{8,9},{10,11},{12,13},{14,15},{16,17},{18,... | collective-permute-start | bytes 1572872 | tf_op jit(solution)/shard_map/ppermute | solution.py:641
  50.9 1.6 %collective-permute-done.3.pair_got = bf16[2,128,256]{2,1,0:T(8,128)(2,1)S(1)} collective-permute-done((bf16[2,128,256]{2,1,0:T(8,128)(2,1)}, bf16[2,128,256]{2,1,0:T(8,128)(2,1)S(1)}, u32[]{:S(2)}, u32[]{:S(2)}) %collective-permute-start.3) | collective-permute-done | bytes 131104 | tf_op jit(solution)/shard_map/ppermute | solution.py:641
  52.5 12.0 %all-to-all-done.1 = bf16[128,3,4,128]{3,2,1,0:T(4,128)(2,1)S(1)} async-done(((bf16[128,3,4,128]{3,2,1,0:T(4,128)(2,1)}), bf16[128,3,4,128]{3,2,1,0:T(4,128)(2,1)S(1)}, u32[]{:S(2)}, u32[]{:S(2)}) %all-to-all-start.1) | async-done | bytes 393248 | tf_op jit(solution)/shard_map/all_to_all | solution.py:617
  64.5 1.7 %shard_map.141.part_own = f32[128,512]{1,0:T(8,128)S(1)} custom-call(s32[1]{0:T(128)} %bitcast.late, bf16[1536,128]{1,0:T(8,128)(2,1)S(1)} %bitcast.31, bf16[2,128,256]{2,1,0:T(8,128)(2,1)} %get-tuple-element.26.pair_keep, bf16[2,128,256]{2,1,0:T(8,128)(2,1)} %copy-done.14, bf16[512,1536]{1,0:T(8,128)(2,1)} %bitcast.28, ...), custom_call_target="tpu_custom_call" | custom-call | tf_op jit(solution)/shard_map/pallas_call | solution.py:590
  66.2 1.3 %collective-permute-start.5 = (f32[128,512]{1,0:T(8,128)S(1)}, f32[128,512]{1,0:T(8,128)S(1)}, u32[]{:S(2)}, u32[]{:S(2)}) collective-permute-start(f32[128,512]{1,0:T(8,128)S(1)} %shard_map.141.part_own), channel_id=1, source_target_pairs={{0,1},{1,0},{2,3},{3,2},{4,5},{5,4},{6,7},{7,6},{8,9},{9,8},{10,11... | collective-permute-start | bytes 786440 | tf_op jit(solution)/shard_map/ppermute | solution.py:641
  67.5 1.2 collective-permute-done.5.part_got
  68.7 2.7 %shard_map.142 = (bf16[1024,128]{1,0:T(8,128)(2,1)}, bf16[128,512]{1,0:T(8,128)(2,1)}, bf16[128,256]{1,0:T(8,128)(2,1)}) custom-call(s32[1]{0:T(128)} %bitcast.late, bf16[128,512]{1,0:T(8,128)(2,1)S(1)} %copy-done.9, f32[128,512]{1,0:T(8,128)S(1)} %shard_map.141.part_own, f32[128,512]{1,0:T(8,128)S(1)} %collective-permute-done.5.part_got, ...), custom_call_target="tpu_custom_call" | custom-call | tf_op jit(solution)/shard_map/pallas_call | solution.py:590
  71.4 6.7 %all-to-all-start.2 = ((bf16[128,1,8,128]{3,2,1,0:T(8,128)(2,1)}), bf16[128,1,8,128]{3,2,1,0:T(8,128)(2,1)S(1)}, u32[]{:S(2)}, u32[]{:S(2)}) async-start(bf16[128,1,8,128]{3,2,1,0:T(8,128)(2,1)} %bitcast.15), calls=%async_computation.2 | async-start | bytes 524288 | tf_op jit(solution)/shard_map/all_to_all | solution.py:617
  78.1 0.1 copy.21
  78.2 1.7 %shard_map.143 = (f32[2,256,256]{2,1,0:T(8,128)S(1)}, f32[512,128]{1,0:T(8,128)S(1)}, f32[8,128]{1,0:T(8,128)S(1)}) custom-call(bf16[1024,128]{1,0:T(8,128)(2,1)S(1)} %bitcast.35, bf16[1536,128]{1,0:T(8,128)(2,1)S(1)} %bitcast.32, f32[2,256,256]{2,1,0:T(8,128)S(1)} %copy-done.8, f32[256,128]{1,0:T(8,128)S(1)} %copy-done.10, bf16[256,256]{1,0:T(8,128)(2,1)S(1)} %copy-done.4, ...), custom_call_target="tpu_custom_call" | custom-call | tf_op jit(solution)/shard_map/pallas_call | solution.py:590
  79.9 13.6 %all-to-all-done.2 = bf16[128,1,8,128]{3,2,1,0:T(8,128)(2,1)S(1)} async-done(((bf16[128,1,8,128]{3,2,1,0:T(8,128)(2,1)}), bf16[128,1,8,128]{3,2,1,0:T(8,128)(2,1)S(1)}, u32[]{:S(2)}, u32[]{:S(2)}) %all-to-all-start.2) | async-done | bytes 262176 | tf_op jit(solution)/shard_map/all_to_all | solution.py:617
  93.6 3.7 %shard_map.144 = bf16[1792,128]{1,0:T(8,128)(2,1)S(1)} custom-call(f32[2,2]{1,0:T(2,128)S(1)} %bitcast.42, bf16[1536,128]{1,0:T(8,128)(2,1)S(1)} %bitcast.33, bf16[1024,128]{1,0:T(8,128)(2,1)S(1)} %bitcast.41, f32[2,256,256]{2,1,0:T(8,128)S(1)} %get-tuple-element.31.spec, f32[512,128]{1,0:T(8,128)S(1)} %get-tuple-element.32.filt_held, ...), custom_call_target="tpu_custom_call" | custom-call | tf_op jit(solution)/shard_map/pallas_call | solution.py:590
  97.3 24.0 %all_to_all.20 = bf16[128,7,2,128]{3,2,1,0:T(2,128)(2,1)S(1)} all-to-all(bf16[128,7,2,128]{3,2,1,0:T(2,128)(2,1)S(1)} %bitcast.38), channel_id=1, replica_groups=mesh['seq'=128,'section'=2] {'seq'}, dimensions={0} | all-to-all | bytes 917504 | tf_op jit(solution)/shard_map/all_to_all | solution.py:617
  121.3 0.5 collective-permute-start.8
  121.8 1.4 %collective-permute-done.8.part_got = bf16[128,256]{1,0:T(8,128)(2,1)S(1)} collective-permute-done((bf16[128,256]{1,0:T(8,128)(2,1)S(1)}, bf16[128,256]{1,0:T(8,128)(2,1)S(1)}, u32[]{:S(2)}, u32[]{:S(2)}) %collective-permute-start.8) | collective-permute-done | bytes 65568 | tf_op jit(solution)/shard_map/ppermute | solution.py:641
  123.3 1.5 %shard_map.145 = (bf16[128,512]{1,0:T(8,128)(2,1)}, bf16[2,128,512]{2,1,0:T(8,128)(2,1)}, f32[2,512]{1,0:T(2,128)}) custom-call(s32[1]{0:T(128)} %bitcast.late, bf16[1792,128]{1,0:T(8,128)(2,1)S(1)} %bitcast.37, bf16[1792,128]{1,0:T(8,128)(2,1)S(1)} %collective-permute-done.7.got, bf16[2,128,512]{2,1,0:T(8,128)(2,1)S(1)} %bitcast.40, ...), custom_call_target="tpu_custom_call" | custom-call | tf_op jit(solution)/shard_map/pallas_call | solution.py:590
  (41 shorter events, 0.1 us)
Async XLA Ops:
  0.6 3.8 %copy-start = (bf16[1,512,1536]{2,1,0:T(8,128)(2,1)S(1)}, bf16[1,512,1536]{2,1,0:T(8,128)(2,1)}, u32[]{:S(2)}) copy-start(bf16[1,512,1536]{2,1,0:T(8,128)(2,1)} %param.16) | copy-start | bytes 4718596
  0.6 21.7 %copy-start.16 = (f32[1,2,512]{2,1,0:T(2,128)S(1)}, f32[1,2,512]{2,1,0:T(2,128)}, u32[]{:S(2)}) copy-start(f32[1,2,512]{2,1,0:T(2,128)} %param.15) | copy-start | bytes 12292
  0.7 35.1 %copy-start.2 = (bf16[512,256]{1,0:T(8,128)(2,1)S(1)}, bf16[512,256]{1,0:T(8,128)(2,1)}, u32[]{:S(2)}) copy-start(bf16[512,256]{1,0:T(8,128)(2,1)} %constant.29.clone.inner_fwd.inner_fwd_in) | copy-start | bytes 786436
  0.7 35.1 %copy-start.3 = (bf16[512,256]{1,0:T(8,128)(2,1)S(1)}, bf16[512,256]{1,0:T(8,128)(2,1)}, u32[]{:S(2)}) copy-start(bf16[512,256]{1,0:T(8,128)(2,1)} %constant.30.clone.inner_inv.inner_inv_in) | copy-start | bytes 786436
  0.7 35.1 %copy-start.4 = (bf16[256,256]{1,0:T(8,128)(2,1)S(1)}, bf16[256,256]{1,0:T(8,128)(2,1)}, u32[]{:S(2)}) copy-start(bf16[256,256]{1,0:T(8,128)(2,1)} %constant.28.clone.outer_fwd.outer_fwd_in) | copy-start | bytes 393220
  0.7 35.1 %copy-start.5 = (bf16[128,512]{1,0:T(8,128)(2,1)S(1)}, bf16[128,512]{1,0:T(8,128)(2,1)}, u32[]{:S(2)}) copy-start(bf16[128,512]{1,0:T(8,128)(2,1)} %constant.31.clone.outer_inv.outer_inv_in) | copy-start | bytes 393220
  0.7 35.1 %copy-start.6 = (f32[2,128,128]{2,1,0:T(8,128)S(1)}, f32[2,128,128]{2,1,0:T(8,128)}, u32[]{:S(2)}) copy-start(f32[2,128,128]{2,1,0:T(8,128)} %constant.32.clone.turns.turns_in) | copy-start | bytes 393220
  4.4 1.8 %collective-permute-start.1 = (bf16[1024,128]{1,0:T(8,128)(2,1)}, bf16[1024,128]{1,0:T(8,128)(2,1)S(1)}, u32[]{:S(2)}, u32[]{:S(2)}) collective-permute-start(bf16[1024,128]{1,0:T(8,128)(2,1)} %get-tuple-element.22), channel_id=1, source_target_pairs={{0,1},{1,0},{2,3},{3,2},{4,5},{5,4},{6,7},{7,6},{8,9},{9,8},{10,11... | collective-permute-start | bytes 786440 | tf_op jit(solution)/shard_map/ppermute | solution.py:641
  4.5 60.0 %collective-permute-start.4 = (bf16[512,1536]{1,0:T(8,128)(2,1)S(1)}, bf16[512,1536]{1,0:T(8,128)(2,1)}, u32[]{:S(2)}, u32[]{:S(2)}) collective-permute-start(bf16[512,1536]{1,0:T(8,128)(2,1)S(1)} %bitcast.29), channel_id=1, source_target_pairs={{1,0},{3,2},{5,4},{7,6},{9,8},{11,10},{13,12},{15,14},{17,16},{19,... | collective-permute-start | bytes 4718600 | tf_op jit(solution)/shard_map/ppermute | solution.py:641
  6.2 33.2 %copy-start.13 = (bf16[1024,128]{1,0:T(8,128)(2,1)}, bf16[1024,128]{1,0:T(8,128)(2,1)S(1)}, u32[]{:S(2)}) copy-start(bf16[1024,128]{1,0:T(8,128)(2,1)S(1)} %collective-permute-done.1.pack_got) | copy-start | bytes 786436
  7.0 28.8 %all-to-all-start = ((bf16[128,1,8,128]{3,2,1,0:T(8,128)(2,1)}), bf16[128,1,8,128]{3,2,1,0:T(8,128)(2,1)S(1)}, u32[]{:S(2)}, u32[]{:S(2)}) async-start(bf16[128,1,8,128]{3,2,1,0:T(8,128)(2,1)} %select_bitcast_fusion), calls=%async_computation | async-start | bytes 524288 | tf_op jit(solution)/shard_map/all_to_all | solution.py:617
  22.4 3.2 %collective-permute-start = (f32[2,512]{1,0:T(2,128)S(1)}, f32[2,512]{1,0:T(2,128)S(1)}, u32[]{:S(2)}, u32[]{:S(2)}) collective-permute-start(f32[2,512]{1,0:T(2,128)S(1)} %bitcast.49), channel_id=1, source_target_pairs={{0,1},{1,0},{2,3},{3,2},{4,5},{5,4},{6,7},{7,6},{8,9},{9,8},{10,11... | collective-permute-start | bytes 12296 | tf_op jit(solution)/shard_map/ppermute | solution.py:641
  24.8 1.6 %collective-permute-start.2 = (bf16[512,128]{1,0:T(8,128)(2,1)}, bf16[512,128]{1,0:T(8,128)(2,1)S(1)}, u32[]{:S(2)}, u32[]{:S(2)}) collective-permute-start(bf16[512,128]{1,0:T(8,128)(2,1)} %get-tuple-element.24), channel_id=1, source_target_pairs={{0,1},{1,0},{2,3},{3,2},{4,5},{5,4},{6,7},{7,6},{8,9},{9,8},{10,11... | collective-permute-start | bytes 393224 | tf_op jit(solution)/shard_map/ppermute | solution.py:641
  26.3 9.4 %copy-start.15 = (bf16[512,128]{1,0:T(8,128)(2,1)}, bf16[512,128]{1,0:T(8,128)(2,1)S(1)}, u32[]{:S(2)}) copy-start(bf16[512,128]{1,0:T(8,128)(2,1)S(1)} %collective-permute-done.2.later_got) | copy-start | bytes 393220
  39.4 25.1 %all-to-all-start.1 = ((bf16[128,3,4,128]{3,2,1,0:T(4,128)(2,1)}), bf16[128,3,4,128]{3,2,1,0:T(4,128)(2,1)S(1)}, u32[]{:S(2)}, u32[]{:S(2)}) async-start(bf16[128,3,4,128]{3,2,1,0:T(4,128)(2,1)} %bitcast.12), calls=%async_computation.1 | async-start | bytes 786432 | tf_op jit(solution)/shard_map/all_to_all | solution.py:617
  47.1 20.4 %collective-permute-start.6 = (bf16[512,512]{1,0:T(8,128)(2,1)}, bf16[512,512]{1,0:T(8,128)(2,1)}, u32[]{:S(2)}, u32[]{:S(2)}) collective-permute-start(bf16[512,512]{1,0:T(8,128)(2,1)} %bitcast.45), channel_id=1, source_target_pairs={{0,1},{2,3},{4,5},{6,7},{8,9},{10,11},{12,13},{14,15},{16,17},{18,... | collective-permute-start | bytes 1572872 | tf_op jit(solution)/shard_map/ppermute | solution.py:641
  50.9 1.6 %collective-permute-start.3 = (bf16[2,128,256]{2,1,0:T(8,128)(2,1)}, bf16[2,128,256]{2,1,0:T(8,128)(2,1)S(1)}, u32[]{:S(2)}, u32[]{:S(2)}) collective-permute-start(bf16[2,128,256]{2,1,0:T(8,128)(2,1)} %get-tuple-element.27), channel_id=1, source_target_pairs={{0,1},{1,0},{2,3},{3,2},{4,5},{5,4},{6,7},{7,6},{8,9},{9,8},{10,11... | collective-permute-start | bytes 393224 | tf_op jit(solution)/shard_map/ppermute | solution.py:641
  52.5 12.0 %copy-start.14 = (bf16[2,128,256]{2,1,0:T(8,128)(2,1)}, bf16[2,128,256]{2,1,0:T(8,128)(2,1)S(1)}, u32[]{:S(2)}) copy-start(bf16[2,128,256]{2,1,0:T(8,128)(2,1)S(1)} %collective-permute-done.3.pair_got) | copy-start | bytes 393220
  64.5 4.2 %copy-start.9 = (bf16[128,512]{1,0:T(8,128)(2,1)S(1)}, bf16[128,512]{1,0:T(8,128)(2,1)}, u32[]{:S(2)}) copy-start(bf16[128,512]{1,0:T(8,128)(2,1)} %inc.1) | copy-start | bytes 393220
  66.2 12.0 %copy-start.8 = (f32[2,256,256]{2,1,0:T(8,128)S(1)}, f32[2,256,256]{2,1,0:T(8,128)}, u32[]{:S(2)}) copy-start(f32[2,256,256]{2,1,0:T(8,128)} %get-tuple-element.29.held) | copy-start | bytes 1572868
  66.2 12.0 %copy-start.10 = (f32[256,128]{1,0:T(8,128)S(1)}, f32[256,128]{1,0:T(8,128)}, u32[]{:S(2)}) copy-start(f32[256,128]{1,0:T(8,128)} %get-tuple-element.30.grad_held) | copy-start | bytes 393220
  66.2 2.5 %collective-permute-start.5 = (f32[128,512]{1,0:T(8,128)S(1)}, f32[128,512]{1,0:T(8,128)S(1)}, u32[]{:S(2)}, u32[]{:S(2)}) collective-permute-start(f32[128,512]{1,0:T(8,128)S(1)} %shard_map.141.part_own), channel_id=1, source_target_pairs={{0,1},{1,0},{2,3},{3,2},{4,5},{5,4},{6,7},{7,6},{8,9},{9,8},{10,11... | collective-permute-start | bytes 786440 | tf_op jit(solution)/shard_map/ppermute | solution.py:641
  71.4 22.1 %all-to-all-start.2 = ((bf16[128,1,8,128]{3,2,1,0:T(8,128)(2,1)}), bf16[128,1,8,128]{3,2,1,0:T(8,128)(2,1)S(1)}, u32[]{:S(2)}, u32[]{:S(2)}) async-start(bf16[128,1,8,128]{3,2,1,0:T(8,128)(2,1)} %bitcast.15), calls=%async_computation.2 | async-start | bytes 524288 | tf_op jit(solution)/shard_map/all_to_all | solution.py:617
  93.6 27.8 %copy-start.12 = (bf16[128,256]{1,0:T(8,128)(2,1)S(1)}, bf16[128,256]{1,0:T(8,128)(2,1)}, u32[]{:S(2)}) copy-start(bf16[128,256]{1,0:T(8,128)(2,1)} %get-tuple-element.34.part_own) | copy-start | bytes 196612
  93.6 29.7 %copy-start.1 = (bf16[1,512,1536]{2,1,0:T(8,128)(2,1)S(1)}, bf16[1,512,1536]{2,1,0:T(8,128)(2,1)}, u32[]{:S(2)}) copy-start(bf16[1,512,1536]{2,1,0:T(8,128)(2,1)} %param.16) | copy-start | bytes 4718596
  93.6 29.7 %copy-start.7 = (bf16[1,2,128,512]{3,2,1,0:T(8,128)(2,1)S(1)}, bf16[1,2,128,512]{3,2,1,0:T(8,128)(2,1)}, u32[]{:S(2)}) copy-start(bf16[1,2,128,512]{3,2,1,0:T(8,128)(2,1)} %param.13) | copy-start | bytes 786436
  93.6 29.7 %copy-start.11 = (bf16[128,512]{1,0:T(8,128)(2,1)S(1)}, bf16[128,512]{1,0:T(8,128)(2,1)}, u32[]{:S(2)}) copy-start(bf16[128,512]{1,0:T(8,128)(2,1)} %get-tuple-element.35.inc) | copy-start | bytes 393220
  121.3 1.9 %collective-permute-start.7 = (bf16[1792,128]{1,0:T(8,128)(2,1)S(1)}, bf16[1792,128]{1,0:T(8,128)(2,1)S(1)}, u32[]{:S(2)}, u32[]{:S(2)}) collective-permute-start(bf16[1792,128]{1,0:T(8,128)(2,1)S(1)} %bitcast.36), channel_id=1, source_target_pairs={{0,1},{1,0},{2,3},{3,2},{4,5},{5,4},{6,7},{7,6},{8,9},{9,8},{10,11... | collective-permute-start | bytes 1376264 | tf_op jit(solution)/shard_map/ppermute | solution.py:641
  121.3 1.9 %collective-permute-start.8 = (bf16[128,256]{1,0:T(8,128)(2,1)S(1)}, bf16[128,256]{1,0:T(8,128)(2,1)S(1)}, u32[]{:S(2)}, u32[]{:S(2)}) collective-permute-start(bf16[128,256]{1,0:T(8,128)(2,1)S(1)} %copy-done.12), channel_id=1, source_target_pairs={{0,1},{1,0},{2,3},{3,2},{4,5},{5,4},{6,7},{7,6},{8,9},{9,8},{10,11... | collective-permute-start | bytes 196616 | tf_op jit(solution)/shard_map/ppermute | solution.py:641

commit v4 on v2

--- a/solution.py
+++ b/solution.py
@@ -142,7 +142,6 @@
     inc,
     first,
     second,
-    packed,
     later,
     gate_two_kept,
     part_two_kept,
@@ -175,9 +174,8 @@
     got_w_out.wait()
     mix_two = mm_t(inc[...], w_out[...])
     put_rows(first, mix_two * gate_two.astype(F32), 3 * per, 4 * per)
-    packed[...] = first[...].astype(BF)
-    sends = [pltpu.make_async_copy(packed, packed_out, out_sems.at[0])]
-    sends[0].start()
+    packed_out[...] = first[...].astype(BF)
+    sends = []
     gate_two_kept[...] = gate_two
     got_conv.wait()
     part_two_kept[...] = (mix_two * conv[1].astype(F32)).astype(BF)
@@ -187,7 +185,7 @@
     for i, (source, target) in enumerate(
         [(gate_two_kept, gate_two_out), (part_two_kept, part_two_out), (later, later_out)]
     ):
-        send = pltpu.make_async_copy(source, target, out_sems.at[1 + i])
+        send = pltpu.make_async_copy(source, target, out_sems.at[i])
         send.start()
         sends.append(send)
     for send in sends:
@@ -306,12 +304,6 @@
             copy.wait()
 
 
-def known_body(per, data, outer_fwd, inner_fwd, turns, spec_out, known):
-    known[...] = data[...].astype(F32)
-    spec_out[0] = to_spectrum(signals(known, 0, per), outer_fwd, inner_fwd, turns)
-    spec_out[1] = to_spectrum(signals(known, 1, per), outer_fwd, inner_fwd, turns)
-
-
 def skip_rows(per, grads, others, out):
     size = out.shape[1]
     rows = out.shape[0] // size
@@ -338,12 +330,12 @@
     third,
     held_in,
     grad_in,
-    spec,
-    outer_fwd_in,
-    inner_fwd_in,
-    inner_inv_in,
-    outer_inv_in,
-    turns_in,
+    spec_in,
+    outer_fwd,
+    inner_fwd,
+    inner_inv,
+    outer_inv,
+    turns,
     packed,
     known,
     other,
@@ -351,36 +343,20 @@
     out,
     held,
     grad_held,
-    outer_fwd,
-    inner_fwd,
-    inner_inv,
-    outer_inv,
-    turns,
+    spec,
     sems,
 ):
     size = first.shape[1]
-    copies = fetch(
-        [
-            (outer_fwd_in, outer_fwd),
-            (turns_in, turns),
-            (inner_fwd_in, inner_fwd),
-            (held_in, held),
-            (inner_inv_in, inner_inv),
-            (outer_inv_in, outer_inv),
-            (grad_in, grad_held),
-        ],
-        sems,
-    )
+    copies = fetch([(held_in, held), (spec_in, spec), (grad_in, grad_held)], sems)
     fresh[...] = third[...].astype(F32)
     known[...] = first[...].astype(F32)
-    for copy in copies:
-        copy.wait()
 
     @pl.when(late[0] == 0)
     def _():
-        other[...] = second[...].astype(F32)
         grad_two = signals(fresh, 0, per)
         spec_two = to_spectrum(grad_two, outer_fwd, inner_fwd, turns)
+        for copy in copies:
+            copy.wait()
         mixed = from_spectrum(conj_times(held[1], spec_two), inner_inv, outer_inv, turns)
         send_rows(out, 3, from_spectrum(conj_times(spec[1], spec_two), inner_inv, outer_inv, turns))
         mix_one = [mixed[k] + gains[1, k] * grad_two[k] for k in range(per)]
@@ -391,6 +367,7 @@
         mixed = from_spectrum(conj_times(held[0], spec_one), inner_inv, outer_inv, turns)
         send_rows(out, 2, from_spectrum(conj_times(spec[0], spec_one), inner_inv, outer_inv, turns))
         send_rows(out, 0, [mixed[k] + gains[0, k] * grad_one[k] for k in range(per)])
+        other[...] = second[...].astype(F32)
         skip_rows(
             per, (grad_one, grad_two), (signals(other, 0, per), signals(other, 1, per)), out
         )
@@ -401,6 +378,8 @@
         values, gated = signals(fresh, 0, per), signals(fresh, 1, per)
         spec_one = to_spectrum(values, outer_fwd, inner_fwd, turns)
         spec_two = to_spectrum(gated, outer_fwd, inner_fwd, turns)
+        for copy in copies:
+            copy.wait()
         send_rows(out, 2, from_spectrum(conj_times(spec_one, held[0]), inner_inv, outer_inv, turns))
         send_rows(out, 3, from_spectrum(conj_times(spec_two, held[1]), inner_inv, outer_inv, turns))
         empty = [jnp.zeros((size, size), F32)] * per
@@ -418,7 +397,23 @@
 
 
 def hand_body(
-    per, late, data, conv, part_two_in, inc_in, w_in, result, scratch, part_two, inc, sems
+    per,
+    late,
+    data,
+    conv,
+    part_two_in,
+    inc_in,
+    w_in,
+    outer_fwd,
+    inner_fwd,
+    turns,
+    result,
+    spec_out,
+    scratch,
+    part_two,
+    inc,
+    spec,
+    sems,
 ):
     @pl.when(late[0] == 1)
     def _():
@@ -432,7 +427,15 @@
 
     @pl.when(late[0] == 0)
     def _():
+        scratch[...] = data[...].astype(F32)
+        copies = []
+        for s in range(2):
+            spec[s] = to_spectrum(signals(scratch, s, per), outer_fwd, inner_fwd, turns)
+            copies.append(pltpu.make_async_copy(spec.at[s], spec_out.at[s], sems.at[s]))
+            copies[s].start()
         result[...] = jnp.zeros_like(result)
+        for copy in copies:
+            copy.wait()
 
 
 def finish_body(
@@ -538,16 +541,16 @@
             pltpu.VMEM((tokens, channels), BF),
             rows(4 * per),
             rows(2 * per),
-            pltpu.VMEM(rows(4 * per), BF),
             pltpu.VMEM(rows(2 * per), BF),
             pltpu.VMEM((tokens, channels), BF),
             pltpu.VMEM((tokens, channels), BF),
             pltpu.SemaphoreType.DMA((6,)),
-            pltpu.SemaphoreType.DMA((4,)),
+            pltpu.SemaphoreType.DMA((3,)),
         ],
         layer_input[0], conv, filters[0], w_in, w_out, grad_output,
-        direct=range(6), direct_out=range(4),
-    )
+        direct=range(6), direct_out=range(1, 4),
+    )
+    packed, own, late = lax.optimization_barrier((packed, own, late))
     first = exchange(packed, parts)
     packed, held, grad_held = call(
         functools.partial(early_body, per),
@@ -559,15 +562,15 @@
         smem=2, direct=(3,), direct_out=(1, 2),
     )
     second = exchange(packed, parts)
-    (done,) = call(
+    done, spec = call(
         functools.partial(hand_body, per),
-        [token_rows],
+        [token_rows, spectra],
         [
             rows(2 * per), pltpu.VMEM((tokens, channels), BF), pltpu.VMEM((tokens, channels), BF),
-            pltpu.SemaphoreType.DMA((2,)),
-        ],
-        late, second, conv, part_two, grad_output, w_in,
-        smem=1, direct=(3, 4),
+            spectra[0], pltpu.SemaphoreType.DMA((2,)),
+        ],
+        late, second, conv, part_two, grad_output, w_in, outer_fwd, inner_fwd, turns,
+        smem=1, direct=(3, 4), direct_out=(1,),
     )
     handed = lax.ppermute(done, "section", [(1, 0)])
     packed, part_two, kept = call(
@@ -581,25 +584,18 @@
         smem=1, direct=(4, 6), direct_out=(1, 2),
     )
     third = exchange(packed, parts)
-    (spec,) = call(
-        functools.partial(known_body, per),
-        [spectra],
-        [rows(2 * per)],
-        second, outer_fwd, inner_fwd, turns,
-    )
     out_rows = 4 * per + 2
     (packed,) = call(
         functools.partial(late_body, per),
         [(rows(out_rows), BF)],
         [
             rows(4 * per), rows(2 * per), rows(2 * per), rows(out_rows), spectra[0], rows(per),
-            pltpu.VMEM(outer_fwd.shape, BF), pltpu.VMEM(inner_fwd.shape, BF),
-            pltpu.VMEM(inner_inv.shape, BF), pltpu.VMEM(outer_inv.shape, BF),
-            turns.shape, pltpu.SemaphoreType.DMA((7,)),
+            spectra[0],
+pltpu.SemaphoreType.DMA((3,)),
         ],
         late, own, first, second, third, held, grad_held, spec,
         outer_fwd, inner_fwd, inner_inv, outer_inv, turns,
-        smem=2, direct=(5, 6, 8, 9, 10, 11, 12),
+        smem=2, direct=range(5, 8),
     )
     back = exchange(packed, parts)
     grad_rows, filter_grads, skip_grads = call(

time: 124 us -> 123 us (level)
  blocking collectives: 46 us -> 102 us
  waiting for transfers between devices: 34 us -> 1.94 us
  starting transfers between devices: 24.5 us -> 1.29 us
    all_to_all x2 -> x4, blocking collectives: 46 us -> 102 us  [exchange(): lax.all_to_all(cut, 'seq', split_axis=0, concat_axis=0, tiled=True)]
    all_to_all x2 -> x0, waiting for transfers between devices: 32 us -> none  [exchange(): lax.all_to_all(cut, 'seq', split_axis=0, concat_axis=0, tiled=True)]
    all_to_all x2 -> x0, starting transfers between devices: 23.2 us -> none  [exchange(): lax.all_to_all(cut, 'seq', split_axis=0, concat_axis=0, tiled=True)]
    unnamed x29 -> x21, local copies, waits for them, and re-layouts: 2.02 us -> 0.15 us
    pallas_call x7 -> x6, Pallas kernels: 16 us -> 15.3 us  [call(): pl.pallas_call(body, out_shape=[(pltpu.HBM if i in direct_out else jax.Sh...]
  transfers between devices with their start and end apart: 3 -> 1, of which waited for: 3 -> 1; matrix products, arithmetic and copies ran while one was open for 0% -> 0% of each run, Pallas kernels for 1% -> 0%
where the time goes in v4:
time: 123 us
  blocking collectives  102 us (83%)
  Pallas kernels  15.3 us (12%)
  waiting for transfers between devices  1.94 us (2%)
  starting transfers between devices  1.29 us (1%)
    all_to_all x4, blocking collectives, exchange(): lax.all_to_all(cut, 'seq', split_axis=0, concat_axis=0, tiled=True)  102 us
    pallas_call x6, Pallas kernels, call(): pl.pallas_call(body, out_shape=[(pltpu.HBM if i in direct_out else jax.Sh...  15.3 us
  transfers between devices with their start and end apart: 1, of which 1 were waited for; matrix products, arithmetic and copies ran while one was open for 0% of the time, Pallas kernels for 0%

profile of v4, /device:TPU:8, one launch (start us, length us, event | category | flops | bytes accessed | tf_op | source)
XLA Modules:
  0.0 122.7 jit_solution(16176787555589123114)
XLA Ops:
  0.6 0.7 reshape_squeeze.3
  1.3 0.1 constant_dynamic-slice_fusion
  1.4 0.1 copy.19
  1.5 0.0 copy-start.4
  1.5 0.0 copy-start.5
  1.5 0.0 copy-start.6
  1.5 0.0 copy-start.7
  1.5 3.5 %shard_map.139 = (bf16[2048,128]{1,0:T(8,128)(2,1)S(1)}, bf16[1024,128]{1,0:T(8,128)(2,1)}, bf16[128,512]{1,0:T(8,128)(2,1)}, bf16[128,512]{1,0:T(8,128)(2,1)}) custom-call(bf16[128,512]{1,0:T(8,128)(2,1)} %bitcast.44, bf16[2,128,512]{2,1,0:T(8,128)(2,1)} %bitcast.27, bf16[2,128,512]{2,1,0:T(8,128)(2,1)} %bitcast.43, bf16[512,1536]{1,0:T(8,128)(2,1)} %bitcast.22, ...), custom_call_target="tpu_custom_call" | custom-call | tf_op jit(solution)/shard_map/pallas_call | solution.py:485
  5.1 0.0 copy-start
  5.1 0.0 copy-start.1
  5.1 35.4 %all_to_all.20 = bf16[128,2,8,128]{3,2,1,0:T(8,128)(2,1)S(1)} all-to-all(bf16[128,2,8,128]{3,2,1,0:T(8,128)(2,1)S(1)} %bitcast.38), channel_id=1, replica_groups=mesh['seq'=128,'section'=2] {'seq'}, dimensions={0} | all-to-all | bytes 1048576 | tf_op jit(solution)/shard_map/all_to_all | solution.py:512
  40.5 0.0 copy-done.2
  40.5 0.0 copy-done.4
  40.5 0.0 copy-done.5
  40.5 0.0 copy-done.6
  40.5 0.0 copy-done.7
  40.5 2.6 %shard_map.140 = (bf16[1024,128]{1,0:T(8,128)(2,1)S(1)}, f32[2,512,256]{2,1,0:T(8,128)}, f32[512,128]{1,0:T(8,128)}) custom-call(s32[1]{0:T(128)} %bitcast.6.late, f32[2,4]{1,0:T(2,128)S(1)} %bitcast.41, bf16[2048,128]{1,0:T(8,128)(2,1)S(1)} %bitcast.25, bf16[1024,128]{1,0:T(8,128)(2,1)} %get-tuple-element.25.later, bf16[256,256]{1,0:T(8,128)(2,1)S(1)} %copy-done.5, ...), custom_call_target="tpu_custom_call" | custom-call | tf_op jit(solution)/shard_map/pallas_call | solution.py:485
  43.1 20.7 %all_to_all.21 = bf16[128,1,8,128]{3,2,1,0:T(8,128)(2,1)S(1)} all-to-all(bf16[128,1,8,128]{3,2,1,0:T(8,128)(2,1)S(1)} %bitcast.40), channel_id=1, replica_groups=mesh['seq'=128,'section'=2] {'seq'}, dimensions={0} | all-to-all | bytes 524288 | tf_op jit(solution)/shard_map/all_to_all | solution.py:512
  63.8 0.0 copy-start.3
  63.8 0.0 copy-done
  63.8 0.0 copy-done.1
  63.8 1.7 %shard_map.141 = (bf16[128,512]{1,0:T(8,128)(2,1)S(1)}, f32[2,512,256]{2,1,0:T(8,128)}) custom-call(s32[1]{0:T(128)} %bitcast.6.late, bf16[1024,128]{1,0:T(8,128)(2,1)S(1)} %bitcast.31, bf16[2,128,512]{2,1,0:T(8,128)(2,1)S(1)} %bitcast.28, bf16[128,512]{1,0:T(8,128)(2,1)} %get-tuple-element.27.part_two_in, bf16[128,512]{1,0:T(8,128)(2,1)} %inc_in.3, ...), custom_call_target="tpu_custom_call" | custom-call | tf_op jit(solution)/shard_map/pallas_call | solution.py:485
  65.6 1.3 %collective-permute-start = (bf16[128,512]{1,0:T(8,128)(2,1)S(1)}, bf16[128,512]{1,0:T(8,128)(2,1)S(1)}, u32[]{:S(2)}, u32[]{:S(2)}) collective-permute-start(bf16[128,512]{1,0:T(8,128)(2,1)S(1)} %get-tuple-element.28.done), channel_id=1, source_target_pairs={{1,0},{3,2},{5,4},{7,6},{9,8},{11,10},{13,12},{15,14},{17,16},{19,... | collective-permute-start | bytes 393224 | tf_op jit(solution)/shard_map/ppermute | solution.py:575
  66.9 1.9 %collective-permute-done.inc = bf16[128,512]{1,0:T(8,128)(2,1)S(1)} collective-permute-done((bf16[128,512]{1,0:T(8,128)(2,1)S(1)}, bf16[128,512]{1,0:T(8,128)(2,1)S(1)}, u32[]{:S(2)}, u32[]{:S(2)}) %collective-permute-start) | collective-permute-done | bytes 131104 | tf_op jit(solution)/shard_map/ppermute | solution.py:575
  68.8 0.0 copy-done.3
  68.8 1.2 %shard_map.142 = (bf16[1024,128]{1,0:T(8,128)(2,1)S(1)}, bf16[128,512]{1,0:T(8,128)(2,1)}, bf16[128,512]{1,0:T(8,128)(2,1)}) custom-call(s32[1]{0:T(128)} %bitcast.6.late, bf16[128,512]{1,0:T(8,128)(2,1)S(1)} %collective-permute-done.inc, bf16[128,512]{1,0:T(8,128)(2,1)S(1)} %get-tuple-element.28.done, bf16[512,512]{1,0:T(8,128)(2,1)S(1)} %bitcast.36, ...), custom_call_target="tpu_custom_call" | custom-call | tf_op jit(solution)/shard_map/pallas_call | solution.py:485
  70.1 21.1 %all_to_all.22 = bf16[128,1,8,128]{3,2,1,0:T(8,128)(2,1)S(1)} all-to-all(bf16[128,1,8,128]{3,2,1,0:T(8,128)(2,1)S(1)} %bitcast.39), channel_id=1, replica_groups=mesh['seq'=128,'section'=2] {'seq'}, dimensions={0} | all-to-all | bytes 524288 | tf_op jit(solution)/shard_map/all_to_all | solution.py:512
  91.2 4.6 %shard_map.143 = bf16[2304,128]{1,0:T(8,128)(2,1)S(1)} custom-call(s32[1]{0:T(128)} %bitcast.6.late, f32[2,4]{1,0:T(2,128)S(1)} %bitcast.42, bf16[2048,128]{1,0:T(8,128)(2,1)S(1)} %bitcast.26, bf16[1024,128]{1,0:T(8,128)(2,1)S(1)} %bitcast.32, bf16[1024,128]{1,0:T(8,128)(2,1)S(1)} %bitcast.37, f32[2,512,256]{2,1,0:T(8,128)} %get-tuple-element.31.held_in, ...), custom_call_target="tpu_custom_call" | custom-call | tf_op jit(solution)/shard_map/pallas_call | solution.py:485
  95.8 25.2 %all_to_all.23 = bf16[128,9,2,128]{3,2,1,0:T(2,128)(2,1)S(1)} all-to-all(bf16[128,9,2,128]{3,2,1,0:T(2,128)(2,1)S(1)} %bitcast.33), channel_id=1, replica_groups=mesh['seq'=128,'section'=2] {'seq'}, dimensions={0} | all-to-all | bytes 1179648 | tf_op jit(solution)/shard_map/all_to_all | solution.py:512
  121.0 0.0 copy-done.8
  121.0 0.0 copy-done.9
  121.0 1.6 %shard_map.144 = (bf16[128,512]{1,0:T(8,128)(2,1)}, bf16[2,128,512]{2,1,0:T(8,128)(2,1)}, f32[2,512]{1,0:T(2,128)}) custom-call(s32[1]{0:T(128)} %bitcast.6.late, bf16[2304,128]{1,0:T(8,128)(2,1)S(1)} %bitcast.34, bf16[2,128,512]{2,1,0:T(8,128)(2,1)S(1)} %bitcast.30, bf16[128,512]{1,0:T(8,128)(2,1)S(1)} %copy-done.8, bf16[128,512]{1,0:T(8,128)(2,1)S(1)} %copy-done.9, ...), custom_call_target="tpu_custom_call" | custom-call | tf_op jit(solution)/shard_map/pallas_call | solution.py:485
  (3 shorter events, 0.0 us)
Async XLA Ops:
  1.5 39.0 %copy-start.2 = (bf16[512,256]{1,0:T(8,128)(2,1)S(1)}, bf16[512,256]{1,0:T(8,128)(2,1)}, u32[]{:S(2)}) copy-start(bf16[512,256]{1,0:T(8,128)(2,1)} %constant.23.clone.inner_fwd) | copy-start | bytes 786436
  1.5 39.0 %copy-start.4 = (f32[2,128,128]{2,1,0:T(8,128)S(1)}, f32[2,128,128]{2,1,0:T(8,128)}, u32[]{:S(2)}) copy-start(f32[2,128,128]{2,1,0:T(8,128)} %constant.26.clone.turns) | copy-start | bytes 393220
  1.5 39.0 %copy-start.5 = (bf16[256,256]{1,0:T(8,128)(2,1)S(1)}, bf16[256,256]{1,0:T(8,128)(2,1)}, u32[]{:S(2)}) copy-start(bf16[256,256]{1,0:T(8,128)(2,1)} %constant.22.clone.outer_fwd) | copy-start | bytes 393220
  1.5 39.0 %copy-start.6 = (bf16[512,256]{1,0:T(8,128)(2,1)S(1)}, bf16[512,256]{1,0:T(8,128)(2,1)}, u32[]{:S(2)}) copy-start(bf16[512,256]{1,0:T(8,128)(2,1)} %constant.24.clone.inner_inv) | copy-start | bytes 786436
  1.5 39.0 %copy-start.7 = (bf16[128,512]{1,0:T(8,128)(2,1)S(1)}, bf16[128,512]{1,0:T(8,128)(2,1)}, u32[]{:S(2)}) copy-start(bf16[128,512]{1,0:T(8,128)(2,1)} %constant.25.clone.outer_inv) | copy-start | bytes 393220
  5.1 58.8 %copy-start = (bf16[1,512,1536]{2,1,0:T(8,128)(2,1)S(1)}, bf16[1,512,1536]{2,1,0:T(8,128)(2,1)}, u32[]{:S(2)}) copy-start(bf16[1,512,1536]{2,1,0:T(8,128)(2,1)} %param.16) | copy-start | bytes 4718596
  5.1 58.7 %copy-start.1 = (bf16[1,2,128,512]{3,2,1,0:T(8,128)(2,1)S(1)}, bf16[1,2,128,512]{3,2,1,0:T(8,128)(2,1)}, u32[]{:S(2)}) copy-start(bf16[1,2,128,512]{3,2,1,0:T(8,128)(2,1)} %param.13) | copy-start | bytes 786436
  63.8 5.0 %copy-start.3 = (bf16[1,512,512]{2,1,0:T(8,128)(2,1)S(1)}, bf16[1,512,512]{2,1,0:T(8,128)(2,1)}, u32[]{:S(2)}) copy-start(bf16[1,512,512]{2,1,0:T(8,128)(2,1)} %param.17) | copy-start | bytes 1572868
  65.6 3.2 %collective-permute-start = (bf16[128,512]{1,0:T(8,128)(2,1)S(1)}, bf16[128,512]{1,0:T(8,128)(2,1)S(1)}, u32[]{:S(2)}, u32[]{:S(2)}) collective-permute-start(bf16[128,512]{1,0:T(8,128)(2,1)S(1)} %get-tuple-element.28.done), channel_id=1, source_target_pairs={{1,0},{3,2},{5,4},{7,6},{9,8},{11,10},{13,12},{15,14},{17,16},{19,... | collective-permute-start | bytes 393224 | tf_op jit(solution)/shard_map/ppermute | solution.py:575
  91.1 29.9 %copy-start.8 = (bf16[128,512]{1,0:T(8,128)(2,1)S(1)}, bf16[128,512]{1,0:T(8,128)(2,1)}, u32[]{:S(2)}) copy-start(bf16[128,512]{1,0:T(8,128)(2,1)} %get-tuple-element.34.part_two) | copy-start | bytes 393220
  91.2 29.9 %copy-start.9 = (bf16[128,512]{1,0:T(8,128)(2,1)S(1)}, bf16[128,512]{1,0:T(8,128)(2,1)}, u32[]{:S(2)}) copy-start(bf16[128,512]{1,0:T(8,128)(2,1)} %get-tuple-element.35.inc) | copy-start | bytes 393220

commit v5 on v4

--- a/solution.py
+++ b/solution.py
@@ -102,14 +102,15 @@
 def put_rows(scratch, value, first, stride):
     size = value.shape[0]
     for k in range(value.shape[1] // size):
-        block = value[:, k * size : (k + 1) * size].astype(F32).T
-        scratch[pl.ds(first + k, size, stride=stride), :] = block
+        block = value[:, k * size : (k + 1) * size].astype(BF).T
+        scratch[pl.ds(first + k, size, stride=stride), :] = block.astype(F32)
 
 
 def get_rows(scratch, first, stride, count):
     size = scratch.shape[1]
     return jnp.concatenate(
-        [scratch[pl.ds(first + k, size, stride=stride), :].T for k in range(count)], axis=1
+        [scratch[pl.ds(first + k, size, stride=stride), :].astype(BF).T for k in range(count)],
+        axis=1,
     )
 
 
@@ -250,6 +251,7 @@
 def early_body(
     per,
     late,
+    place,
     gains,
     data,
     later,
@@ -277,7 +279,7 @@
         spec_two = to_spectrum(grad_two, outer_fwd, inner_fwd, turns)
         spec[1] = spec_two
         mixed = from_spectrum(conj_times(filt_two, spec_two), inner_inv, outer_inv, turns)
-        mix_one = [mixed[k] + gains[1, k] * grad_two[k] for k in range(per)]
+        mix_one = [mixed[k] + gains[1, k * size + place[0]] * grad_two[k] for k in range(per)]
         send_rows(out, 1, mix_one)
         gate_one = signals(known, 2, per)
         grad_one = [mix_one[k] * gate_one[k] for k in range(per)]
@@ -288,7 +290,7 @@
         spec[0] = spec_one
         copies = fetch([(spec, spec_out), (grad, grad_out)], sems)
         mixed = from_spectrum(conj_times(filt_one, spec_one), inner_inv, outer_inv, turns)
-        send_rows(out, 0, [mixed[k] + gains[0, k] * grad_one[k] for k in range(per)])
+        send_rows(out, 0, [mixed[k] + gains[0, k * size + place[0]] * grad_one[k] for k in range(per)])
         packed[...] = out[...].astype(BF)
         for copy in copies:
             copy.wait()
@@ -324,6 +326,7 @@
 def late_body(
     per,
     late,
+    place,
     gains,
     first,
     second,
@@ -359,14 +362,14 @@
             copy.wait()
         mixed = from_spectrum(conj_times(held[1], spec_two), inner_inv, outer_inv, turns)
         send_rows(out, 3, from_spectrum(conj_times(spec[1], spec_two), inner_inv, outer_inv, turns))
-        mix_one = [mixed[k] + gains[1, k] * grad_two[k] for k in range(per)]
+        mix_one = [mixed[k] + gains[1, k * size + place[0]] * grad_two[k] for k in range(per)]
         send_rows(out, 1, mix_one)
         gate_one = signals(known, 2, per)
         grad_one = [mix_one[k] * gate_one[k] for k in range(per)]
         spec_one = to_spectrum(grad_one, outer_fwd, inner_fwd, turns)
         mixed = from_spectrum(conj_times(held[0], spec_one), inner_inv, outer_inv, turns)
         send_rows(out, 2, from_spectrum(conj_times(spec[0], spec_one), inner_inv, outer_inv, turns))
-        send_rows(out, 0, [mixed[k] + gains[0, k] * grad_one[k] for k in range(per)])
+        send_rows(out, 0, [mixed[k] + gains[0, k * size + place[0]] * grad_one[k] for k in range(per)])
         other[...] = second[...].astype(F32)
         skip_rows(
             per, (grad_one, grad_two), (signals(other, 0, per), signals(other, 1, per)), out
@@ -391,7 +394,7 @@
 
 
 def input_grad(inc, values, mix_one, conv_one, part_two, w_in):
-    gate_one = mix_one * conv_one.astype(F32)
+    gate_one = mix_one.astype(F32) * conv_one.astype(F32)
     proj = jnp.concatenate([values.astype(BF), gate_one.astype(BF), part_two], axis=1)
     return (inc.astype(F32) + mm_t(proj, w_in)).astype(BF)
 
@@ -466,8 +469,8 @@
     def _():
         result[...] = inc[...]
 
-    filt_grads[0] = (get_rows(scratch, 2 * per, stride, per) * rescale).astype(BF)
-    filt_grads[1] = (get_rows(scratch, 3 * per, stride, per) * rescale).astype(BF)
+    filt_grads[0] = (get_rows(scratch, 2 * per, stride, per).astype(F32) * rescale).astype(BF)
+    filt_grads[1] = (get_rows(scratch, 3 * per, stride, per).astype(F32) * rescale).astype(BF)
     sums = scratch[pl.ds(4 * per, size, stride=stride), :].T
     sums = (sums[: 2 * per] + sums[2 * per : 4 * per]) * rescale
     for w in range(2):
@@ -507,7 +510,7 @@
 
 def exchange(rows, parts):
     per_part = rows.shape[0] // parts
-    tile = math.gcd(per_part, 8)
+    tile = math.gcd(per_part, 2)
     cut = rows.reshape(parts, per_part // tile, tile, rows.shape[1])
     return lax.all_to_all(cut, "seq", split_axis=0, concat_axis=0, tiled=True).reshape(rows.shape)
 
@@ -519,9 +522,7 @@
     w_in, w_out, conv = weight_in[0], weight_out[0], conv_out[0]
     outer_fwd, inner_fwd, inner_inv, outer_inv, turns = transform_tables(parts, tokens)
     late = lax.axis_index("section").astype(jnp.int32).reshape(1)
-    own = lax.dynamic_slice_in_dim(
-        skip_gain[0].reshape(2, per, parts), lax.axis_index("seq"), 1, axis=2
-    )[:, :, 0]
+    place = lax.axis_index("seq").astype(jnp.int32).reshape(1)
 
     def rows(count):
         return (parts * count, tokens)
@@ -550,7 +551,7 @@
         layer_input[0], conv, filters[0], w_in, w_out, grad_output,
         direct=range(6), direct_out=range(1, 4),
     )
-    packed, own, late = lax.optimization_barrier((packed, own, late))
+    packed, late, place = lax.optimization_barrier((packed, late, place))
     first = exchange(packed, parts)
     packed, held, grad_held = call(
         functools.partial(early_body, per),
@@ -558,8 +559,8 @@
         [
             rows(4 * per), rows(2 * per), spectra[0], rows(per), pltpu.SemaphoreType.DMA((3,)),
         ],
-        late, own, first, later, outer_fwd, inner_fwd, inner_inv, outer_inv, turns,
-        smem=2, direct=(3,), direct_out=(1, 2),
+        late, place, skip_gain[0], first, later, outer_fwd, inner_fwd, inner_inv, outer_inv, turns,
+        smem=3, direct=(4,), direct_out=(1, 2),
     )
     second = exchange(packed, parts)
     done, spec = call(
@@ -572,7 +573,7 @@
         late, second, conv, part_two, grad_output, w_in, outer_fwd, inner_fwd, turns,
         smem=1, direct=(3, 4), direct_out=(1,),
     )
-    handed = lax.ppermute(done, "section", [(1, 0)])
+    handed = lax.ppermute(done, "section", [(0, 1), (1, 0)])
     packed, part_two, kept = call(
         regrad_body,
         [(rows(2 * per), BF), token_rows, token_rows],
@@ -593,9 +594,9 @@
             spectra[0],
 pltpu.SemaphoreType.DMA((3,)),
         ],
-        late, own, first, second, third, held, grad_held, spec,
+        late, place, skip_gain[0], first, second, third, held, grad_held, spec,
         outer_fwd, inner_fwd, inner_inv, outer_inv, turns,
-        smem=2, direct=range(5, 8),
+        smem=3, direct=range(6, 9),
     )
     back = exchange(packed, parts)
     grad_rows, filter_grads, skip_grads = call(

time: 123 us -> 120 us (0.976)
  no operation moved by 1% of the time
where the time goes in v5:
time: 120 us
  blocking collectives  102 us (85%)
  Pallas kernels  15.3 us (13%)
  waiting for transfers between devices  1.33 us (1%)
    all_to_all x4, blocking collectives, exchange(): lax.all_to_all(cut, 'seq', split_axis=0, concat_axis=0, tiled=True)  102 us
    pallas_call x6, Pallas kernels, call(): pl.pallas_call(body, out_shape=[(pltpu.HBM if i in direct_out else jax.Sh...  15.3 us
  transfers between devices with their start and end apart: 1, of which 1 were waited for; matrix products, arithmetic and copies ran while one was open for 0% of the time, Pallas kernels for 0%

profile of v5, /device:TPU:8, one launch (start us, length us, event | category | flops | bytes accessed | tf_op | source)
XLA Modules:
  0.0 120.1 jit_solution(3022734563046700381)
XLA Ops:
  0.6 0.0 copy-start.2
  0.6 0.0 copy-start.4
  0.7 0.0 copy-start.5
  0.7 0.0 copy-start.6
  0.7 0.0 copy-start.7
  0.7 0.0 copy-start.10
  0.7 3.5 %shard_map.139 = (bf16[2048,128]{1,0:T(8,128)(2,1)S(1)}, bf16[1024,128]{1,0:T(8,128)(2,1)}, bf16[128,512]{1,0:T(8,128)(2,1)}, bf16[128,512]{1,0:T(8,128)(2,1)}) custom-call(bf16[128,512]{1,0:T(8,128)(2,1)} %bitcast.41, bf16[2,128,512]{2,1,0:T(8,128)(2,1)} %bitcast.24, bf16[2,128,512]{2,1,0:T(8,128)(2,1)} %bitcast.40, bf16[512,1536]{1,0:T(8,128)(2,1)} %bitcast.19, ...), custom_call_target="tpu_custom_call" | custom-call | tf_op jit(solution)/shard_map/pallas_call | solution.py:488
  4.2 0.0 copy-start
  4.3 0.0 copy-start.1
  4.3 35.4 %all_to_all.20 = bf16[128,8,2,128]{3,2,1,0:T(2,128)(2,1)S(1)} all-to-all(bf16[128,8,2,128]{3,2,1,0:T(2,128)(2,1)S(1)} %bitcast.35), channel_id=1, replica_groups=mesh['seq'=128,'section'=2] {'seq'}, dimensions={0} | all-to-all | bytes 1048576 | tf_op jit(solution)/shard_map/all_to_all | solution.py:515
  39.6 0.0 copy-done.2
  39.6 0.0 copy-done.4
  39.6 0.0 copy-done.5
  39.7 0.0 copy-done.6
  39.7 0.0 copy-done.7
  39.7 0.0 copy-done.10
  39.7 2.6 %shard_map.140 = (bf16[1024,128]{1,0:T(8,128)(2,1)S(1)}, f32[2,512,256]{2,1,0:T(8,128)}, f32[512,128]{1,0:T(8,128)}) custom-call(s32[1]{0:T(128)} %bitcast.5.late, s32[1]{0:T(128)} %bitcast.6.place, f32[2,512]{1,0:T(2,128)S(1)} %bitcast.38, bf16[2048,128]{1,0:T(8,128)(2,1)S(1)} %bitcast.22, bf16[1024,128]{1,0:T(8,128)(2,1)} %get-tuple-element.25.later, ...), custom_call_target="tpu_custom_call" | custom-call | tf_op jit(solution)/shard_map/pallas_call | solution.py:488
  42.3 20.7 %all_to_all.21 = bf16[128,4,2,128]{3,2,1,0:T(2,128)(2,1)S(1)} all-to-all(bf16[128,4,2,128]{3,2,1,0:T(2,128)(2,1)S(1)} %bitcast.37), channel_id=1, replica_groups=mesh['seq'=128,'section'=2] {'seq'}, dimensions={0} | all-to-all | bytes 524288 | tf_op jit(solution)/shard_map/all_to_all | solution.py:515
  63.0 0.0 copy-start.3
  63.0 0.0 copy-done
  63.0 0.0 copy-done.1
  63.0 1.7 %shard_map.141 = (bf16[128,512]{1,0:T(8,128)(2,1)S(1)}, f32[2,512,256]{2,1,0:T(8,128)}) custom-call(s32[1]{0:T(128)} %bitcast.5.late, bf16[1024,128]{1,0:T(8,128)(2,1)S(1)} %bitcast.29, bf16[2,128,512]{2,1,0:T(8,128)(2,1)S(1)} %bitcast.25, bf16[128,512]{1,0:T(8,128)(2,1)} %get-tuple-element.27.part_two_in, bf16[128,512]{1,0:T(8,128)(2,1)} %inc_in.3, ...), custom_call_target="tpu_custom_call" | custom-call | tf_op jit(solution)/shard_map/pallas_call | solution.py:488
  64.8 0.1 collective-permute-start
  64.9 1.3 %collective-permute-done.inc = bf16[128,512]{1,0:T(8,128)(2,1)S(1)} collective-permute-done((bf16[128,512]{1,0:T(8,128)(2,1)S(1)}, bf16[128,512]{1,0:T(8,128)(2,1)S(1)}, u32[]{:S(2)}, u32[]{:S(2)}) %collective-permute-start) | collective-permute-done | bytes 131104 | tf_op jit(solution)/shard_map/ppermute | solution.py:576
  66.2 0.0 copy-done.3
  66.2 1.2 %shard_map.142 = (bf16[1024,128]{1,0:T(8,128)(2,1)S(1)}, bf16[128,512]{1,0:T(8,128)(2,1)}, bf16[128,512]{1,0:T(8,128)(2,1)}) custom-call(s32[1]{0:T(128)} %bitcast.5.late, bf16[128,512]{1,0:T(8,128)(2,1)S(1)} %collective-permute-done.inc, bf16[128,512]{1,0:T(8,128)(2,1)S(1)} %get-tuple-element.28.done, bf16[512,512]{1,0:T(8,128)(2,1)S(1)} %bitcast.33, ...), custom_call_target="tpu_custom_call" | custom-call | tf_op jit(solution)/shard_map/pallas_call | solution.py:488
  67.5 21.1 %all_to_all.22 = bf16[128,4,2,128]{3,2,1,0:T(2,128)(2,1)S(1)} all-to-all(bf16[128,4,2,128]{3,2,1,0:T(2,128)(2,1)S(1)} %bitcast.36), channel_id=1, replica_groups=mesh['seq'=128,'section'=2] {'seq'}, dimensions={0} | all-to-all | bytes 524288 | tf_op jit(solution)/shard_map/all_to_all | solution.py:515
  88.6 4.7 %shard_map.143 = bf16[2304,128]{1,0:T(8,128)(2,1)S(1)} custom-call(s32[1]{0:T(128)} %bitcast.5.late, s32[1]{0:T(128)} %bitcast.6.place, f32[2,512]{1,0:T(2,128)S(1)} %bitcast.39, bf16[2048,128]{1,0:T(8,128)(2,1)S(1)} %bitcast.23, bf16[1024,128]{1,0:T(8,128)(2,1)S(1)} %bitcast.30, bf16[1024,128]{1,0:T(8,128)(2,1)S(1)} %bitcast.34, ...), custom_call_target="tpu_custom_call" | custom-call | tf_op jit(solution)/shard_map/pallas_call | solution.py:488
  93.3 25.2 %all_to_all.23 = bf16[128,9,2,128]{3,2,1,0:T(2,128)(2,1)S(1)} all-to-all(bf16[128,9,2,128]{3,2,1,0:T(2,128)(2,1)S(1)} %bitcast.28), channel_id=1, replica_groups=mesh['seq'=128,'section'=2] {'seq'}, dimensions={0} | all-to-all | bytes 1179648 | tf_op jit(solution)/shard_map/all_to_all | solution.py:515
  118.5 0.0 copy-done.8
  118.5 0.0 copy-done.9
  118.5 1.5 %shard_map.144 = (bf16[128,512]{1,0:T(8,128)(2,1)}, bf16[2,128,512]{2,1,0:T(8,128)(2,1)}, f32[2,512]{1,0:T(2,128)}) custom-call(s32[1]{0:T(128)} %bitcast.5.late, bf16[2304,128]{1,0:T(8,128)(2,1)S(1)} %bitcast.31, bf16[2,128,512]{2,1,0:T(8,128)(2,1)S(1)} %bitcast.27, bf16[128,512]{1,0:T(8,128)(2,1)S(1)} %copy-done.8, bf16[128,512]{1,0:T(8,128)(2,1)S(1)} %copy-done.9, ...), custom_call_target="tpu_custom_call" | custom-call | tf_op jit(solution)/shard_map/pallas_call | solution.py:488
  (2 shorter events, 0.0 us)
Async XLA Ops:
  0.6 39.0 %copy-start.2 = (bf16[512,256]{1,0:T(8,128)(2,1)S(1)}, bf16[512,256]{1,0:T(8,128)(2,1)}, u32[]{:S(2)}) copy-start(bf16[512,256]{1,0:T(8,128)(2,1)} %constant.19.clone.inner_fwd) | copy-start | bytes 786436
  0.6 39.0 %copy-start.4 = (f32[2,128,128]{2,1,0:T(8,128)S(1)}, f32[2,128,128]{2,1,0:T(8,128)}, u32[]{:S(2)}) copy-start(f32[2,128,128]{2,1,0:T(8,128)} %constant.22.clone.turns) | copy-start | bytes 393220
  0.7 39.0 %copy-start.5 = (bf16[256,256]{1,0:T(8,128)(2,1)S(1)}, bf16[256,256]{1,0:T(8,128)(2,1)}, u32[]{:S(2)}) copy-start(bf16[256,256]{1,0:T(8,128)(2,1)} %constant.18.clone.outer_fwd) | copy-start | bytes 393220
  0.7 39.0 %copy-start.6 = (bf16[512,256]{1,0:T(8,128)(2,1)S(1)}, bf16[512,256]{1,0:T(8,128)(2,1)}, u32[]{:S(2)}) copy-start(bf16[512,256]{1,0:T(8,128)(2,1)} %constant.20.clone.inner_inv) | copy-start | bytes 786436
  0.7 39.0 %copy-start.7 = (bf16[128,512]{1,0:T(8,128)(2,1)S(1)}, bf16[128,512]{1,0:T(8,128)(2,1)}, u32[]{:S(2)}) copy-start(bf16[128,512]{1,0:T(8,128)(2,1)} %constant.21.clone.outer_inv) | copy-start | bytes 393220
  0.7 39.0 %copy-start.10 = (f32[1,2,512]{2,1,0:T(2,128)S(1)}, f32[1,2,512]{2,1,0:T(2,128)}, u32[]{:S(2)}) copy-start(f32[1,2,512]{2,1,0:T(2,128)} %param.15) | copy-start | bytes 12292
  4.2 58.8 %copy-start = (bf16[1,512,1536]{2,1,0:T(8,128)(2,1)S(1)}, bf16[1,512,1536]{2,1,0:T(8,128)(2,1)}, u32[]{:S(2)}) copy-start(bf16[1,512,1536]{2,1,0:T(8,128)(2,1)} %param.16) | copy-start | bytes 4718596
  4.3 58.8 %copy-start.1 = (bf16[1,2,128,512]{3,2,1,0:T(8,128)(2,1)S(1)}, bf16[1,2,128,512]{3,2,1,0:T(8,128)(2,1)}, u32[]{:S(2)}) copy-start(bf16[1,2,128,512]{3,2,1,0:T(8,128)(2,1)} %param.13) | copy-start | bytes 786436
  63.0 3.2 %copy-start.3 = (bf16[1,512,512]{2,1,0:T(8,128)(2,1)S(1)}, bf16[1,512,512]{2,1,0:T(8,128)(2,1)}, u32[]{:S(2)}) copy-start(bf16[1,512,512]{2,1,0:T(8,128)(2,1)} %param.17) | copy-start | bytes 1572868
  64.8 1.4 %collective-permute-start = (bf16[128,512]{1,0:T(8,128)(2,1)S(1)}, bf16[128,512]{1,0:T(8,128)(2,1)S(1)}, u32[]{:S(2)}, u32[]{:S(2)}) collective-permute-start(bf16[128,512]{1,0:T(8,128)(2,1)S(1)} %get-tuple-element.28.done), channel_id=1, source_target_pairs={{0,1},{1,0},{2,3},{3,2},{4,5},{5,4},{6,7},{7,6},{8,9},{9,8},{10,11... | collective-permute-start | bytes 393224 | tf_op jit(solution)/shard_map/ppermute | solution.py:576
  88.6 30.0 %copy-start.8 = (bf16[128,512]{1,0:T(8,128)(2,1)S(1)}, bf16[128,512]{1,0:T(8,128)(2,1)}, u32[]{:S(2)}) copy-start(bf16[128,512]{1,0:T(8,128)(2,1)} %get-tuple-element.34.part_two) | copy-start | bytes 393220
  88.6 30.0 %copy-start.9 = (bf16[128,512]{1,0:T(8,128)(2,1)S(1)}, bf16[128,512]{1,0:T(8,128)(2,1)}, u32[]{:S(2)}) copy-start(bf16[128,512]{1,0:T(8,128)(2,1)} %get-tuple-element.35.inc) | copy-start | bytes 393220

commit v6 on v5

--- a/solution.py
+++ b/solution.py
@@ -143,11 +143,7 @@
     inc,
     first,
     second,
-    later,
-    gate_two_kept,
-    part_two_kept,
     sems,
-    out_sems,
 ):
     channels = rows.shape[1]
     per = channels // rows.shape[0]
@@ -176,63 +172,33 @@
     mix_two = mm_t(inc[...], w_out[...])
     put_rows(first, mix_two * gate_two.astype(F32), 3 * per, 4 * per)
     packed_out[...] = first[...].astype(BF)
-    sends = []
-    gate_two_kept[...] = gate_two
+    gate_two_out[...] = gate_two
     got_conv.wait()
-    part_two_kept[...] = (mix_two * conv[1].astype(F32)).astype(BF)
+    part_two_out[...] = (mix_two * conv[1].astype(F32)).astype(BF)
     put_rows(second, projected[:, :channels], 0, 2 * per)
     put_rows(second, gate_one.astype(F32) * conv[0].astype(F32), per, 2 * per)
-    later[...] = second[...].astype(BF)
-    for i, (source, target) in enumerate(
-        [(gate_two_kept, gate_two_out), (part_two_kept, part_two_out), (later, later_out)]
-    ):
-        send = pltpu.make_async_copy(source, target, out_sems.at[i])
-        send.start()
-        sends.append(send)
-    for send in sends:
-        send.wait()
-
-
-def regrad_body(
-    late,
-    inc,
-    done,
-    w_out,
-    gate_two_in,
-    conv,
-    later,
-    packed,
-    part_two_out,
-    kept_out,
-    part_two,
-    gate_two,
-    scratch,
-    sems,
-):
-    per = inc.shape[1] // inc.shape[0]
+    later_out[...] = second[...].astype(BF)
+
+
+def regrad_body(late, inc, done, w_out, gate_two, conv, later, packed, part_two, kept, scratch):
+    size = inc.shape[0]
+    per = inc.shape[1] // size
 
     @pl.when(late[0] == 0)
     def _():
-        gate, keep = fetch([(gate_two_in, gate_two), (inc, kept_out)], sems)
+        kept[...] = inc[...]
         mix_two = mm_t(inc[...], w_out[...])
         part_two[...] = (mix_two * conv[1].astype(F32)).astype(BF)
-        part = pltpu.make_async_copy(part_two, part_two_out, sems.at[2])
-        part.start()
-        gate.wait()
         put_rows(scratch, mix_two * gate_two[...].astype(F32), 0, 2 * per)
         for k in range(per):
-            empty = jnp.zeros((inc.shape[0], inc.shape[0]), F32)
-            scratch[pl.ds(per + k, inc.shape[0], stride=2 * per), :] = empty
+            scratch[pl.ds(per + k, size, stride=2 * per), :] = jnp.zeros((size, size), F32)
         packed[...] = scratch[...].astype(BF)
-        keep.wait()
-        part.wait()
 
     @pl.when(late[0] == 1)
     def _():
+        kept[...] = done[...]
         part_two[...] = jnp.zeros_like(part_two)
-        copies = fetch([(done, kept_out), (part_two, part_two_out), (later, packed)], sems)
-        for copy in copies:
-            copy.wait()
+        packed[...] = later[...]
 
 
 def signals(scratch, s, per):
@@ -261,13 +227,10 @@
     outer_inv,
     turns,
     packed,
-    spec_out,
-    grad_out,
+    spec,
+    grad,
     known,
     out,
-    spec,
-    grad,
-    sems,
 ):
     size = data.shape[1]
 
@@ -288,22 +251,17 @@
         filt_one = to_spectrum(signals(known, 0, per), outer_fwd, inner_fwd, turns)
         spec_one = to_spectrum(grad_one, outer_fwd, inner_fwd, turns)
         spec[0] = spec_one
-        copies = fetch([(spec, spec_out), (grad, grad_out)], sems)
         mixed = from_spectrum(conj_times(filt_one, spec_one), inner_inv, outer_inv, turns)
         send_rows(out, 0, [mixed[k] + gains[0, k * size + place[0]] * grad_one[k] for k in range(per)])
         packed[...] = out[...].astype(BF)
-        for copy in copies:
-            copy.wait()
 
     @pl.when(late[0] == 0)
     def _():
+        packed[...] = later[...]
         known[...] = data[...].astype(F32)
         grad[...] = jnp.zeros_like(grad)
         spec[0] = to_spectrum(signals(known, 0, per), outer_fwd, inner_fwd, turns)
         spec[1] = to_spectrum(signals(known, 1, per), outer_fwd, inner_fwd, turns)
-        copies = fetch([(spec, spec_out), (grad, grad_out), (later, packed)], sems)
-        for copy in copies:
-            copy.wait()
 
 
 def skip_rows(per, grads, others, out):
@@ -331,9 +289,9 @@
     first,
     second,
     third,
-    held_in,
-    grad_in,
-    spec_in,
+    held,
+    grad_held,
+    spec,
     outer_fwd,
     inner_fwd,
     inner_inv,
@@ -344,13 +302,8 @@
     other,
     fresh,
     out,
-    held,
-    grad_held,
-    spec,
-    sems,
 ):
     size = first.shape[1]
-    copies = fetch([(held_in, held), (spec_in, spec), (grad_in, grad_held)], sems)
     fresh[...] = third[...].astype(F32)
     known[...] = first[...].astype(F32)
 
@@ -358,8 +311,6 @@
     def _():
         grad_two = signals(fresh, 0, per)
         spec_two = to_spectrum(grad_two, outer_fwd, inner_fwd, turns)
-        for copy in copies:
-            copy.wait()
         mixed = from_spectrum(conj_times(held[1], spec_two), inner_inv, outer_inv, turns)
         send_rows(out, 3, from_spectrum(conj_times(spec[1], spec_two), inner_inv, outer_inv, turns))
         mix_one = [mixed[k] + gains[1, k * size + place[0]] * grad_two[k] for k in range(per)]
@@ -381,8 +332,6 @@
         values, gated = signals(fresh, 0, per), signals(fresh, 1, per)
         spec_one = to_spectrum(values, outer_fwd, inner_fwd, turns)
         spec_two = to_spectrum(gated, outer_fwd, inner_fwd, turns)
-        for copy in copies:
-            copy.wait()
         send_rows(out, 2, from_spectrum(conj_times(spec_one, held[0]), inner_inv, outer_inv, turns))
         send_rows(out, 3, from_spectrum(conj_times(spec_two, held[1]), inner_inv, outer_inv, turns))
         empty = [jnp.zeros((size, size), F32)] * per
@@ -404,41 +353,29 @@
     late,
     data,
     conv,
-    part_two_in,
-    inc_in,
+    part_two,
+    inc,
     w_in,
     outer_fwd,
     inner_fwd,
     turns,
     result,
-    spec_out,
+    spec,
     scratch,
-    part_two,
-    inc,
-    spec,
-    sems,
 ):
     @pl.when(late[0] == 1)
     def _():
-        copies = fetch([(part_two_in, part_two), (inc_in, inc)], sems)
         scratch[...] = data[...].astype(F32)
         values = get_rows(scratch, 0, 2 * per, per)
         mix_one = get_rows(scratch, per, 2 * per, per)
-        for copy in copies:
-            copy.wait()
         result[...] = input_grad(inc[...], values, mix_one, conv[0], part_two[...], w_in[...])
 
     @pl.when(late[0] == 0)
     def _():
         scratch[...] = data[...].astype(F32)
-        copies = []
         for s in range(2):
             spec[s] = to_spectrum(signals(scratch, s, per), outer_fwd, inner_fwd, turns)
-            copies.append(pltpu.make_async_copy(spec.at[s], spec_out.at[s], sems.at[s]))
-            copies[s].start()
         result[...] = jnp.zeros_like(result)
-        for copy in copies:
-            copy.wait()
 
 
 def finish_body(
@@ -542,47 +479,37 @@
             pltpu.VMEM((tokens, channels), BF),
             rows(4 * per),
             rows(2 * per),
-            pltpu.VMEM(rows(2 * per), BF),
-            pltpu.VMEM((tokens, channels), BF),
-            pltpu.VMEM((tokens, channels), BF),
             pltpu.SemaphoreType.DMA((6,)),
-            pltpu.SemaphoreType.DMA((3,)),
         ],
         layer_input[0], conv, filters[0], w_in, w_out, grad_output,
-        direct=range(6), direct_out=range(1, 4),
+        direct=range(6),
     )
     packed, late, place = lax.optimization_barrier((packed, late, place))
     first = exchange(packed, parts)
     packed, held, grad_held = call(
         functools.partial(early_body, per),
         [(rows(2 * per), BF), spectra, (rows(per), F32)],
-        [
-            rows(4 * per), rows(2 * per), spectra[0], rows(per), pltpu.SemaphoreType.DMA((3,)),
-        ],
+        [rows(4 * per), rows(2 * per)],
         late, place, skip_gain[0], first, later, outer_fwd, inner_fwd, inner_inv, outer_inv, turns,
-        smem=3, direct=(4,), direct_out=(1, 2),
+        smem=3,
     )
     second = exchange(packed, parts)
     done, spec = call(
         functools.partial(hand_body, per),
         [token_rows, spectra],
         [
-            rows(2 * per), pltpu.VMEM((tokens, channels), BF), pltpu.VMEM((tokens, channels), BF),
-            spectra[0], pltpu.SemaphoreType.DMA((2,)),
+            rows(2 * per),
         ],
         late, second, conv, part_two, grad_output, w_in, outer_fwd, inner_fwd, turns,
-        smem=1, direct=(3, 4), direct_out=(1,),
+        smem=1,
     )
     handed = lax.ppermute(done, "section", [(0, 1), (1, 0)])
     packed, part_two, kept = call(
         regrad_body,
         [(rows(2 * per), BF), token_rows, token_rows],
-        [
-            pltpu.VMEM((tokens, channels), BF), pltpu.VMEM((tokens, channels), BF), rows(2 * per),
-            pltpu.SemaphoreType.DMA((3,)),
-        ],
+        [rows(2 * per)],
         late, handed, done, w_out, gate_two, conv, later,
-        smem=1, direct=(4, 6), direct_out=(1, 2),
+        smem=1,
     )
     third = exchange(packed, parts)
     out_rows = 4 * per + 2
@@ -590,13 +517,11 @@
         functools.partial(late_body, per),
         [(rows(out_rows), BF)],
         [
-            rows(4 * per), rows(2 * per), rows(2 * per), rows(out_rows), spectra[0], rows(per),
-            spectra[0],
-pltpu.SemaphoreType.DMA((3,)),
+            rows(4 * per), rows(2 * per), rows(2 * per), rows(out_rows),
         ],
         late, place, skip_gain[0], first, second, third, held, grad_held, spec,
         outer_fwd, inner_fwd, inner_inv, outer_inv, turns,
-        smem=3, direct=range(6, 9),
+        smem=3,
     )
     back = exchange(packed, parts)
     grad_rows, filter_grads, skip_grads = call(

time: 120 us -> 116 us (0.967)
  Pallas kernels: 15.3 us -> 10.8 us
    pallas_call x6, Pallas kernels: 15.3 us -> 10.8 us  [call(): pl.pallas_call(body, out_shape=[(pltpu.HBM if i in direct_out else jax.Sh...]
where the time goes in v6:
time: 116 us; the launch traced here: 115 us
  blocking collectives  102 us (88%)
  Pallas kernels  10.8 us (9%)
  waiting for transfers between devices  1.33 us (1%)
    all_to_all x4, blocking collectives, exchange(): lax.all_to_all(cut, 'seq', split_axis=0, concat_axis=0, tiled=True)  102 us
    pallas_call x6, Pallas kernels, call(): pl.pallas_call(body, out_shape=[(pltpu.HBM if i in direct_out else jax.Sh...  10.8 us
  transfers between devices with their start and end apart: 1, of which 1 were waited for; matrix products, arithmetic and copies ran while one was open for 0% of the time, Pallas kernels for 0%

profile of v6, /device:TPU:8, one launch (start us, length us, event | category | flops | bytes accessed | tf_op | source)
XLA Modules:
  0.0 115.5 jit_solution(18399717931938808993)
XLA Ops:
  0.6 0.0 copy-start.2
  0.6 0.0 copy-start.4
  0.7 0.0 copy-start.5
  0.7 0.0 copy-start.6
  0.7 0.0 copy-start.8
  0.7 0.0 copy-start.9
  0.7 2.8 %shard_map.139 = (bf16[2048,128]{1,0:T(8,128)(2,1)S(1)}, bf16[1024,128]{1,0:T(8,128)(2,1)S(1)}, bf16[128,512]{1,0:T(8,128)(2,1)S(1)}, bf16[128,512]{1,0:T(8,128)(2,1)S(1)}) custom-call(bf16[128,512]{1,0:T(8,128)(2,1)} %bitcast.41, bf16[2,128,512]{2,1,0:T(8,128)(2,1)} %bitcast.24, bf16[2,128,512]{2,1,0:T(8,128)(2,1)} %bitcast.40, bf16[512,1536]{1,0:T(8,128)(2,1)} %bitcast.19, ...), custom_call_target="tpu_custom_call" | custom-call | tf_op jit(solution)/shard_map/pallas_call | solution.py:425
  3.5 0.0 copy-start
  3.5 0.0 copy-start.1
  3.5 0.0 copy-start.7
  3.5 35.4 %all_to_all.20 = bf16[128,8,2,128]{3,2,1,0:T(2,128)(2,1)S(1)} all-to-all(bf16[128,8,2,128]{3,2,1,0:T(2,128)(2,1)S(1)} %bitcast.35), channel_id=1, replica_groups=mesh['seq'=128,'section'=2] {'seq'}, dimensions={0} | all-to-all | bytes 1048576 | tf_op jit(solution)/shard_map/all_to_all | solution.py:452
  38.9 0.0 copy-done.2
  38.9 0.0 copy-done.4
  38.9 0.0 copy-done.5
  38.9 0.0 copy-done.6
  38.9 0.0 copy-done.8
  38.9 0.0 copy-done.9
  39.0 1.5 %shard_map.140 = (bf16[1024,128]{1,0:T(8,128)(2,1)S(1)}, f32[2,512,256]{2,1,0:T(8,128)S(1)}, f32[512,128]{1,0:T(8,128)S(1)}) custom-call(s32[1]{0:T(128)} %bitcast.5.late, s32[1]{0:T(128)} %bitcast.6.place, f32[2,512]{1,0:T(2,128)S(1)} %bitcast.38, bf16[2048,128]{1,0:T(8,128)(2,1)S(1)} %bitcast.22, bf16[1024,128]{1,0:T(8,128)(2,1)S(1)} %get-tuple-element.25.later, ...), custom_call_target="tpu_custom_call" | custom-call | tf_op jit(solution)/shard_map/pallas_call | solution.py:425
  40.4 21.2 %all_to_all.21 = bf16[128,4,2,128]{3,2,1,0:T(2,128)(2,1)S(1)} all-to-all(bf16[128,4,2,128]{3,2,1,0:T(2,128)(2,1)S(1)} %bitcast.37), channel_id=1, replica_groups=mesh['seq'=128,'section'=2] {'seq'}, dimensions={0} | all-to-all | bytes 524288 | tf_op jit(solution)/shard_map/all_to_all | solution.py:452
  61.7 0.0 copy-start.3
  61.7 0.0 copy-done
  61.7 0.0 copy-done.1
  61.7 0.0 copy-done.7
  61.7 0.7 shard_map.141
  62.4 0.1 collective-permute-start
  62.5 1.3 %collective-permute-done.inc = bf16[128,512]{1,0:T(8,128)(2,1)S(1)} collective-permute-done((bf16[128,512]{1,0:T(8,128)(2,1)S(1)}, bf16[128,512]{1,0:T(8,128)(2,1)S(1)}, u32[]{:S(2)}, u32[]{:S(2)}) %collective-permute-start) | collective-permute-done | bytes 131104 | tf_op jit(solution)/shard_map/ppermute | solution.py:506
  63.9 0.0 copy-done.3
  63.9 0.5 shard_map.142
  64.3 20.8 %all_to_all.22 = bf16[128,4,2,128]{3,2,1,0:T(2,128)(2,1)S(1)} all-to-all(bf16[128,4,2,128]{3,2,1,0:T(2,128)(2,1)S(1)} %bitcast.36), channel_id=1, replica_groups=mesh['seq'=128,'section'=2] {'seq'}, dimensions={0} | all-to-all | bytes 524288 | tf_op jit(solution)/shard_map/all_to_all | solution.py:452
  85.1 3.7 %shard_map.143 = bf16[2304,128]{1,0:T(8,128)(2,1)S(1)} custom-call(s32[1]{0:T(128)} %bitcast.5.late, s32[1]{0:T(128)} %bitcast.6.place, f32[2,512]{1,0:T(2,128)S(1)} %bitcast.39, bf16[2048,128]{1,0:T(8,128)(2,1)S(1)} %bitcast.23, bf16[1024,128]{1,0:T(8,128)(2,1)S(1)} %bitcast.30, bf16[1024,128]{1,0:T(8,128)(2,1)S(1)} %bitcast.34, ...), custom_call_target="tpu_custom_call" | custom-call | tf_op jit(solution)/shard_map/pallas_call | solution.py:425
  88.9 25.0 %all_to_all.23 = bf16[128,9,2,128]{3,2,1,0:T(2,128)(2,1)S(1)} all-to-all(bf16[128,9,2,128]{3,2,1,0:T(2,128)(2,1)S(1)} %bitcast.28), channel_id=1, replica_groups=mesh['seq'=128,'section'=2] {'seq'}, dimensions={0} | all-to-all | bytes 1179648 | tf_op jit(solution)/shard_map/all_to_all | solution.py:452
  113.9 1.5 %shard_map.144 = (bf16[128,512]{1,0:T(8,128)(2,1)}, bf16[2,128,512]{2,1,0:T(8,128)(2,1)}, f32[2,512]{1,0:T(2,128)}) custom-call(s32[1]{0:T(128)} %bitcast.5.late, bf16[2304,128]{1,0:T(8,128)(2,1)S(1)} %bitcast.31, bf16[2,128,512]{2,1,0:T(8,128)(2,1)S(1)} %bitcast.27, bf16[128,512]{1,0:T(8,128)(2,1)S(1)} %get-tuple-element.34.part_two, ...), custom_call_target="tpu_custom_call" | custom-call | tf_op jit(solution)/shard_map/pallas_call | solution.py:425
Async XLA Ops:
  0.6 38.3 %copy-start.2 = (bf16[512,256]{1,0:T(8,128)(2,1)S(1)}, bf16[512,256]{1,0:T(8,128)(2,1)}, u32[]{:S(2)}) copy-start(bf16[512,256]{1,0:T(8,128)(2,1)} %constant.19.clone.inner_fwd) | copy-start | bytes 786436
  0.6 38.3 %copy-start.4 = (f32[2,128,128]{2,1,0:T(8,128)S(1)}, f32[2,128,128]{2,1,0:T(8,128)}, u32[]{:S(2)}) copy-start(f32[2,128,128]{2,1,0:T(8,128)} %constant.22.clone.turns) | copy-start | bytes 393220
  0.7 38.3 %copy-start.5 = (bf16[256,256]{1,0:T(8,128)(2,1)S(1)}, bf16[256,256]{1,0:T(8,128)(2,1)}, u32[]{:S(2)}) copy-start(bf16[256,256]{1,0:T(8,128)(2,1)} %constant.18.clone.outer_fwd) | copy-start | bytes 393220
  0.7 38.2 %copy-start.6 = (bf16[512,256]{1,0:T(8,128)(2,1)S(1)}, bf16[512,256]{1,0:T(8,128)(2,1)}, u32[]{:S(2)}) copy-start(bf16[512,256]{1,0:T(8,128)(2,1)} %constant.20.clone.inner_inv) | copy-start | bytes 786436
  0.7 38.2 %copy-start.8 = (bf16[128,512]{1,0:T(8,128)(2,1)S(1)}, bf16[128,512]{1,0:T(8,128)(2,1)}, u32[]{:S(2)}) copy-start(bf16[128,512]{1,0:T(8,128)(2,1)} %constant.21.clone.outer_inv) | copy-start | bytes 393220
  0.7 38.2 %copy-start.9 = (f32[1,2,512]{2,1,0:T(2,128)S(1)}, f32[1,2,512]{2,1,0:T(2,128)}, u32[]{:S(2)}) copy-start(f32[1,2,512]{2,1,0:T(2,128)} %param.15) | copy-start | bytes 12292
  3.5 58.2 %copy-start = (bf16[1,512,1536]{2,1,0:T(8,128)(2,1)S(1)}, bf16[1,512,1536]{2,1,0:T(8,128)(2,1)}, u32[]{:S(2)}) copy-start(bf16[1,512,1536]{2,1,0:T(8,128)(2,1)} %param.16) | copy-start | bytes 4718596
  3.5 58.2 %copy-start.1 = (bf16[1,2,128,512]{3,2,1,0:T(8,128)(2,1)S(1)}, bf16[1,2,128,512]{3,2,1,0:T(8,128)(2,1)}, u32[]{:S(2)}) copy-start(bf16[1,2,128,512]{3,2,1,0:T(8,128)(2,1)} %param.13) | copy-start | bytes 786436
  3.5 58.2 %copy-start.7 = (bf16[128,512]{1,0:T(8,128)(2,1)S(1)}, bf16[128,512]{1,0:T(8,128)(2,1)}, u32[]{:S(2)}) copy-start(bf16[128,512]{1,0:T(8,128)(2,1)} %inc.1) | copy-start | bytes 393220
  61.7 2.2 %copy-start.3 = (bf16[1,512,512]{2,1,0:T(8,128)(2,1)S(1)}, bf16[1,512,512]{2,1,0:T(8,128)(2,1)}, u32[]{:S(2)}) copy-start(bf16[1,512,512]{2,1,0:T(8,128)(2,1)} %param.17) | copy-start | bytes 1572868
  62.4 1.4 %collective-permute-start = (bf16[128,512]{1,0:T(8,128)(2,1)S(1)}, bf16[128,512]{1,0:T(8,128)(2,1)S(1)}, u32[]{:S(2)}, u32[]{:S(2)}) collective-permute-start(bf16[128,512]{1,0:T(8,128)(2,1)S(1)} %get-tuple-element.28.done), channel_id=1, source_target_pairs={{0,1},{1,0},{2,3},{3,2},{4,5},{5,4},{6,7},{7,6},{8,9},{9,8},{10,11... | collective-permute-start | bytes 393224 | tf_op jit(solution)/shard_map/ppermute | solution.py:506

commit v7 on v6

--- a/solution.py
+++ b/solution.py
@@ -126,70 +126,71 @@
 
 def prepare_body(
     rows_in,
-    conv_in,
     filt_in,
     w_in_in,
     w_out_in,
     inc_in,
-    packed_out,
-    later_out,
-    gate_two_out,
-    part_two_out,
+    packed,
+    projected,
+    mix_two,
     rows,
-    conv,
     filt,
     w_in,
     w_out,
     inc,
     first,
-    second,
     sems,
 ):
     channels = rows.shape[1]
     per = channels // rows.shape[0]
-    got_filt, got_rows, got_w_in, got_inc, got_w_out, got_conv = fetch(
-        [
-            (filt_in, filt),
-            (rows_in, rows),
-            (w_in_in, w_in),
-            (inc_in, inc),
-            (w_out_in, w_out),
-            (conv_in, conv),
-        ],
+    blocks = [pl.ds(b * channels, channels) for b in (2, 1, 0)]
+    copies = fetch(
+        [(filt_in, filt), (inc_in, inc), (w_out_in, w_out), (rows_in, rows)]
+        + [(w_in_in.at[:, block], w_in.at[:, block]) for block in blocks],
         sems,
     )
-    got_filt.wait()
+    copies[0].wait()
     put_rows(first, filt[0], 0, 4 * per)
     put_rows(first, filt[1], per, 4 * per)
-    got_rows.wait()
-    got_w_in.wait()
-    projected = mm(rows[...], w_in[...]).astype(BF)
-    gate_one = projected[:, channels : 2 * channels]
-    gate_two = projected[:, 2 * channels :]
+    for copy in copies[1:3]:
+        copy.wait()
+    mixed = mm_t(inc[...], w_out[...])
+    mix_two[...] = mixed
+    for copy in copies[3:5]:
+        copy.wait()
+    gate_two = mm(rows[...], w_in[:, blocks[0]]).astype(BF)
+    projected[:, blocks[0]] = gate_two
+    put_rows(first, mixed * gate_two.astype(F32), 3 * per, 4 * per)
+    copies[5].wait()
+    gate_one = mm(rows[...], w_in[:, blocks[1]]).astype(BF)
+    projected[:, blocks[1]] = gate_one
     put_rows(first, gate_one, 2 * per, 4 * per)
-    got_inc.wait()
-    got_w_out.wait()
-    mix_two = mm_t(inc[...], w_out[...])
-    put_rows(first, mix_two * gate_two.astype(F32), 3 * per, 4 * per)
-    packed_out[...] = first[...].astype(BF)
-    gate_two_out[...] = gate_two
-    got_conv.wait()
-    part_two_out[...] = (mix_two * conv[1].astype(F32)).astype(BF)
-    put_rows(second, projected[:, :channels], 0, 2 * per)
-    put_rows(second, gate_one.astype(F32) * conv[0].astype(F32), per, 2 * per)
-    later_out[...] = second[...].astype(BF)
-
-
-def regrad_body(late, inc, done, w_out, gate_two, conv, later, packed, part_two, kept, scratch):
+    packed[...] = first[...].astype(BF)
+    copies[6].wait()
+    projected[:, blocks[2]] = mm(rows[...], w_in[:, blocks[2]]).astype(BF)
+
+
+def pack_known(scratch, projected, conv, packed):
+    channels = conv.shape[2]
+    per = channels // conv.shape[1]
+    gate_one = projected[:, pl.ds(channels, channels)].astype(F32)
+    put_rows(scratch, projected[:, pl.ds(0, channels)], 0, 2 * per)
+    put_rows(scratch, gate_one * conv[0].astype(F32), per, 2 * per)
+    packed[...] = scratch[...].astype(BF)
+
+
+def regrad_body(late, inc, done, w_out, projected, conv, packed, part_two, kept, scratch):
     size = inc.shape[0]
-    per = inc.shape[1] // size
+    channels = inc.shape[1]
+    per = channels // size
 
     @pl.when(late[0] == 0)
     def _():
         kept[...] = inc[...]
         mix_two = mm_t(inc[...], w_out[...])
         part_two[...] = (mix_two * conv[1].astype(F32)).astype(BF)
-        put_rows(scratch, mix_two * gate_two[...].astype(F32), 0, 2 * per)
+        gate_two = projected[:, pl.ds(2 * channels, channels)].astype(F32)
+        put_rows(scratch, mix_two * gate_two, 0, 2 * per)
         for k in range(per):
             scratch[pl.ds(per + k, size, stride=2 * per), :] = jnp.zeros((size, size), F32)
         packed[...] = scratch[...].astype(BF)
@@ -198,7 +199,7 @@
     def _():
         kept[...] = done[...]
         part_two[...] = jnp.zeros_like(part_two)
-        packed[...] = later[...]
+        pack_known(scratch, projected, conv, packed)
 
 
 def signals(scratch, s, per):
@@ -220,7 +221,8 @@
     place,
     gains,
     data,
-    later,
+    projected,
+    conv,
     outer_fwd,
     inner_fwd,
     inner_inv,
@@ -242,7 +244,7 @@
         spec_two = to_spectrum(grad_two, outer_fwd, inner_fwd, turns)
         spec[1] = spec_two
         mixed = from_spectrum(conj_times(filt_two, spec_two), inner_inv, outer_inv, turns)
-        mix_one = [mixed[k] + gains[1, k * size + place[0]] * grad_two[k] for k in range(per)]
+        mix_one = [mixed[k] + gain_of(gains, 1, k, place, size) * grad_two[k] for k in range(per)]
         send_rows(out, 1, mix_one)
         gate_one = signals(known, 2, per)
         grad_one = [mix_one[k] * gate_one[k] for k in range(per)]
@@ -252,16 +254,22 @@
         spec_one = to_spectrum(grad_one, outer_fwd, inner_fwd, turns)
         spec[0] = spec_one
         mixed = from_spectrum(conj_times(filt_one, spec_one), inner_inv, outer_inv, turns)
-        send_rows(out, 0, [mixed[k] + gains[0, k * size + place[0]] * grad_one[k] for k in range(per)])
+        send_rows(out, 0, [mixed[k] + gain_of(gains, 0, k, place, size) * grad_one[k] for k in range(per)])
         packed[...] = out[...].astype(BF)
 
     @pl.when(late[0] == 0)
     def _():
-        packed[...] = later[...]
+        pack_known(out, projected, conv, packed)
         known[...] = data[...].astype(F32)
         grad[...] = jnp.zeros_like(grad)
         spec[0] = to_spectrum(signals(known, 0, per), outer_fwd, inner_fwd, turns)
         spec[1] = to_spectrum(signals(known, 1, per), outer_fwd, inner_fwd, turns)
+
+
+def gain_of(gains, w, k, place, size):
+    row = gains[pl.ds(w, 1), k * size : (k + 1) * size]
+    lane = lax.broadcasted_iota(jnp.int32, row.shape, 1)
+    return jnp.sum(jnp.where(lane == place[0], row, 0.0), axis=1, keepdims=True)
 
 
 def skip_rows(per, grads, others, out):
@@ -312,15 +320,20 @@
         grad_two = signals(fresh, 0, per)
         spec_two = to_spectrum(grad_two, outer_fwd, inner_fwd, turns)
         mixed = from_spectrum(conj_times(held[1], spec_two), inner_inv, outer_inv, turns)
-        send_rows(out, 3, from_spectrum(conj_times(spec[1], spec_two), inner_inv, outer_inv, turns))
-        mix_one = [mixed[k] + gains[1, k * size + place[0]] * grad_two[k] for k in range(per)]
+        mix_one = [mixed[k] + gain_of(gains, 1, k, place, size) * grad_two[k] for k in range(per)]
         send_rows(out, 1, mix_one)
         gate_one = signals(known, 2, per)
         grad_one = [mix_one[k] * gate_one[k] for k in range(per)]
         spec_one = to_spectrum(grad_one, outer_fwd, inner_fwd, turns)
-        mixed = from_spectrum(conj_times(held[0], spec_one), inner_inv, outer_inv, turns)
-        send_rows(out, 2, from_spectrum(conj_times(spec[0], spec_one), inner_inv, outer_inv, turns))
-        send_rows(out, 0, [mixed[k] + gains[0, k * size + place[0]] * grad_one[k] for k in range(per)])
+        products = [
+            conj_times(held[0], spec_one),
+            conj_times(spec[0], spec_one),
+            conj_times(spec[1], spec_two),
+        ]
+        mixed = from_spectrum(jnp.concatenate(products, axis=0), inner_inv, outer_inv, turns)
+        send_rows(out, 2, mixed[per : 2 * per])
+        send_rows(out, 3, mixed[2 * per :])
+        send_rows(out, 0, [mixed[k] + gain_of(gains, 0, k, place, size) * grad_one[k] for k in range(per)])
         other[...] = second[...].astype(F32)
         skip_rows(
             per, (grad_one, grad_two), (signals(other, 0, per), signals(other, 1, per)), out
@@ -353,7 +366,7 @@
     late,
     data,
     conv,
-    part_two,
+    mix_two,
     inc,
     w_in,
     outer_fwd,
@@ -368,7 +381,8 @@
         scratch[...] = data[...].astype(F32)
         values = get_rows(scratch, 0, 2 * per, per)
         mix_one = get_rows(scratch, per, 2 * per, per)
-        result[...] = input_grad(inc[...], values, mix_one, conv[0], part_two[...], w_in[...])
+        part_two = (mix_two[...] * conv[1].astype(F32)).astype(BF)
+        result[...] = input_grad(inc[...], values, mix_one, conv[0], part_two, w_in[...])
 
     @pl.when(late[0] == 0)
     def _():
@@ -387,14 +401,24 @@
     part_two,
     inc,
     w_in,
+    result_out,
+    filt_out,
+    skip_grads,
+    scratch,
     result,
     filt_grads,
-    skip_grads,
-    scratch,
+    sems,
 ):
     size = data.shape[1]
     stride = data.shape[0] // size
     scratch[...] = data[...].astype(F32)
+    copies = []
+    for s in range(2):
+        filt_grads[s] = (
+            get_rows(scratch, (2 + s) * per, stride, per).astype(F32) * rescale
+        ).astype(BF)
+        copies.append(pltpu.make_async_copy(filt_grads.at[s], filt_out.at[s], sems.at[s]))
+        copies[s].start()
 
     @pl.when(late[0] == 0)
     def _():
@@ -406,14 +430,16 @@
     def _():
         result[...] = inc[...]
 
-    filt_grads[0] = (get_rows(scratch, 2 * per, stride, per).astype(F32) * rescale).astype(BF)
-    filt_grads[1] = (get_rows(scratch, 3 * per, stride, per).astype(F32) * rescale).astype(BF)
+    copies.append(pltpu.make_async_copy(result, result_out, sems.at[2]))
+    copies[2].start()
     sums = scratch[pl.ds(4 * per, size, stride=stride), :].T
     sums = (sums[: 2 * per] + sums[2 * per : 4 * per]) * rescale
     for w in range(2):
         for k in range(per):
             row = w * per + k
             skip_grads[pl.ds(w, 1), pl.ds(k * size, size)] = sums[row : row + 1]
+    for copy in copies:
+        copy.wait()
 
 
 def call(body, out_shapes, scratch, *operands, smem=0, direct=(), direct_out=(), limit=VMEM_LIMIT):
@@ -467,22 +493,20 @@
     token_rows = ((tokens, channels), BF)
     spectra = ((2, per * parts, 2 * tokens), F32)
 
-    packed, later, gate_two, part_two = call(
+    packed, projected, mix_two = call(
         prepare_body,
-        [(rows(4 * per), BF), (rows(2 * per), BF), token_rows, token_rows],
+        [(rows(4 * per), BF), ((tokens, 3 * channels), BF), ((tokens, channels), F32)],
         [
             pltpu.VMEM((tokens, channels), BF),
-            pltpu.VMEM((2, tokens, channels), BF),
             pltpu.VMEM((2, tokens, channels), BF),
             pltpu.VMEM(w_in.shape, BF),
             pltpu.VMEM(w_out.shape, BF),
             pltpu.VMEM((tokens, channels), BF),
             rows(4 * per),
-            rows(2 * per),
-            pltpu.SemaphoreType.DMA((6,)),
-        ],
-        layer_input[0], conv, filters[0], w_in, w_out, grad_output,
-        direct=range(6),
+            pltpu.SemaphoreType.DMA((7,)),
+        ],
+        layer_input[0], filters[0], w_in, w_out, grad_output,
+        direct=range(5),
     )
     packed, late, place = lax.optimization_barrier((packed, late, place))
     first = exchange(packed, parts)
@@ -490,8 +514,8 @@
         functools.partial(early_body, per),
         [(rows(2 * per), BF), spectra, (rows(per), F32)],
         [rows(4 * per), rows(2 * per)],
-        late, place, skip_gain[0], first, later, outer_fwd, inner_fwd, inner_inv, outer_inv, turns,
-        smem=3,
+        late, place, skip_gain[0], first, projected, conv, outer_fwd, inner_fwd, inner_inv, outer_inv, turns,
+        smem=2,
     )
     second = exchange(packed, parts)
     done, spec = call(
@@ -500,7 +524,7 @@
         [
             rows(2 * per),
         ],
-        late, second, conv, part_two, grad_output, w_in, outer_fwd, inner_fwd, turns,
+        late, second, conv, mix_two, grad_output, w_in, outer_fwd, inner_fwd, turns,
         smem=1,
     )
     handed = lax.ppermute(done, "section", [(0, 1), (1, 0)])
@@ -508,7 +532,7 @@
         regrad_body,
         [(rows(2 * per), BF), token_rows, token_rows],
         [rows(2 * per)],
-        late, handed, done, w_out, gate_two, conv, later,
+        late, handed, done, w_out, projected, conv,
         smem=1,
     )
     third = exchange(packed, parts)
@@ -521,15 +545,18 @@
         ],
         late, place, skip_gain[0], first, second, third, held, grad_held, spec,
         outer_fwd, inner_fwd, inner_inv, outer_inv, turns,
-        smem=3,
+        smem=2,
     )
     back = exchange(packed, parts)
     grad_rows, filter_grads, skip_grads = call(
         functools.partial(finish_body, per, 1.0 / math.sqrt(parts * tokens)),
         [token_rows, ((2, tokens, channels), BF), ((2, channels), F32)],
-        [rows(out_rows)],
+        [
+            rows(out_rows), pltpu.VMEM((tokens, channels), BF),
+            pltpu.VMEM((2, tokens, channels), BF), pltpu.SemaphoreType.DMA((3,)),
+        ],
         late, back, conv, part_two, kept, w_in,
-        smem=1,
+        smem=1, direct_out=(0, 1),
     )
     return (grad_rows[None], filter_grads[None], skip_grads[None])
 

time: 116 us -> 115 us (level)
  no operation moved by 1% of the time
where the time goes in v7:
time: 115 us
  blocking collectives  103 us (90%)
  Pallas kernels  9.83 us (9%)
  waiting for transfers between devices  1.33 us (1%)
    all_to_all x4, blocking collectives, exchange(): lax.all_to_all(cut, 'seq', split_axis=0, concat_axis=0, tiled=True)  103 us
    pallas_call x6, Pallas kernels, call(): pl.pallas_call(body, out_shape=[(pltpu.HBM if i in direct_out else jax.Sh...  9.83 us
  transfers between devices with their start and end apart: 1, of which 1 were waited for; matrix products, arithmetic and copies ran while one was open for 0% of the time, Pallas kernels for 0%

profile of v7, /device:TPU:8, one launch (start us, length us, event | category | flops | bytes accessed | tf_op | source)
XLA Modules:
  0.0 115.0 jit_solution(13611271435669744727)
XLA Ops:
  0.6 0.0 copy-start.1
  0.6 0.0 copy-start.2
  0.7 0.0 copy-start.4
  0.7 0.0 copy-start.5
  0.7 0.0 copy-start.6
  0.7 0.0 copy-start.8
  0.7 0.0 copy-start.9
  0.7 2.7 %shard_map.139 = (bf16[2048,128]{1,0:T(8,128)(2,1)S(1)}, bf16[128,1536]{1,0:T(8,128)(2,1)S(1)}, f32[128,512]{1,0:T(8,128)S(1)}) custom-call(bf16[128,512]{1,0:T(8,128)(2,1)} %bitcast.41, bf16[2,128,512]{2,1,0:T(8,128)(2,1)} %bitcast.40, bf16[512,1536]{1,0:T(8,128)(2,1)} %bitcast.19, bf16[512,512]{1,0:T(8,128)(2,1)} %bitcast.32, bf16[128,512]{1,0:T(8,128)(2,1)} %inc.1), custom_call_target="tpu_custom_call" | custom-call | tf_op jit(solution)/shard_map/pallas_call | solution.py:451
  3.4 35.2 %all_to_all.20 = bf16[128,8,2,128]{3,2,1,0:T(2,128)(2,1)S(1)} all-to-all(bf16[128,8,2,128]{3,2,1,0:T(2,128)(2,1)S(1)} %bitcast.35), channel_id=1, replica_groups=mesh['seq'=128,'section'=2] {'seq'}, dimensions={0} | all-to-all | bytes 1048576 | tf_op jit(solution)/shard_map/all_to_all | solution.py:478
  38.6 0.0 copy-start
  38.6 0.0 copy-start.7
  38.6 0.0 copy-done.1
  38.6 0.0 copy-done.2
  38.6 0.0 copy-done.4
  38.6 0.0 copy-done.5
  38.7 0.0 copy-done.6
  38.7 0.0 copy-done.8
  38.7 0.0 copy-done.9
  38.7 0.9 shard_map.140
  39.6 21.2 %all_to_all.21 = bf16[128,4,2,128]{3,2,1,0:T(2,128)(2,1)S(1)} all-to-all(bf16[128,4,2,128]{3,2,1,0:T(2,128)(2,1)S(1)} %bitcast.37), channel_id=1, replica_groups=mesh['seq'=128,'section'=2] {'seq'}, dimensions={0} | all-to-all | bytes 524288 | tf_op jit(solution)/shard_map/all_to_all | solution.py:478
  60.8 0.0 copy-start.3
  60.8 0.0 copy-done
  60.8 0.0 copy-done.7
  60.8 0.7 shard_map.141
  61.5 0.1 collective-permute-start
  61.6 1.3 %collective-permute-done.inc = bf16[128,512]{1,0:T(8,128)(2,1)S(1)} collective-permute-done((bf16[128,512]{1,0:T(8,128)(2,1)S(1)}, bf16[128,512]{1,0:T(8,128)(2,1)S(1)}, u32[]{:S(2)}, u32[]{:S(2)}) %collective-permute-start) | collective-permute-done | bytes 131104 | tf_op jit(solution)/shard_map/ppermute | solution.py:530
  63.0 0.0 copy-done.3
  63.0 0.5 shard_map.142
  63.5 20.9 %all_to_all.22 = bf16[128,4,2,128]{3,2,1,0:T(2,128)(2,1)S(1)} all-to-all(bf16[128,4,2,128]{3,2,1,0:T(2,128)(2,1)S(1)} %bitcast.36), channel_id=1, replica_groups=mesh['seq'=128,'section'=2] {'seq'}, dimensions={0} | all-to-all | bytes 524288 | tf_op jit(solution)/shard_map/all_to_all | solution.py:478
  84.4 2.9 %shard_map.143 = bf16[2304,128]{1,0:T(8,128)(2,1)S(1)} custom-call(s32[1]{0:T(128)} %bitcast.4.late, s32[1]{0:T(128)} %bitcast.5.place, f32[2,512]{1,0:T(2,128)S(1)} %bitcast.39, bf16[2048,128]{1,0:T(8,128)(2,1)S(1)} %bitcast.23, bf16[1024,128]{1,0:T(8,128)(2,1)S(1)} %bitcast.30, bf16[1024,128]{1,0:T(8,128)(2,1)S(1)} %bitcast.34, ...), custom_call_target="tpu_custom_call" | custom-call | tf_op jit(solution)/shard_map/pallas_call | solution.py:451
  87.4 25.4 %all_to_all.23 = bf16[128,9,2,128]{3,2,1,0:T(2,128)(2,1)S(1)} all-to-all(bf16[128,9,2,128]{3,2,1,0:T(2,128)(2,1)S(1)} %bitcast.28), channel_id=1, replica_groups=mesh['seq'=128,'section'=2] {'seq'}, dimensions={0} | all-to-all | bytes 1179648 | tf_op jit(solution)/shard_map/all_to_all | solution.py:478
  112.7 2.1 %shard_map.144 = (bf16[128,512]{1,0:T(8,128)(2,1)}, bf16[2,128,512]{2,1,0:T(8,128)(2,1)}, f32[2,512]{1,0:T(2,128)}) custom-call(s32[1]{0:T(128)} %bitcast.4.late, bf16[2304,128]{1,0:T(8,128)(2,1)S(1)} %bitcast.31, bf16[2,128,512]{2,1,0:T(8,128)(2,1)S(1)} %bitcast.27, bf16[128,512]{1,0:T(8,128)(2,1)S(1)} %get-tuple-element.32.part_two, ...), custom_call_target="tpu_custom_call" | custom-call | tf_op jit(solution)/shard_map/pallas_call | solution.py:451
Async XLA Ops:
  0.6 38.0 %copy-start.1 = (bf16[1,2,128,512]{3,2,1,0:T(8,128)(2,1)S(1)}, bf16[1,2,128,512]{3,2,1,0:T(8,128)(2,1)}, u32[]{:S(2)}) copy-start(bf16[1,2,128,512]{3,2,1,0:T(8,128)(2,1)} %param.13) | copy-start | bytes 786436
  0.6 38.0 %copy-start.2 = (bf16[512,256]{1,0:T(8,128)(2,1)S(1)}, bf16[512,256]{1,0:T(8,128)(2,1)}, u32[]{:S(2)}) copy-start(bf16[512,256]{1,0:T(8,128)(2,1)} %constant.19.clone.inner_fwd) | copy-start | bytes 786436
  0.7 38.0 %copy-start.4 = (f32[2,128,128]{2,1,0:T(8,128)S(1)}, f32[2,128,128]{2,1,0:T(8,128)}, u32[]{:S(2)}) copy-start(f32[2,128,128]{2,1,0:T(8,128)} %constant.22.clone.turns) | copy-start | bytes 393220
  0.7 38.0 %copy-start.5 = (bf16[256,256]{1,0:T(8,128)(2,1)S(1)}, bf16[256,256]{1,0:T(8,128)(2,1)}, u32[]{:S(2)}) copy-start(bf16[256,256]{1,0:T(8,128)(2,1)} %constant.18.clone.outer_fwd) | copy-start | bytes 393220
  0.7 38.0 %copy-start.6 = (bf16[512,256]{1,0:T(8,128)(2,1)S(1)}, bf16[512,256]{1,0:T(8,128)(2,1)}, u32[]{:S(2)}) copy-start(bf16[512,256]{1,0:T(8,128)(2,1)} %constant.20.clone.inner_inv) | copy-start | bytes 786436
  0.7 38.0 %copy-start.8 = (bf16[128,512]{1,0:T(8,128)(2,1)S(1)}, bf16[128,512]{1,0:T(8,128)(2,1)}, u32[]{:S(2)}) copy-start(bf16[128,512]{1,0:T(8,128)(2,1)} %constant.21.clone.outer_inv) | copy-start | bytes 393220
  0.7 38.0 %copy-start.9 = (f32[1,2,512]{2,1,0:T(2,128)S(1)}, f32[1,2,512]{2,1,0:T(2,128)}, u32[]{:S(2)}) copy-start(f32[1,2,512]{2,1,0:T(2,128)} %param.15) | copy-start | bytes 12292
  38.6 22.2 %copy-start = (bf16[1,512,1536]{2,1,0:T(8,128)(2,1)S(1)}, bf16[1,512,1536]{2,1,0:T(8,128)(2,1)}, u32[]{:S(2)}) copy-start(bf16[1,512,1536]{2,1,0:T(8,128)(2,1)} %param.16) | copy-start | bytes 4718596
  38.6 22.2 %copy-start.7 = (bf16[128,512]{1,0:T(8,128)(2,1)S(1)}, bf16[128,512]{1,0:T(8,128)(2,1)}, u32[]{:S(2)}) copy-start(bf16[128,512]{1,0:T(8,128)(2,1)} %inc.1) | copy-start | bytes 393220
  60.8 2.2 %copy-start.3 = (bf16[1,512,512]{2,1,0:T(8,128)(2,1)S(1)}, bf16[1,512,512]{2,1,0:T(8,128)(2,1)}, u32[]{:S(2)}) copy-start(bf16[1,512,512]{2,1,0:T(8,128)(2,1)} %param.17) | copy-start | bytes 1572868
  61.5 1.4 %collective-permute-start = (bf16[128,512]{1,0:T(8,128)(2,1)S(1)}, bf16[128,512]{1,0:T(8,128)(2,1)S(1)}, u32[]{:S(2)}, u32[]{:S(2)}) collective-permute-start(bf16[128,512]{1,0:T(8,128)(2,1)S(1)} %get-tuple-element.27.done), channel_id=1, source_target_pairs={{0,1},{1,0},{2,3},{3,2},{4,5},{5,4},{6,7},{7,6},{8,9},{9,8},{10,11... | collective-permute-start | bytes 393224 | tf_op jit(solution)/shard_map/ppermute | solution.py:530

commit v8 on v7

--- a/solution.py
+++ b/solution.py
@@ -30,7 +30,7 @@
     cos_in, sin_in = np.cos(inner), np.sin(inner)
     outer_fwd = split_table(np.concatenate([np.cos(outer), -np.sin(outer)], 0), 1)
     inner_fwd = split_table(np.block([[cos_in, -sin_in], [sin_in, cos_in]]), 0)
-    inner_inv = split_table(np.block([[cos_in, sin_in], [-sin_in, cos_in]]), 0)
+    inner_inv = np.block([[cos_in, sin_in], [-sin_in, cos_in]]).astype(ml_dtypes.bfloat16)
     outer_inv = split_table(
         np.concatenate([np.cos(outer).T, -np.sin(outer).T], 1) * (2.0 / period), 1
     )
@@ -84,7 +84,7 @@
     size = turns.shape[1]
     count = product.shape[0] // size
     data = product.astype(BF)
-    mixed = mm(jnp.concatenate([data, data], axis=1), inner[...])
+    mixed = mm(data, inner[...])
     turn_cos, turn_sin = turns[0], turns[1]
     reals, imags = [], []
     for c in range(count):
@@ -131,13 +131,13 @@
     w_out_in,
     inc_in,
     packed,
-    projected,
+    gates,
     mix_two,
     rows,
-    filt,
     w_in,
     w_out,
     inc,
+    filt,
     first,
     sems,
 ):
@@ -159,27 +159,28 @@
     for copy in copies[3:5]:
         copy.wait()
     gate_two = mm(rows[...], w_in[:, blocks[0]]).astype(BF)
-    projected[:, blocks[0]] = gate_two
+    gates[1] = gate_two
     put_rows(first, mixed * gate_two.astype(F32), 3 * per, 4 * per)
     copies[5].wait()
     gate_one = mm(rows[...], w_in[:, blocks[1]]).astype(BF)
-    projected[:, blocks[1]] = gate_one
+    gates[0] = gate_one
     put_rows(first, gate_one, 2 * per, 4 * per)
     packed[...] = first[...].astype(BF)
     copies[6].wait()
-    projected[:, blocks[2]] = mm(rows[...], w_in[:, blocks[2]]).astype(BF)
-
-
-def pack_known(scratch, projected, conv, packed):
-    channels = conv.shape[2]
-    per = channels // conv.shape[1]
-    gate_one = projected[:, pl.ds(channels, channels)].astype(F32)
-    put_rows(scratch, projected[:, pl.ds(0, channels)], 0, 2 * per)
-    put_rows(scratch, gate_one * conv[0].astype(F32), per, 2 * per)
+
+
+def pack_known(scratch, rows, w_in, gates, conv, packed):
+    channels = rows.shape[1]
+    per = channels // rows.shape[0]
+    values = mm(rows[...], w_in[:, pl.ds(0, channels)]).astype(BF)
+    put_rows(scratch, values, 0, 2 * per)
+    put_rows(scratch, gates[0].astype(F32) * conv[0].astype(F32), per, 2 * per)
     packed[...] = scratch[...].astype(BF)
 
 
-def regrad_body(late, inc, done, w_out, projected, conv, packed, part_two, kept, scratch):
+def regrad_body(
+    late, inc, done, w_out, rows, w_in, gates, conv, packed, part_two, kept, scratch
+):
     size = inc.shape[0]
     channels = inc.shape[1]
     per = channels // size
@@ -189,8 +190,7 @@
         kept[...] = inc[...]
         mix_two = mm_t(inc[...], w_out[...])
         part_two[...] = (mix_two * conv[1].astype(F32)).astype(BF)
-        gate_two = projected[:, pl.ds(2 * channels, channels)].astype(F32)
-        put_rows(scratch, mix_two * gate_two, 0, 2 * per)
+        put_rows(scratch, mix_two * gates[1].astype(F32), 0, 2 * per)
         for k in range(per):
             scratch[pl.ds(per + k, size, stride=2 * per), :] = jnp.zeros((size, size), F32)
         packed[...] = scratch[...].astype(BF)
@@ -199,7 +199,7 @@
     def _():
         kept[...] = done[...]
         part_two[...] = jnp.zeros_like(part_two)
-        pack_known(scratch, projected, conv, packed)
+        pack_known(scratch, rows, w_in, gates, conv, packed)
 
 
 def signals(scratch, s, per):
@@ -221,7 +221,9 @@
     place,
     gains,
     data,
-    projected,
+    rows,
+    w_in,
+    gates,
     conv,
     outer_fwd,
     inner_fwd,
@@ -259,9 +261,10 @@
 
     @pl.when(late[0] == 0)
     def _():
-        pack_known(out, projected, conv, packed)
+        pack_known(out, rows, w_in, gates, conv, packed)
         known[...] = data[...].astype(F32)
-        grad[...] = jnp.zeros_like(grad)
+        for k, gate_one in enumerate(signals(known, 2, per)):
+            grad[pl.ds(k * size, size), :] = gate_one
         spec[0] = to_spectrum(signals(known, 0, per), outer_fwd, inner_fwd, turns)
         spec[1] = to_spectrum(signals(known, 1, per), outer_fwd, inner_fwd, turns)
 
@@ -295,7 +298,7 @@
     place,
     gains,
     first,
-    second,
+    plain,
     third,
     held,
     grad_held,
@@ -307,41 +310,35 @@
     turns,
     packed,
     known,
-    other,
     fresh,
     out,
 ):
     size = first.shape[1]
     fresh[...] = third[...].astype(F32)
-    known[...] = first[...].astype(F32)
 
     @pl.when(late[0] == 0)
     def _():
         grad_two = signals(fresh, 0, per)
         spec_two = to_spectrum(grad_two, outer_fwd, inner_fwd, turns)
         mixed = from_spectrum(conj_times(held[1], spec_two), inner_inv, outer_inv, turns)
+        send_rows(out, 3, from_spectrum(conj_times(spec[1], spec_two), inner_inv, outer_inv, turns))
         mix_one = [mixed[k] + gain_of(gains, 1, k, place, size) * grad_two[k] for k in range(per)]
         send_rows(out, 1, mix_one)
-        gate_one = signals(known, 2, per)
+        gate_one = [grad_held[pl.ds(k * size, size), :] for k in range(per)]
         grad_one = [mix_one[k] * gate_one[k] for k in range(per)]
         spec_one = to_spectrum(grad_one, outer_fwd, inner_fwd, turns)
-        products = [
-            conj_times(held[0], spec_one),
-            conj_times(spec[0], spec_one),
-            conj_times(spec[1], spec_two),
+        mixed = from_spectrum(conj_times(held[0], spec_one), inner_inv, outer_inv, turns)
+        send_rows(out, 2, from_spectrum(conj_times(spec[0], spec_one), inner_inv, outer_inv, turns))
+        send_rows(out, 0, [mixed[k] + gain_of(gains, 0, k, place, size) * grad_one[k] for k in range(per)])
+        others = [
+            [plain[pl.ds((s * per + k) * size, size), :] for k in range(per)] for s in range(2)
         ]
-        mixed = from_spectrum(jnp.concatenate(products, axis=0), inner_inv, outer_inv, turns)
-        send_rows(out, 2, mixed[per : 2 * per])
-        send_rows(out, 3, mixed[2 * per :])
-        send_rows(out, 0, [mixed[k] + gain_of(gains, 0, k, place, size) * grad_one[k] for k in range(per)])
-        other[...] = second[...].astype(F32)
-        skip_rows(
-            per, (grad_one, grad_two), (signals(other, 0, per), signals(other, 1, per)), out
-        )
+        skip_rows(per, (grad_one, grad_two), others, out)
         packed[...] = out[...].astype(BF)
 
     @pl.when(late[0] == 1)
     def _():
+        known[...] = first[...].astype(F32)
         values, gated = signals(fresh, 0, per), signals(fresh, 1, per)
         spec_one = to_spectrum(values, outer_fwd, inner_fwd, turns)
         spec_two = to_spectrum(gated, outer_fwd, inner_fwd, turns)
@@ -374,6 +371,7 @@
     turns,
     result,
     spec,
+    plain,
     scratch,
 ):
     @pl.when(late[0] == 1)
@@ -387,8 +385,12 @@
     @pl.when(late[0] == 0)
     def _():
         scratch[...] = data[...].astype(F32)
+        size = data.shape[1]
         for s in range(2):
-            spec[s] = to_spectrum(signals(scratch, s, per), outer_fwd, inner_fwd, turns)
+            blocks = signals(scratch, s, per)
+            for k in range(per):
+                plain[pl.ds((s * per + k) * size, size), :] = blocks[k]
+            spec[s] = to_spectrum(blocks, outer_fwd, inner_fwd, turns)
         result[...] = jnp.zeros_like(result)
 
 
@@ -401,24 +403,14 @@
     part_two,
     inc,
     w_in,
-    result_out,
-    filt_out,
+    result,
+    filt_grads,
     skip_grads,
     scratch,
-    result,
-    filt_grads,
-    sems,
 ):
     size = data.shape[1]
     stride = data.shape[0] // size
     scratch[...] = data[...].astype(F32)
-    copies = []
-    for s in range(2):
-        filt_grads[s] = (
-            get_rows(scratch, (2 + s) * per, stride, per).astype(F32) * rescale
-        ).astype(BF)
-        copies.append(pltpu.make_async_copy(filt_grads.at[s], filt_out.at[s], sems.at[s]))
-        copies[s].start()
 
     @pl.when(late[0] == 0)
     def _():
@@ -430,16 +422,14 @@
     def _():
         result[...] = inc[...]
 
-    copies.append(pltpu.make_async_copy(result, result_out, sems.at[2]))
-    copies[2].start()
+    filt_grads[0] = (get_rows(scratch, 2 * per, stride, per).astype(F32) * rescale).astype(BF)
+    filt_grads[1] = (get_rows(scratch, 3 * per, stride, per).astype(F32) * rescale).astype(BF)
     sums = scratch[pl.ds(4 * per, size, stride=stride), :].T
     sums = (sums[: 2 * per] + sums[2 * per : 4 * per]) * rescale
     for w in range(2):
         for k in range(per):
             row = w * per + k
             skip_grads[pl.ds(w, 1), pl.ds(k * size, size)] = sums[row : row + 1]
-    for copy in copies:
-        copy.wait()
 
 
 def call(body, out_shapes, scratch, *operands, smem=0, direct=(), direct_out=(), limit=VMEM_LIMIT):
@@ -493,17 +483,14 @@
     token_rows = ((tokens, channels), BF)
     spectra = ((2, per * parts, 2 * tokens), F32)
 
-    packed, projected, mix_two = call(
+    packed, gates, mix_two, rows_in, w_in, w_out, incoming = call(
         prepare_body,
-        [(rows(4 * per), BF), ((tokens, 3 * channels), BF), ((tokens, channels), F32)],
         [
-            pltpu.VMEM((tokens, channels), BF),
-            pltpu.VMEM((2, tokens, channels), BF),
-            pltpu.VMEM(w_in.shape, BF),
-            pltpu.VMEM(w_out.shape, BF),
-            pltpu.VMEM((tokens, channels), BF),
-            rows(4 * per),
-            pltpu.SemaphoreType.DMA((7,)),
+            (rows(4 * per), BF), ((2, tokens, channels), BF), ((tokens, channels), F32),
+            token_rows, (w_in.shape, BF), (w_out.shape, BF), token_rows,
+        ],
+        [
+            pltpu.VMEM((2, tokens, channels), BF), rows(4 * per), pltpu.SemaphoreType.DMA((7,)),
         ],
         layer_input[0], filters[0], w_in, w_out, grad_output,
         direct=range(5),
@@ -514,17 +501,18 @@
         functools.partial(early_body, per),
         [(rows(2 * per), BF), spectra, (rows(per), F32)],
         [rows(4 * per), rows(2 * per)],
-        late, place, skip_gain[0], first, projected, conv, outer_fwd, inner_fwd, inner_inv, outer_inv, turns,
+        late, place, skip_gain[0], first, rows_in, w_in, gates, conv,
+        outer_fwd, inner_fwd, inner_inv, outer_inv, turns,
         smem=2,
     )
     second = exchange(packed, parts)
-    done, spec = call(
+    done, spec, plain = call(
         functools.partial(hand_body, per),
-        [token_rows, spectra],
+        [token_rows, spectra, (rows(2 * per), F32)],
         [
             rows(2 * per),
         ],
-        late, second, conv, mix_two, grad_output, w_in, outer_fwd, inner_fwd, turns,
+        late, second, conv, mix_two, incoming, w_in, outer_fwd, inner_fwd, turns,
         smem=1,
     )
     handed = lax.ppermute(done, "section", [(0, 1), (1, 0)])
@@ -532,7 +520,7 @@
         regrad_body,
         [(rows(2 * per), BF), token_rows, token_rows],
         [rows(2 * per)],
-        late, handed, done, w_out, projected, conv,
+        late, handed, done, w_out, rows_in, w_in, gates, conv,
         smem=1,
     )
     third = exchange(packed, parts)
@@ -541,9 +529,9 @@
         functools.partial(late_body, per),
         [(rows(out_rows), BF)],
         [
-            rows(4 * per), rows(2 * per), rows(2 * per), rows(out_rows),
-        ],
-        late, place, skip_gain[0], first, second, third, held, grad_held, spec,
+            rows(4 * per), rows(2 * per), rows(out_rows),
+        ],
+        late, place, skip_gain[0], first, plain, third, held, grad_held, spec,
         outer_fwd, inner_fwd, inner_inv, outer_inv, turns,
         smem=2,
     )
@@ -551,12 +539,9 @@
     grad_rows, filter_grads, skip_grads = call(
         functools.partial(finish_body, per, 1.0 / math.sqrt(parts * tokens)),
         [token_rows, ((2, tokens, channels), BF), ((2, channels), F32)],
-        [
-            rows(out_rows), pltpu.VMEM((tokens, channels), BF),
-            pltpu.VMEM((2, tokens, channels), BF), pltpu.SemaphoreType.DMA((3,)),
-        ],
+        [rows(out_rows)],
         late, back, conv, part_two, kept, w_in,
-        smem=1, direct_out=(0, 1),
+        smem=1,
     )
     return (grad_rows[None], filter_grads[None], skip_grads[None])
 

time: 115 us -> 114 us (level)
  Pallas kernels: 9.83 us -> 8.4 us
    pallas_call x6, Pallas kernels: 9.83 us -> 8.4 us  [call(): pl.pallas_call(body, out_shape=[(pltpu.HBM if i in direct_out else jax.Sh...]
where the time goes in v8:
time: 114 us
  blocking collectives  103 us (90%)
  Pallas kernels  8.4 us (7%)
  waiting for transfers between devices  1.33 us (1%)
    all_to_all x4, blocking collectives, exchange(): lax.all_to_all(cut, 'seq', split_axis=0, concat_axis=0, tiled=True)  103 us
    pallas_call x6, Pallas kernels, call(): pl.pallas_call(body, out_shape=[(pltpu.HBM if i in direct_out else jax.Sh...  8.4 us
  transfers between devices with their start and end apart: 1, of which 1 were waited for; matrix products, arithmetic and copies ran while one was open for 0% of the time, Pallas kernels for 0%

profile of v8, /device:TPU:8, one launch (start us, length us, event | category | flops | bytes accessed | tf_op | source)
XLA Modules:
  0.0 113.9 jit_solution(14134383408245303622)
XLA Ops:
  0.6 0.0 copy-start
  0.6 0.0 copy-start.1
  0.7 0.0 copy-start.2
  0.7 0.0 copy-start.3
  0.7 0.0 copy-start.4
  0.7 0.0 copy-start.5
  0.7 0.0 copy-start.6
  0.7 2.4 %shard_map.139 = (bf16[2048,128]{1,0:T(8,128)(2,1)S(1)}, bf16[2,128,512]{2,1,0:T(8,128)(2,1)S(1)}, f32[128,512]{1,0:T(8,128)S(1)}, bf16[128,512]{1,0:T(8,128)(2,...) custom-call(bf16[128,512]{1,0:T(8,128)(2,1)} %bitcast.37, ...), custom_call_target="tpu_custom_call" | custom-call | tf_op jit(solution)/shard_map/pallas_call | solution.py:441
  3.1 35.2 %all_to_all.20 = bf16[128,8,2,128]{3,2,1,0:T(2,128)(2,1)S(1)} all-to-all(bf16[128,8,2,128]{3,2,1,0:T(2,128)(2,1)S(1)} %bitcast.29), channel_id=1, replica_groups=mesh['seq'=128,'section'=2] {'seq'}, dimensions={0} | all-to-all | bytes 1048576 | tf_op jit(solution)/shard_map/all_to_all | solution.py:468
  38.4 0.0 copy-done
  38.4 0.0 copy-done.1
  38.4 0.0 copy-done.2
  38.4 0.0 copy-done.3
  38.4 0.0 copy-done.4
  38.4 0.0 copy-done.5
  38.4 0.0 copy-done.6
  38.4 1.0 shard_map.140
  39.5 20.8 %all_to_all.21 = bf16[128,4,2,128]{3,2,1,0:T(2,128)(2,1)S(1)} all-to-all(bf16[128,4,2,128]{3,2,1,0:T(2,128)(2,1)S(1)} %bitcast.31), channel_id=1, replica_groups=mesh['seq'=128,'section'=2] {'seq'}, dimensions={0} | all-to-all | bytes 524288 | tf_op jit(solution)/shard_map/all_to_all | solution.py:468
  60.3 0.7 shard_map.141
  61.1 0.1 collective-permute-start
  61.2 1.3 %collective-permute-done.inc = bf16[128,512]{1,0:T(8,128)(2,1)S(1)} collective-permute-done((bf16[128,512]{1,0:T(8,128)(2,1)S(1)}, bf16[128,512]{1,0:T(8,128)(2,1)S(1)}, u32[]{:S(2)}, u32[]{:S(2)}) %collective-permute-start) | collective-permute-done | bytes 131104 | tf_op jit(solution)/shard_map/ppermute | solution.py:518
  62.5 0.5 shard_map.142
  63.0 21.1 %all_to_all.22 = bf16[128,4,2,128]{3,2,1,0:T(2,128)(2,1)S(1)} all-to-all(bf16[128,4,2,128]{3,2,1,0:T(2,128)(2,1)S(1)} %bitcast.30), channel_id=1, replica_groups=mesh['seq'=128,'section'=2] {'seq'}, dimensions={0} | all-to-all | bytes 524288 | tf_op jit(solution)/shard_map/all_to_all | solution.py:468
  84.1 2.2 %shard_map.143 = bf16[2304,128]{1,0:T(8,128)(2,1)S(1)} custom-call(s32[1]{0:T(128)} %bitcast.4.late, s32[1]{0:T(128)} %bitcast.5.place, f32[2,512]{1,0:T(2,128)S(1)} %bitcast.33, bf16[2048,128]{1,0:T(8,128)(2,1)S(1)} %bitcast.20, f32[1024,128]{1,0:T(8,128)S(1)} %get-tuple-element.35.plain, bf16[1024,128]{1,0:T(8,128)(2,1)S(1)} %bitcast.27, ...), custom_call_target="tpu_custom_call" | custom-call | tf_op jit(solution)/shard_map/pallas_call | solution.py:441
  86.3 26.1 %all_to_all.23 = bf16[128,9,2,128]{3,2,1,0:T(2,128)(2,1)S(1)} all-to-all(bf16[128,9,2,128]{3,2,1,0:T(2,128)(2,1)S(1)} %bitcast.25), channel_id=1, replica_groups=mesh['seq'=128,'section'=2] {'seq'}, dimensions={0} | all-to-all | bytes 1179648 | tf_op jit(solution)/shard_map/all_to_all | solution.py:468
  112.4 1.5 %shard_map.144 = (bf16[128,512]{1,0:T(8,128)(2,1)}, bf16[2,128,512]{2,1,0:T(8,128)(2,1)}, f32[2,512]{1,0:T(2,128)}) custom-call(s32[1]{0:T(128)} %bitcast.4.late, bf16[2304,128]{1,0:T(8,128)(2,1)S(1)} %bitcast.26, bf16[2,128,512]{2,1,0:T(8,128)(2,1)S(1)} %bitcast.24, bf16[128,512]{1,0:T(8,128)(2,1)S(1)} %get-tuple-element.42.part_two, ...), custom_call_target="tpu_custom_call" | custom-call | tf_op jit(solution)/shard_map/pallas_call | solution.py:441
Async XLA Ops:
  0.6 37.8 %copy-start = (bf16[1,2,128,512]{3,2,1,0:T(8,128)(2,1)S(1)}, bf16[1,2,128,512]{3,2,1,0:T(8,128)(2,1)}, u32[]{:S(2)}) copy-start(bf16[1,2,128,512]{3,2,1,0:T(8,128)(2,1)} %param.13) | copy-start | bytes 786436
  0.6 37.7 %copy-start.1 = (bf16[512,256]{1,0:T(8,128)(2,1)S(1)}, bf16[512,256]{1,0:T(8,128)(2,1)}, u32[]{:S(2)}) copy-start(bf16[512,256]{1,0:T(8,128)(2,1)} %constant.19.clone.inner_fwd) | copy-start | bytes 786436
  0.7 37.7 %copy-start.2 = (f32[2,128,128]{2,1,0:T(8,128)S(1)}, f32[2,128,128]{2,1,0:T(8,128)}, u32[]{:S(2)}) copy-start(f32[2,128,128]{2,1,0:T(8,128)} %constant.22.clone.turns) | copy-start | bytes 393220
  0.7 37.7 %copy-start.3 = (bf16[256,256]{1,0:T(8,128)(2,1)S(1)}, bf16[256,256]{1,0:T(8,128)(2,1)}, u32[]{:S(2)}) copy-start(bf16[256,256]{1,0:T(8,128)(2,1)} %constant.18.clone.outer_fwd) | copy-start | bytes 393220
  0.7 37.7 %copy-start.4 = (bf16[128,512]{1,0:T(8,128)(2,1)S(1)}, bf16[128,512]{1,0:T(8,128)(2,1)}, u32[]{:S(2)}) copy-start(bf16[128,512]{1,0:T(8,128)(2,1)} %constant.21.clone.outer_inv) | copy-start | bytes 393220
  0.7 37.7 %copy-start.5 = (bf16[256,256]{1,0:T(8,128)(2,1)S(1)}, bf16[256,256]{1,0:T(8,128)(2,1)}, u32[]{:S(2)}) copy-start(bf16[256,256]{1,0:T(8,128)(2,1)} %constant.20.clone.inner_inv) | copy-start | bytes 393220
  0.7 37.7 %copy-start.6 = (f32[1,2,512]{2,1,0:T(2,128)S(1)}, f32[1,2,512]{2,1,0:T(2,128)}, u32[]{:S(2)}) copy-start(f32[1,2,512]{2,1,0:T(2,128)} %param.15) | copy-start | bytes 12292
  61.1 1.4 %collective-permute-start = (bf16[128,512]{1,0:T(8,128)(2,1)S(1)}, bf16[128,512]{1,0:T(8,128)(2,1)S(1)}, u32[]{:S(2)}, u32[]{:S(2)}) collective-permute-start(bf16[128,512]{1,0:T(8,128)(2,1)S(1)} %get-tuple-element.36.done), channel_id=1, source_target_pairs={{0,1},{1,0},{2,3},{3,2},{4,5},{5,4},{6,7},{7,6},{8,9},{9,8},{10,11... | collective-permute-start | bytes 393224 | tf_op jit(solution)/shard_map/ppermute | solution.py:518

commit v9 on v8

--- a/solution.py
+++ b/solution.py
@@ -403,33 +403,47 @@
     part_two,
     inc,
     w_in,
+    result_out,
+    filt_out,
+    skip_out,
+    scratch,
     result,
     filt_grads,
     skip_grads,
-    scratch,
+    sems,
 ):
     size = data.shape[1]
     stride = data.shape[0] // size
     scratch[...] = data[...].astype(F32)
-
-    @pl.when(late[0] == 0)
-    def _():
-        values = get_rows(scratch, 0, stride, per)
-        mix_one = get_rows(scratch, per, stride, per)
-        result[...] = input_grad(inc[...], values, mix_one, conv[0], part_two[...], w_in[...])
-
-    @pl.when(late[0] == 1)
-    def _():
-        result[...] = inc[...]
-
-    filt_grads[0] = (get_rows(scratch, 2 * per, stride, per).astype(F32) * rescale).astype(BF)
-    filt_grads[1] = (get_rows(scratch, 3 * per, stride, per).astype(F32) * rescale).astype(BF)
     sums = scratch[pl.ds(4 * per, size, stride=stride), :].T
     sums = (sums[: 2 * per] + sums[2 * per : 4 * per]) * rescale
     for w in range(2):
         for k in range(per):
             row = w * per + k
             skip_grads[pl.ds(w, 1), pl.ds(k * size, size)] = sums[row : row + 1]
+    copies = [pltpu.make_async_copy(skip_grads, skip_out, sems.at[0])]
+    copies[0].start()
+    for s in range(2):
+        filt_grads[s] = (
+            get_rows(scratch, (2 + s) * per, stride, per).astype(F32) * rescale
+        ).astype(BF)
+        copies.append(pltpu.make_async_copy(filt_grads.at[s], filt_out.at[s], sems.at[1 + s]))
+        copies[1 + s].start()
+
+    @pl.when(late[0] == 0)
+    def _():
+        values = get_rows(scratch, 0, stride, per)
+        mix_one = get_rows(scratch, per, stride, per)
+        result[...] = input_grad(inc[...], values, mix_one, conv[0], part_two[...], w_in[...])
+
+    @pl.when(late[0] == 1)
+    def _():
+        result[...] = inc[...]
+
+    copies.append(pltpu.make_async_copy(result, result_out, sems.at[3]))
+    copies[3].start()
+    for copy in copies:
+        copy.wait()
 
 
 def call(body, out_shapes, scratch, *operands, smem=0, direct=(), direct_out=(), limit=VMEM_LIMIT):
@@ -539,9 +553,12 @@
     grad_rows, filter_grads, skip_grads = call(
         functools.partial(finish_body, per, 1.0 / math.sqrt(parts * tokens)),
         [token_rows, ((2, tokens, channels), BF), ((2, channels), F32)],
-        [rows(out_rows)],
+        [
+            rows(out_rows), pltpu.VMEM((tokens, channels), BF),
+            pltpu.VMEM((2, tokens, channels), BF), (2, channels), pltpu.SemaphoreType.DMA((4,)),
+        ],
         late, back, conv, part_two, kept, w_in,
-        smem=1,
+        smem=1, direct_out=range(3),
     )
     return (grad_rows[None], filter_grads[None], skip_grads[None])
 

time: 114 us -> 114 us (level)
  no operation moved by 1% of the time
where the time goes in v9:
time: 114 us
  blocking collectives  103 us (90%)
  Pallas kernels  8.42 us (7%)
  waiting for transfers between devices  1.33 us (1%)
    all_to_all x4, blocking collectives, exchange(): lax.all_to_all(cut, 'seq', split_axis=0, concat_axis=0, tiled=True)  103 us
    pallas_call x6, Pallas kernels, call(): pl.pallas_call(body, out_shape=[(pltpu.HBM if i in direct_out else jax.Sh...  8.42 us
  transfers between devices with their start and end apart: 1, of which 1 were waited for; matrix products, arithmetic and copies ran while one was open for 0% of the time, Pallas kernels for 0%

profile of v9, /device:TPU:8, one launch (start us, length us, event | category | flops | bytes accessed | tf_op | source)
XLA Modules:
  0.0 114.1 jit_solution(840400195238299342)
XLA Ops:
  0.6 0.0 copy-start
  0.6 0.0 copy-start.1
  0.7 0.0 copy-start.2
  0.7 0.0 copy-start.3
  0.7 0.0 copy-start.4
  0.7 0.0 copy-start.5
  0.7 0.0 copy-start.6
  0.7 2.4 %shard_map.139 = (bf16[2048,128]{1,0:T(8,128)(2,1)S(1)}, bf16[2,128,512]{2,1,0:T(8,128)(2,1)S(1)}, f32[128,512]{1,0:T(8,128)S(1)}, bf16[128,512]{1,0:T(8,128)(2,...) custom-call(bf16[128,512]{1,0:T(8,128)(2,1)} %bitcast.37, ...), custom_call_target="tpu_custom_call" | custom-call | tf_op jit(solution)/shard_map/pallas_call | solution.py:455
  3.1 35.2 %all_to_all.20 = bf16[128,8,2,128]{3,2,1,0:T(2,128)(2,1)S(1)} all-to-all(bf16[128,8,2,128]{3,2,1,0:T(2,128)(2,1)S(1)} %bitcast.29), channel_id=1, replica_groups=mesh['seq'=128,'section'=2] {'seq'}, dimensions={0} | all-to-all | bytes 1048576 | tf_op jit(solution)/shard_map/all_to_all | solution.py:482
  38.4 0.0 copy-done
  38.4 0.0 copy-done.1
  38.4 0.0 copy-done.2
  38.4 0.0 copy-done.3
  38.4 0.0 copy-done.4
  38.4 0.0 copy-done.5
  38.4 0.0 copy-done.6
  38.4 1.0 shard_map.140
  39.5 20.8 %all_to_all.21 = bf16[128,4,2,128]{3,2,1,0:T(2,128)(2,1)S(1)} all-to-all(bf16[128,4,2,128]{3,2,1,0:T(2,128)(2,1)S(1)} %bitcast.31), channel_id=1, replica_groups=mesh['seq'=128,'section'=2] {'seq'}, dimensions={0} | all-to-all | bytes 524288 | tf_op jit(solution)/shard_map/all_to_all | solution.py:482
  60.3 0.7 shard_map.141
  61.1 0.1 collective-permute-start
  61.2 1.3 %collective-permute-done.inc = bf16[128,512]{1,0:T(8,128)(2,1)S(1)} collective-permute-done((bf16[128,512]{1,0:T(8,128)(2,1)S(1)}, bf16[128,512]{1,0:T(8,128)(2,1)S(1)}, u32[]{:S(2)}, u32[]{:S(2)}) %collective-permute-start) | collective-permute-done | bytes 131104 | tf_op jit(solution)/shard_map/ppermute | solution.py:532
  62.5 0.5 shard_map.142
  63.0 21.1 %all_to_all.22 = bf16[128,4,2,128]{3,2,1,0:T(2,128)(2,1)S(1)} all-to-all(bf16[128,4,2,128]{3,2,1,0:T(2,128)(2,1)S(1)} %bitcast.30), channel_id=1, replica_groups=mesh['seq'=128,'section'=2] {'seq'}, dimensions={0} | all-to-all | bytes 524288 | tf_op jit(solution)/shard_map/all_to_all | solution.py:482
  84.1 2.2 %shard_map.143 = bf16[2304,128]{1,0:T(8,128)(2,1)S(1)} custom-call(s32[1]{0:T(128)} %bitcast.4.late, s32[1]{0:T(128)} %bitcast.5.place, f32[2,512]{1,0:T(2,128)S(1)} %bitcast.33, bf16[2048,128]{1,0:T(8,128)(2,1)S(1)} %bitcast.20, f32[1024,128]{1,0:T(8,128)S(1)} %get-tuple-element.35.plain, bf16[1024,128]{1,0:T(8,128)(2,1)S(1)} %bitcast.27, ...), custom_call_target="tpu_custom_call" | custom-call | tf_op jit(solution)/shard_map/pallas_call | solution.py:455
  86.3 26.1 %all_to_all.23 = bf16[128,9,2,128]{3,2,1,0:T(2,128)(2,1)S(1)} all-to-all(bf16[128,9,2,128]{3,2,1,0:T(2,128)(2,1)S(1)} %bitcast.25), channel_id=1, replica_groups=mesh['seq'=128,'section'=2] {'seq'}, dimensions={0} | all-to-all | bytes 1179648 | tf_op jit(solution)/shard_map/all_to_all | solution.py:482
  112.4 1.6 %shard_map.144 = (bf16[128,512]{1,0:T(8,128)(2,1)}, bf16[2,128,512]{2,1,0:T(8,128)(2,1)}, f32[2,512]{1,0:T(2,128)}) custom-call(s32[1]{0:T(128)} %bitcast.4.late, bf16[2304,128]{1,0:T(8,128)(2,1)S(1)} %bitcast.26, bf16[2,128,512]{2,1,0:T(8,128)(2,1)S(1)} %bitcast.24, bf16[128,512]{1,0:T(8,128)(2,1)S(1)} %get-tuple-element.42.part_two, ...), custom_call_target="tpu_custom_call" | custom-call | tf_op jit(solution)/shard_map/pallas_call | solution.py:455
Async XLA Ops:
  0.6 37.8 %copy-start = (bf16[1,2,128,512]{3,2,1,0:T(8,128)(2,1)S(1)}, bf16[1,2,128,512]{3,2,1,0:T(8,128)(2,1)}, u32[]{:S(2)}) copy-start(bf16[1,2,128,512]{3,2,1,0:T(8,128)(2,1)} %param.13) | copy-start | bytes 786436
  0.6 37.7 %copy-start.1 = (bf16[512,256]{1,0:T(8,128)(2,1)S(1)}, bf16[512,256]{1,0:T(8,128)(2,1)}, u32[]{:S(2)}) copy-start(bf16[512,256]{1,0:T(8,128)(2,1)} %constant.19.clone.inner_fwd) | copy-start | bytes 786436
  0.7 37.7 %copy-start.2 = (f32[2,128,128]{2,1,0:T(8,128)S(1)}, f32[2,128,128]{2,1,0:T(8,128)}, u32[]{:S(2)}) copy-start(f32[2,128,128]{2,1,0:T(8,128)} %constant.22.clone.turns) | copy-start | bytes 393220
  0.7 37.7 %copy-start.3 = (bf16[256,256]{1,0:T(8,128)(2,1)S(1)}, bf16[256,256]{1,0:T(8,128)(2,1)}, u32[]{:S(2)}) copy-start(bf16[256,256]{1,0:T(8,128)(2,1)} %constant.18.clone.outer_fwd) | copy-start | bytes 393220
  0.7 37.7 %copy-start.4 = (bf16[128,512]{1,0:T(8,128)(2,1)S(1)}, bf16[128,512]{1,0:T(8,128)(2,1)}, u32[]{:S(2)}) copy-start(bf16[128,512]{1,0:T(8,128)(2,1)} %constant.21.clone.outer_inv) | copy-start | bytes 393220
  0.7 37.7 %copy-start.5 = (bf16[256,256]{1,0:T(8,128)(2,1)S(1)}, bf16[256,256]{1,0:T(8,128)(2,1)}, u32[]{:S(2)}) copy-start(bf16[256,256]{1,0:T(8,128)(2,1)} %constant.20.clone.inner_inv) | copy-start | bytes 393220
  0.7 37.7 %copy-start.6 = (f32[1,2,512]{2,1,0:T(2,128)S(1)}, f32[1,2,512]{2,1,0:T(2,128)}, u32[]{:S(2)}) copy-start(f32[1,2,512]{2,1,0:T(2,128)} %param.15) | copy-start | bytes 12292
  61.1 1.4 %collective-permute-start = (bf16[128,512]{1,0:T(8,128)(2,1)S(1)}, bf16[128,512]{1,0:T(8,128)(2,1)S(1)}, u32[]{:S(2)}, u32[]{:S(2)}) collective-permute-start(bf16[128,512]{1,0:T(8,128)(2,1)S(1)} %get-tuple-element.36.done), channel_id=1, source_target_pairs={{0,1},{1,0},{2,3},{3,2},{4,5},{5,4},{6,7},{7,6},{8,9},{9,8},{10,11... | collective-permute-start | bytes 393224 | tf_op jit(solution)/shard_map/ppermute | solution.py:532

commit v10 on v8

--- a/solution.py
+++ b/solution.py
@@ -125,6 +125,8 @@
 
 
 def prepare_body(
+    late,
+    place,
     rows_in,
     filt_in,
     w_in_in,
@@ -275,7 +277,7 @@
     return jnp.sum(jnp.where(lane == place[0], row, 0.0), axis=1, keepdims=True)
 
 
-def skip_rows(per, grads, others, out):
+def skip_rows(per, first, grads, others, out):
     size = out.shape[1]
     rows = out.shape[0] // size
     lane = lax.broadcasted_iota(jnp.int32, (1, size), 1)
@@ -287,8 +289,8 @@
             high = total.astype(BF).astype(F32)
             skip_row = jnp.where(lane == w * per + k, high, skip_row)
             skip_row = jnp.where(lane == (2 + w) * per + k, total - high, skip_row)
-    out[pl.ds(4 * per, size, stride=rows), :] = jnp.broadcast_to(skip_row, (size, size))
-    for r in range(4 * per + 1, rows):
+    out[pl.ds(first, size, stride=rows), :] = jnp.broadcast_to(skip_row, (size, size))
+    for r in range(first + 1, rows):
         out[pl.ds(r, size, stride=rows), :] = jnp.zeros((size, size), F32)
 
 
@@ -309,9 +311,11 @@
     outer_inv,
     turns,
     packed,
+    packed_late,
     known,
     fresh,
     out,
+    out_late,
 ):
     size = first.shape[1]
     fresh[...] = third[...].astype(F32)
@@ -333,7 +337,7 @@
         others = [
             [plain[pl.ds((s * per + k) * size, size), :] for k in range(per)] for s in range(2)
         ]
-        skip_rows(per, (grad_one, grad_two), others, out)
+        skip_rows(per, 4 * per, (grad_one, grad_two), others, out)
         packed[...] = out[...].astype(BF)
 
     @pl.when(late[0] == 1)
@@ -342,14 +346,13 @@
         values, gated = signals(fresh, 0, per), signals(fresh, 1, per)
         spec_one = to_spectrum(values, outer_fwd, inner_fwd, turns)
         spec_two = to_spectrum(gated, outer_fwd, inner_fwd, turns)
-        send_rows(out, 2, from_spectrum(conj_times(spec_one, held[0]), inner_inv, outer_inv, turns))
-        send_rows(out, 3, from_spectrum(conj_times(spec_two, held[1]), inner_inv, outer_inv, turns))
-        empty = [jnp.zeros((size, size), F32)] * per
-        send_rows(out, 0, empty)
-        send_rows(out, 1, empty)
+        for s, spec_in in enumerate((spec_one, spec_two)):
+            product = conj_times(spec_in, held[s])
+            send_rows(out_late, s, from_spectrum(product, inner_inv, outer_inv, turns))
         grad_one = [grad_held[pl.ds(k * size, size), :] for k in range(per)]
-        skip_rows(per, (grad_one, signals(known, 3, per)), (values, gated), out)
-        packed[...] = out[...].astype(BF)
+        grads = (grad_one, signals(known, 3, per))
+        skip_rows(per, 2 * per, grads, (values, gated), out_late)
+        packed_late[...] = out_late[...].astype(BF)
 
 
 def input_grad(inc, values, mix_one, conv_one, part_two, w_in):
@@ -394,42 +397,35 @@
         result[...] = jnp.zeros_like(result)
 
 
-def finish_body(
-    per,
-    rescale,
-    late,
-    data,
-    conv,
-    part_two,
-    inc,
-    w_in,
-    result,
-    filt_grads,
-    skip_grads,
-    scratch,
-):
-    size = data.shape[1]
-    stride = data.shape[0] // size
-    scratch[...] = data[...].astype(F32)
-
-    @pl.when(late[0] == 0)
-    def _():
-        values = get_rows(scratch, 0, stride, per)
-        mix_one = get_rows(scratch, per, stride, per)
-        result[...] = input_grad(inc[...], values, mix_one, conv[0], part_two[...], w_in[...])
-
-    @pl.when(late[0] == 1)
-    def _():
-        result[...] = inc[...]
-
-    filt_grads[0] = (get_rows(scratch, 2 * per, stride, per).astype(F32) * rescale).astype(BF)
-    filt_grads[1] = (get_rows(scratch, 3 * per, stride, per).astype(F32) * rescale).astype(BF)
-    sums = scratch[pl.ds(4 * per, size, stride=stride), :].T
+def filter_and_skip(per, first, rescale, scratch, filt_grads, skip_grads):
+    size = scratch.shape[1]
+    stride = scratch.shape[0] // size
+    for s in range(2):
+        rows = get_rows(scratch, first + s * per, stride, per).astype(F32)
+        filt_grads[s] = (rows * rescale).astype(BF)
+    sums = scratch[pl.ds(first + 2 * per, size, stride=stride), :].T
     sums = (sums[: 2 * per] + sums[2 * per : 4 * per]) * rescale
     for w in range(2):
         for k in range(per):
             row = w * per + k
             skip_grads[pl.ds(w, 1), pl.ds(k * size, size)] = sums[row : row + 1]
+
+
+def finish_early_body(
+    per, rescale, data, conv, part_two, inc, w_in, result, filt_grads, skip_grads, scratch
+):
+    stride = data.shape[0] // data.shape[1]
+    scratch[...] = data[...].astype(F32)
+    values = get_rows(scratch, 0, stride, per)
+    mix_one = get_rows(scratch, per, stride, per)
+    result[...] = input_grad(inc[...], values, mix_one, conv[0], part_two[...], w_in[...])
+    filter_and_skip(per, 2 * per, rescale, scratch, filt_grads, skip_grads)
+
+
+def finish_late_body(per, rescale, data, inc, result, filt_grads, skip_grads, scratch):
+    scratch[...] = data[...].astype(F32)
+    result[...] = inc[...]
+    filter_and_skip(per, 0, rescale, scratch, filt_grads, skip_grads)
 
 
 def call(body, out_shapes, scratch, *operands, smem=0, direct=(), direct_out=(), limit=VMEM_LIMIT):
@@ -474,7 +470,8 @@
     per = channels // parts
     w_in, w_out, conv = weight_in[0], weight_out[0], conv_out[0]
     outer_fwd, inner_fwd, inner_inv, outer_inv, turns = transform_tables(parts, tokens)
-    late = lax.axis_index("section").astype(jnp.int32).reshape(1)
+    is_late = lax.axis_index("section") == 1
+    late = is_late.astype(jnp.int32).reshape(1)
     place = lax.axis_index("seq").astype(jnp.int32).reshape(1)
 
     def rows(count):
@@ -492,10 +489,9 @@
         [
             pltpu.VMEM((2, tokens, channels), BF), rows(4 * per), pltpu.SemaphoreType.DMA((7,)),
         ],
-        layer_input[0], filters[0], w_in, w_out, grad_output,
-        direct=range(5),
-    )
-    packed, late, place = lax.optimization_barrier((packed, late, place))
+        late, place, layer_input[0], filters[0], w_in, w_out, grad_output,
+        smem=2, direct=range(2, 7),
+    )
     first = exchange(packed, parts)
     packed, held, grad_held = call(
         functools.partial(early_body, per),
@@ -525,23 +521,38 @@
     )
     third = exchange(packed, parts)
     out_rows = 4 * per + 2
-    (packed,) = call(
+    late_rows = 2 * per + 2
+    packed, packed_late = call(
         functools.partial(late_body, per),
-        [(rows(out_rows), BF)],
+        [(rows(out_rows), BF), (rows(late_rows), BF)],
         [
-            rows(4 * per), rows(2 * per), rows(out_rows),
+            rows(4 * per), rows(2 * per), rows(out_rows), rows(late_rows),
         ],
         late, place, skip_gain[0], first, plain, third, held, grad_held, spec,
         outer_fwd, inner_fwd, inner_inv, outer_inv, turns,
         smem=2,
     )
-    back = exchange(packed, parts)
-    grad_rows, filter_grads, skip_grads = call(
-        functools.partial(finish_body, per, 1.0 / math.sqrt(parts * tokens)),
-        [token_rows, ((2, tokens, channels), BF), ((2, channels), F32)],
-        [rows(out_rows)],
-        late, back, conv, part_two, kept, w_in,
-        smem=1,
+    rescale = 1.0 / math.sqrt(parts * tokens)
+    outputs = [token_rows, ((2, tokens, channels), BF), ((2, channels), F32)]
+
+    def finish_early(packed, packed_late, conv, part_two, kept, w_in):
+        return call(
+            functools.partial(finish_early_body, per, rescale),
+            outputs,
+            [rows(out_rows)],
+            exchange(packed, parts), conv, part_two, kept, w_in,
+        )
+
+    def finish_late(packed, packed_late, conv, part_two, kept, w_in):
+        return call(
+            functools.partial(finish_late_body, per, rescale),
+            outputs,
+            [rows(late_rows)],
+            exchange(packed_late, parts), kept,
+        )
+
+    grad_rows, filter_grads, skip_grads = lax.cond(
+        is_late, finish_late, finish_early, packed, packed_late, conv, part_two, kept, w_in
     )
     return (grad_rows[None], filter_grads[None], skip_grads[None])
 

time: 114 us -> 111 us (0.974)
  blocking collectives: 103 us -> 100 us
    all_to_all x4, blocking collectives: 103 us -> 100 us  [exchange(): lax.all_to_all(cut, 'seq', split_axis=0, concat_axis=0, tiled=True)]
where the time goes in v10:
time: 111 us
  blocking collectives  100 us (90%)
  Pallas kernels  8.23 us (7%)
  waiting for transfers between devices  1.33 us (1%)
    all_to_all x4, blocking collectives, exchange(): lax.all_to_all(cut, 'seq', split_axis=0, concat_axis=0, tiled=True)  100 us
    pallas_call x6, Pallas kernels, call(): pl.pallas_call(body, out_shape=[(pltpu.HBM if i in direct_out else jax.Sh...  8.23 us
  transfers between devices with their start and end apart: 1, of which 1 were waited for; matrix products, arithmetic and copies ran while one was open for 0% of the time, Pallas kernels for 0%

profile of v10, /device:TPU:8, one launch (start us, length us, event | category | flops | bytes accessed | tf_op | source)
XLA Modules:
  0.0 110.8 jit_solution(186670244807871360)
XLA Ops:
  0.6 0.0 copy-start
  0.7 0.0 copy-start.1
  0.7 0.0 copy-start.2
  0.7 0.0 copy-start.3
  0.7 0.0 copy-start.4
  0.7 0.0 copy-start.5
  0.7 0.0 copy-start.6
  0.7 2.4 %shard_map.139 = (bf16[2048,128]{1,0:T(8,128)(2,1)S(1)}, bf16[2,128,512]{2,1,0:T(8,128)(2,1)S(1)}, f32[128,512]{1,0:T(8,128)S(1)}, bf16[128,512]{1,0:T(8,128)(2,...) custom-call(s32[1]{0:T(128)} %bitcast.4.late, s32[1]{0:T(128)} %bitcast.5.place, ...), custom_call_target="tpu_custom_call" | custom-call | tf_op jit(solution)/shard_map/pallas_call | solution.py:437
  3.1 35.2 %all_to_all.25 = bf16[128,8,2,128]{3,2,1,0:T(2,128)(2,1)S(1)} all-to-all(bf16[128,8,2,128]{3,2,1,0:T(2,128)(2,1)S(1)} %bitcast.27), channel_id=1, replica_groups=mesh['seq'=128,'section'=2] {'seq'}, dimensions={0} | all-to-all | bytes 1048576 | tf_op jit(solution)/shard_map/all_to_all | solution.py:464
  38.4 0.0 copy-done
  38.4 0.0 copy-done.1
  38.4 0.0 copy-done.2
  38.4 0.0 copy-done.3
  38.4 0.0 copy-done.4
  38.4 0.0 copy-done.5
  38.4 0.0 copy-done.6
  38.4 1.0 shard_map.140
  39.5 20.8 %all_to_all.26 = bf16[128,4,2,128]{3,2,1,0:T(2,128)(2,1)S(1)} all-to-all(bf16[128,4,2,128]{3,2,1,0:T(2,128)(2,1)S(1)} %bitcast.29), channel_id=1, replica_groups=mesh['seq'=128,'section'=2] {'seq'}, dimensions={0} | all-to-all | bytes 524288 | tf_op jit(solution)/shard_map/all_to_all | solution.py:464
  60.3 0.7 shard_map.141
  61.0 0.1 collective-permute-start
  61.1 1.3 %collective-permute-done.inc = bf16[128,512]{1,0:T(8,128)(2,1)S(1)} collective-permute-done((bf16[128,512]{1,0:T(8,128)(2,1)S(1)}, bf16[128,512]{1,0:T(8,128)(2,1)S(1)}, u32[]{:S(2)}, u32[]{:S(2)}) %collective-permute-start) | collective-permute-done | bytes 131104 | tf_op jit(solution)/shard_map/ppermute | solution.py:514
  62.5 0.5 shard_map.142
  63.0 21.1 %all_to_all.27 = bf16[128,4,2,128]{3,2,1,0:T(2,128)(2,1)S(1)} all-to-all(bf16[128,4,2,128]{3,2,1,0:T(2,128)(2,1)S(1)} %bitcast.28), channel_id=1, replica_groups=mesh['seq'=128,'section'=2] {'seq'}, dimensions={0} | all-to-all | bytes 524288 | tf_op jit(solution)/shard_map/all_to_all | solution.py:464
  84.1 2.2 %shard_map.143 = (bf16[2304,128]{1,0:T(8,128)(2,1)S(1)}, bf16[1280,128]{1,0:T(8,128)(2,1)S(1)}) custom-call(s32[1]{0:T(128)} %bitcast.4.late, s32[1]{0:T(128)} %bitcast.5.place, f32[2,512]{1,0:T(2,128)S(1)} %bitcast.31, bf16[2048,128]{1,0:T(8,128)(2,1)S(1)} %bitcast.22, f32[1024,128]{1,0:T(8,128)S(1)} %get-tuple-element.64.plain, ...), custom_call_target="tpu_custom_call" | custom-call | tf_op jit(solution)/shard_map/pallas_call | solution.py:437
  86.3 24.5 %conditional.1 = ((bf16[128,512]{1,0:T(8,128)(2,1)}, bf16[2,128,512]{2,1,0:T(8,128)(2,1)}, f32[2,512]{1,0:T(2,128)})) conditional(s32[]{:T(128)} %convert_element_type.4, (bf16[2304,128]{1,0:T(8,128)(2,1)S(1)}, bf16[2,128,512]{2,1,0:T(8,128)(2,1)S(1)}, bf16[128,512]{1,0:T(8,128)(2,1)S(1)}, bf16[128,512]{1,0:T(8,128)(2,1)S(1)}, ...), branch_computations={%region_0.0_spmd, %region_1.0_spmd} | conditional | bytes 1179656 | solution.py:554
  86.3 23.1 %all_to_all.23 = bf16[128,9,2,128]{3,2,1,0:T(2,128)(2,1)S(1)} all-to-all(bf16[128,9,2,128]{3,2,1,0:T(2,128)(2,1)S(1)} %bitcast.37), channel_id=1, replica_groups=mesh['seq'=128,'section'=2] {'seq'}, dimensions={0} | all-to-all | bytes 1179648 | tf_op jit(solution)/shard_map/cond/branch_0_fun/all_to_all | solution.py:464
  109.4 1.4 %branch_0_fun.1 = (bf16[128,512]{1,0:T(8,128)(2,1)}, bf16[2,128,512]{2,1,0:T(8,128)(2,1)}, f32[2,512]{1,0:T(2,128)}) custom-call(bf16[2304,128]{1,0:T(8,128)(2,1)S(1)} %bitcast.23, bf16[2,128,512]{2,1,0:T(8,128)(2,1)S(1)} %get-tuple-element.24.conv, bf16[128,512]{1,0:T(8,128)(2,1)S(1)} %get-tuple-element.25.part_two, ...), custom_call_target="tpu_custom_call" | custom-call | tf_op jit(solution)/shard_map/cond/branch_0_fun/pallas_call | solution.py:437
Async XLA Ops:
  0.6 37.8 %copy-start = (bf16[512,256]{1,0:T(8,128)(2,1)S(1)}, bf16[512,256]{1,0:T(8,128)(2,1)}, u32[]{:S(2)}) copy-start(bf16[512,256]{1,0:T(8,128)(2,1)} %constant.21.clone.inner_fwd) | copy-start | bytes 786436
  0.7 37.7 %copy-start.1 = (f32[2,128,128]{2,1,0:T(8,128)S(1)}, f32[2,128,128]{2,1,0:T(8,128)}, u32[]{:S(2)}) copy-start(f32[2,128,128]{2,1,0:T(8,128)} %constant.24.clone.turns) | copy-start | bytes 393220
  0.7 37.7 %copy-start.2 = (bf16[256,256]{1,0:T(8,128)(2,1)S(1)}, bf16[256,256]{1,0:T(8,128)(2,1)}, u32[]{:S(2)}) copy-start(bf16[256,256]{1,0:T(8,128)(2,1)} %constant.20.clone.outer_fwd) | copy-start | bytes 393220
  0.7 37.7 %copy-start.3 = (bf16[128,512]{1,0:T(8,128)(2,1)S(1)}, bf16[128,512]{1,0:T(8,128)(2,1)}, u32[]{:S(2)}) copy-start(bf16[128,512]{1,0:T(8,128)(2,1)} %constant.23.clone.outer_inv) | copy-start | bytes 393220
  0.7 37.7 %copy-start.4 = (bf16[256,256]{1,0:T(8,128)(2,1)S(1)}, bf16[256,256]{1,0:T(8,128)(2,1)}, u32[]{:S(2)}) copy-start(bf16[256,256]{1,0:T(8,128)(2,1)} %constant.22.clone.inner_inv) | copy-start | bytes 393220
  0.7 37.7 %copy-start.5 = (f32[1,2,512]{2,1,0:T(2,128)S(1)}, f32[1,2,512]{2,1,0:T(2,128)}, u32[]{:S(2)}) copy-start(f32[1,2,512]{2,1,0:T(2,128)} %param.17) | copy-start | bytes 12292
  0.7 37.7 %copy-start.6 = (bf16[1,2,128,512]{3,2,1,0:T(8,128)(2,1)S(1)}, bf16[1,2,128,512]{3,2,1,0:T(8,128)(2,1)}, u32[]{:S(2)}) copy-start(bf16[1,2,128,512]{3,2,1,0:T(8,128)(2,1)} %param.15) | copy-start | bytes 786436
  61.0 1.4 %collective-permute-start = (bf16[128,512]{1,0:T(8,128)(2,1)S(1)}, bf16[128,512]{1,0:T(8,128)(2,1)S(1)}, u32[]{:S(2)}, u32[]{:S(2)}) collective-permute-start(bf16[128,512]{1,0:T(8,128)(2,1)S(1)} %get-tuple-element.65.done), channel_id=1, source_target_pairs={{0,1},{1,0},{2,3},{3,2},{4,5},{5,4},{6,7},{7,6},{8,9},{9,8},{10,11... | collective-permute-start | bytes 393224 | tf_op jit(solution)/shard_map/ppermute | solution.py:514

commit v11 on v10

--- a/solution.py
+++ b/solution.py
@@ -180,28 +180,16 @@
     packed[...] = scratch[...].astype(BF)
 
 
-def regrad_body(
-    late, inc, done, w_out, rows, w_in, gates, conv, packed, part_two, kept, scratch
-):
-    size = inc.shape[0]
-    channels = inc.shape[1]
-    per = channels // size
-
-    @pl.when(late[0] == 0)
-    def _():
-        kept[...] = inc[...]
-        mix_two = mm_t(inc[...], w_out[...])
-        part_two[...] = (mix_two * conv[1].astype(F32)).astype(BF)
-        put_rows(scratch, mix_two * gates[1].astype(F32), 0, 2 * per)
-        for k in range(per):
-            scratch[pl.ds(per + k, size, stride=2 * per), :] = jnp.zeros((size, size), F32)
-        packed[...] = scratch[...].astype(BF)
-
-    @pl.when(late[0] == 1)
-    def _():
-        kept[...] = done[...]
-        part_two[...] = jnp.zeros_like(part_two)
-        pack_known(scratch, rows, w_in, gates, conv, packed)
+def regrad_body(inc, w_out, gates, conv, packed, part_two, scratch):
+    per = inc.shape[1] // inc.shape[0]
+    mix_two = mm_t(inc[...], w_out[...])
+    part_two[...] = (mix_two * conv[1].astype(F32)).astype(BF)
+    put_rows(scratch, mix_two * gates[1].astype(F32), 0, per)
+    packed[...] = scratch[...].astype(BF)
+
+
+def known_body(rows, w_in, gates, conv, packed, scratch):
+    pack_known(scratch, rows, w_in, gates, conv, packed)
 
 
 def signals(scratch, s, per):
@@ -294,12 +282,10 @@
         out[pl.ds(r, size, stride=rows), :] = jnp.zeros((size, size), F32)
 
 
-def late_body(
+def early_tick_body(
     per,
-    late,
     place,
     gains,
-    first,
     plain,
     third,
     held,
@@ -311,48 +297,59 @@
     outer_inv,
     turns,
     packed,
-    packed_late,
+    fresh,
+    out,
+):
+    size = third.shape[1]
+    fresh[...] = third[...].astype(F32)
+    grad_two = signals(fresh, 0, per)
+    spec_two = to_spectrum(grad_two, outer_fwd, inner_fwd, turns)
+    mixed = from_spectrum(conj_times(held[1], spec_two), inner_inv, outer_inv, turns)
+    send_rows(out, 3, from_spectrum(conj_times(spec[1], spec_two), inner_inv, outer_inv, turns))
+    mix_one = [mixed[k] + gain_of(gains, 1, k, place, size) * grad_two[k] for k in range(per)]
+    send_rows(out, 1, mix_one)
+    gate_one = [grad_held[pl.ds(k * size, size), :] for k in range(per)]
+    grad_one = [mix_one[k] * gate_one[k] for k in range(per)]
+    spec_one = to_spectrum(grad_one, outer_fwd, inner_fwd, turns)
+    mixed = from_spectrum(conj_times(held[0], spec_one), inner_inv, outer_inv, turns)
+    send_rows(out, 2, from_spectrum(conj_times(spec[0], spec_one), inner_inv, outer_inv, turns))
+    send_rows(out, 0, [mixed[k] + gain_of(gains, 0, k, place, size) * grad_one[k] for k in range(per)])
+    others = [
+        [plain[pl.ds((s * per + k) * size, size), :] for k in range(per)] for s in range(2)
+    ]
+    skip_rows(per, 4 * per, (grad_one, grad_two), others, out)
+    packed[...] = out[...].astype(BF)
+
+
+def late_tick_body(
+    per,
+    first,
+    third,
+    held,
+    grad_held,
+    outer_fwd,
+    inner_fwd,
+    inner_inv,
+    outer_inv,
+    turns,
+    packed,
     known,
     fresh,
     out,
-    out_late,
 ):
-    size = first.shape[1]
+    size = third.shape[1]
     fresh[...] = third[...].astype(F32)
-
-    @pl.when(late[0] == 0)
-    def _():
-        grad_two = signals(fresh, 0, per)
-        spec_two = to_spectrum(grad_two, outer_fwd, inner_fwd, turns)
-        mixed = from_spectrum(conj_times(held[1], spec_two), inner_inv, outer_inv, turns)
-        send_rows(out, 3, from_spectrum(conj_times(spec[1], spec_two), inner_inv, outer_inv, turns))
-        mix_one = [mixed[k] + gain_of(gains, 1, k, place, size) * grad_two[k] for k in range(per)]
-        send_rows(out, 1, mix_one)
-        gate_one = [grad_held[pl.ds(k * size, size), :] for k in range(per)]
-        grad_one = [mix_one[k] * gate_one[k] for k in range(per)]
-        spec_one = to_spectrum(grad_one, outer_fwd, inner_fwd, turns)
-        mixed = from_spectrum(conj_times(held[0], spec_one), inner_inv, outer_inv, turns)
-        send_rows(out, 2, from_spectrum(conj_times(spec[0], spec_one), inner_inv, outer_inv, turns))
-        send_rows(out, 0, [mixed[k] + gain_of(gains, 0, k, place, size) * grad_one[k] for k in range(per)])
-        others = [
-            [plain[pl.ds((s * per + k) * size, size), :] for k in range(per)] for s in range(2)
-        ]
-        skip_rows(per, 4 * per, (grad_one, grad_two), others, out)
-        packed[...] = out[...].astype(BF)
-
-    @pl.when(late[0] == 1)
-    def _():
-        known[...] = first[...].astype(F32)
-        values, gated = signals(fresh, 0, per), signals(fresh, 1, per)
-        spec_one = to_spectrum(values, outer_fwd, inner_fwd, turns)
-        spec_two = to_spectrum(gated, outer_fwd, inner_fwd, turns)
-        for s, spec_in in enumerate((spec_one, spec_two)):
-            product = conj_times(spec_in, held[s])
-            send_rows(out_late, s, from_spectrum(product, inner_inv, outer_inv, turns))
-        grad_one = [grad_held[pl.ds(k * size, size), :] for k in range(per)]
-        grads = (grad_one, signals(known, 3, per))
-        skip_rows(per, 2 * per, grads, (values, gated), out_late)
-        packed_late[...] = out_late[...].astype(BF)
+    known[...] = first[...].astype(F32)
+    values, gated = signals(fresh, 0, per), signals(fresh, 1, per)
+    spec_one = to_spectrum(values, outer_fwd, inner_fwd, turns)
+    spec_two = to_spectrum(gated, outer_fwd, inner_fwd, turns)
+    for s, spec_in in enumerate((spec_one, spec_two)):
+        product = conj_times(spec_in, held[s])
+        send_rows(out, s, from_spectrum(product, inner_inv, outer_inv, turns))
+    grad_one = [grad_held[pl.ds(k * size, size), :] for k in range(per)]
+    grads = (grad_one, signals(known, 3, per))
+    skip_rows(per, 2 * per, grads, (values, gated), out)
+    packed[...] = out[...].astype(BF)
 
 
 def input_grad(inc, values, mix_one, conv_one, part_two, w_in):
@@ -512,48 +509,57 @@
         smem=1,
     )
     handed = lax.ppermute(done, "section", [(0, 1), (1, 0)])
-    packed, part_two, kept = call(
-        regrad_body,
-        [(rows(2 * per), BF), token_rows, token_rows],
-        [rows(2 * per)],
-        late, handed, done, w_out, rows_in, w_in, gates, conv,
-        smem=1,
-    )
-    third = exchange(packed, parts)
-    out_rows = 4 * per + 2
-    late_rows = 2 * per + 2
-    packed, packed_late = call(
-        functools.partial(late_body, per),
-        [(rows(out_rows), BF), (rows(late_rows), BF)],
-        [
-            rows(4 * per), rows(2 * per), rows(out_rows), rows(late_rows),
-        ],
-        late, place, skip_gain[0], first, plain, third, held, grad_held, spec,
-        outer_fwd, inner_fwd, inner_inv, outer_inv, turns,
-        smem=2,
-    )
     rescale = 1.0 / math.sqrt(parts * tokens)
     outputs = [token_rows, ((2, tokens, channels), BF), ((2, channels), F32)]
-
-    def finish_early(packed, packed_late, conv, part_two, kept, w_in):
+    tables = (outer_fwd, inner_fwd, inner_inv, outer_inv, turns)
+    gains = skip_gain[0]
+
+    def early_section():
+        count = 4 * per + 2
+        packed, part_two = call(
+            regrad_body,
+            [(rows(per), BF), token_rows],
+            [rows(per)],
+            handed, w_out, gates, conv,
+        )
+        third = exchange(packed, parts)
+        (packed,) = call(
+            functools.partial(early_tick_body, per),
+            [(rows(count), BF)],
+            [rows(per), rows(count)],
+            place, gains, plain, third, held, grad_held, spec, *tables,
+            smem=1,
+        )
         return call(
             functools.partial(finish_early_body, per, rescale),
             outputs,
-            [rows(out_rows)],
-            exchange(packed, parts), conv, part_two, kept, w_in,
-        )
-
-    def finish_late(packed, packed_late, conv, part_two, kept, w_in):
+            [rows(count)],
+            exchange(packed, parts), conv, part_two, handed, w_in,
+        )
+
+    def late_section():
+        count = 2 * per + 2
+        (packed,) = call(
+            known_body,
+            [(rows(2 * per), BF)],
+            [rows(2 * per)],
+            rows_in, w_in, gates, conv,
+        )
+        third = exchange(packed, parts)
+        (packed,) = call(
+            functools.partial(late_tick_body, per),
+            [(rows(count), BF)],
+            [rows(4 * per), rows(2 * per), rows(count)],
+            first, third, held, grad_held, *tables,
+        )
         return call(
             functools.partial(finish_late_body, per, rescale),
             outputs,
-            [rows(late_rows)],
-            exchange(packed_late, parts), kept,
-        )
-
-    grad_rows, filter_grads, skip_grads = lax.cond(
-        is_late, finish_late, finish_early, packed, packed_late, conv, part_two, kept, w_in
-    )
+            [rows(count)],
+            exchange(packed, parts), done,
+        )
+
+    grad_rows, filter_grads, skip_grads = lax.cond(is_late, late_section, early_section)
     return (grad_rows[None], filter_grads[None], skip_grads[None])
 
 

time: 111 us -> 111 us (level)
  no operation moved by 1% of the time
where the time goes in v11:
time: 111 us; the launch traced here: 110 us
  blocking collectives  100 us (90%)
  Pallas kernels  7.89 us (7%)
  waiting for transfers between devices  1.33 us (1%)
    all_to_all x4, blocking collectives, exchange(): lax.all_to_all(cut, 'seq', split_axis=0, concat_axis=0, tiled=True)  100 us
    pallas_call x6, Pallas kernels, call(): pl.pallas_call(body, out_shape=[(pltpu.HBM if i in direct_out else jax.Sh...  7.89 us
  transfers between devices with their start and end apart: 1, of which 1 were waited for; matrix products, arithmetic and copies ran while one was open for 0% of the time, Pallas kernels for 0%

profile of v11, /device:TPU:8, one launch (start us, length us, event | category | flops | bytes accessed | tf_op | source)
XLA Modules:
  0.0 110.3 jit_solution(3523793420008188380)
XLA Ops:
  0.6 0.0 copy-start
  0.6 0.0 copy-start.1
  0.7 0.0 copy-start.2
  0.7 0.0 copy-start.3
  0.7 0.0 copy-start.4
  0.7 0.0 copy-start.5
  0.7 0.0 copy-start.6
  0.7 2.4 %shard_map.139 = (bf16[2048,128]{1,0:T(8,128)(2,1)S(1)}, bf16[2,128,512]{2,1,0:T(8,128)(2,1)S(1)}, f32[128,512]{1,0:T(8,128)S(1)}, bf16[128,512]{1,0:T(8,128)(2,...) custom-call(s32[1]{0:T(128)} %bitcast.8.late, s32[1]{0:T(128)} %bitcast.9.place, ...), custom_call_target="tpu_custom_call" | custom-call | tf_op jit(solution)/shard_map/pallas_call | solution.py:434
  3.1 35.2 %all_to_all.30 = bf16[128,8,2,128]{3,2,1,0:T(2,128)(2,1)S(1)} all-to-all(bf16[128,8,2,128]{3,2,1,0:T(2,128)(2,1)S(1)} %bitcast.31), channel_id=1, replica_groups=mesh['seq'=128,'section'=2] {'seq'}, dimensions={0} | all-to-all | bytes 1048576 | tf_op jit(solution)/shard_map/all_to_all | solution.py:461
  38.4 0.0 copy-done
  38.4 0.0 copy-done.1
  38.4 0.0 copy-done.2
  38.4 0.0 copy-done.3
  38.4 0.0 copy-done.4
  38.4 0.0 copy-done.5
  38.4 0.0 copy-done.6
  38.4 1.0 shard_map.140
  39.5 20.8 %all_to_all.31 = bf16[128,4,2,128]{3,2,1,0:T(2,128)(2,1)S(1)} all-to-all(bf16[128,4,2,128]{3,2,1,0:T(2,128)(2,1)S(1)} %bitcast.32), channel_id=1, replica_groups=mesh['seq'=128,'section'=2] {'seq'}, dimensions={0} | all-to-all | bytes 524288 | tf_op jit(solution)/shard_map/all_to_all | solution.py:461
  60.3 0.7 shard_map.141
  61.0 0.1 collective-permute-start
  61.1 1.3 %collective-permute-done = bf16[128,512]{1,0:T(8,128)(2,1)S(1)} collective-permute-done((bf16[128,512]{1,0:T(8,128)(2,1)S(1)}, bf16[128,512]{1,0:T(8,128)(2,1)S(1)}, u32[]{:S(2)}, u32[]{:S(2)}) %collective-permute-start) | collective-permute-done | bytes 131104 | tf_op jit(solution)/shard_map/ppermute | solution.py:511
  62.4 47.8 %conditional.1 = ((bf16[128,512]{1,0:T(8,128)(2,1)}, bf16[2,128,512]{2,1,0:T(8,128)(2,1)}, f32[2,512]{1,0:T(2,128)})) conditional(s32[]{:T(128)} %convert_element_type.4, (bf16[128,512]{1,0:T(8,128)(2,1)S(1)}, bf16[512,512]{1,0:T(8,128)(2,1)S(1)}, bf16[2,128,512]{2,1,0:T(8,128)(2,1)S(1)}, bf16[2,128,512]{2,1,0:T(8,128)(2,1)S(1)}, s32[1]{0:T(128)}, ...), branch_computations={%region_0.0_spmd, %region_1.0_spmd} | conditional | bytes 1441800 | solution.py:562
  62.4 0.4 branch_0_fun.3
  62.8 19.1 %all_to_all.26 = bf16[128,2,2,128]{3,2,1,0:T(2,128)(2,1)S(1)} all-to-all(bf16[128,2,2,128]{3,2,1,0:T(2,128)(2,1)S(1)} %bitcast.33), channel_id=1, replica_groups=mesh['seq'=128,'section'=2] {'seq'}, dimensions={0} | all-to-all | bytes 262144 | tf_op jit(solution)/shard_map/cond/branch_0_fun/all_to_all | solution.py:461
  81.9 1.9 %branch_0_fun.4 = bf16[2304,128]{1,0:T(8,128)(2,1)S(1)} custom-call(s32[1]{0:T(128)} %get-tuple-element.67.place, f32[2,512]{1,0:T(2,128)S(1)} %get-tuple-element.68.gains, f32[1024,128]{1,0:T(8,128)S(1)} %get-tuple-element.69.plain, bf16[512,128]{1,0:T(8,128)(2,1)S(1)} %bitcast.30, f32[2,512,256]{2,1,0:T(8,128)S(1)} %get-tuple-element.75.held, ...), custom_call_target="tpu_custom_call" | custom-call | tf_op jit(solution)/shard_map/cond/branch_0_fun/pallas_call | solution.py:434
  83.9 25.0 %all_to_all.27 = bf16[128,9,2,128]{3,2,1,0:T(2,128)(2,1)S(1)} all-to-all(bf16[128,9,2,128]{3,2,1,0:T(2,128)(2,1)S(1)} %bitcast.24), channel_id=1, replica_groups=mesh['seq'=128,'section'=2] {'seq'}, dimensions={0} | all-to-all | bytes 1179648 | tf_op jit(solution)/shard_map/cond/branch_0_fun/all_to_all | solution.py:461
  108.9 1.4 %branch_0_fun.5 = (bf16[128,512]{1,0:T(8,128)(2,1)}, bf16[2,128,512]{2,1,0:T(8,128)(2,1)}, f32[2,512]{1,0:T(2,128)}) custom-call(bf16[2304,128]{1,0:T(8,128)(2,1)S(1)} %bitcast.23, bf16[2,128,512]{2,1,0:T(8,128)(2,1)S(1)} %get-tuple-element.73.conv, bf16[128,512]{1,0:T(8,128)(2,1)S(1)} %get-tuple-element.83.part_two, ...), custom_call_target="tpu_custom_call" | custom-call | tf_op jit(solution)/shard_map/cond/branch_0_fun/pallas_call | solution.py:434
Async XLA Ops:
  0.6 37.7 %copy-start = (bf16[1,2,128,512]{3,2,1,0:T(8,128)(2,1)S(1)}, bf16[1,2,128,512]{3,2,1,0:T(8,128)(2,1)}, u32[]{:S(2)}) copy-start(bf16[1,2,128,512]{3,2,1,0:T(8,128)(2,1)} %param.15) | copy-start | bytes 786436
  0.6 37.7 %copy-start.1 = (bf16[512,256]{1,0:T(8,128)(2,1)S(1)}, bf16[512,256]{1,0:T(8,128)(2,1)}, u32[]{:S(2)}) copy-start(bf16[512,256]{1,0:T(8,128)(2,1)} %constant.21.clone.inner_fwd) | copy-start | bytes 786436
  0.7 37.7 %copy-start.2 = (f32[2,128,128]{2,1,0:T(8,128)S(1)}, f32[2,128,128]{2,1,0:T(8,128)}, u32[]{:S(2)}) copy-start(f32[2,128,128]{2,1,0:T(8,128)} %constant.24.clone.turns) | copy-start | bytes 393220
  0.7 37.7 %copy-start.3 = (bf16[256,256]{1,0:T(8,128)(2,1)S(1)}, bf16[256,256]{1,0:T(8,128)(2,1)}, u32[]{:S(2)}) copy-start(bf16[256,256]{1,0:T(8,128)(2,1)} %constant.20.clone.outer_fwd) | copy-start | bytes 393220
  0.7 37.7 %copy-start.4 = (bf16[128,512]{1,0:T(8,128)(2,1)S(1)}, bf16[128,512]{1,0:T(8,128)(2,1)}, u32[]{:S(2)}) copy-start(bf16[128,512]{1,0:T(8,128)(2,1)} %constant.23.clone.outer_inv) | copy-start | bytes 393220
  0.7 37.7 %copy-start.5 = (bf16[256,256]{1,0:T(8,128)(2,1)S(1)}, bf16[256,256]{1,0:T(8,128)(2,1)}, u32[]{:S(2)}) copy-start(bf16[256,256]{1,0:T(8,128)(2,1)} %constant.22.clone.inner_inv) | copy-start | bytes 393220
  0.7 37.7 %copy-start.6 = (f32[1,2,512]{2,1,0:T(2,128)S(1)}, f32[1,2,512]{2,1,0:T(2,128)}, u32[]{:S(2)}) copy-start(f32[1,2,512]{2,1,0:T(2,128)} %param.17) | copy-start | bytes 12292
  61.0 1.4 %collective-permute-start = (bf16[128,512]{1,0:T(8,128)(2,1)S(1)}, bf16[128,512]{1,0:T(8,128)(2,1)S(1)}, u32[]{:S(2)}, u32[]{:S(2)}) collective-permute-start(bf16[128,512]{1,0:T(8,128)(2,1)S(1)} %get-tuple-element.127), channel_id=1, source_target_pairs={{0,1},{1,0},{2,3},{3,2},{4,5},{5,4},{6,7},{7,6},{8,9},{9,8},{10,11... | collective-permute-start | bytes 393224 | tf_op jit(solution)/shard_map/ppermute | solution.py:511
